TPU v7x, 128 devices: a whole 4x4x4 slice. The times are simulated.
128 devices in a mesh: dp: 16 (over z, y), tensor: 8 (over x, core).
Axes of the slice: x: 4, y: 4, z: 4, core: 2. Of those that a mesh axis runs over, the one named last changes fastest.
Arguments:
- acts: bfloat16 [8192, 4096], P('dp'), may hold values from -0.25 to 0.25
- up_cot: bfloat16 [8192, 7168], P('dp', 'tensor'), may hold values from -6 to 6
- up_weight: bfloat16 [4096, 7168], P(None, 'tensor'), may hold values from -0.0625 to 0.0625
- error_buf: bfloat16 [16, 4096, 7168], P('dp', None, 'tensor'), may hold values from -4 to 4
- q_init: float32 [64, 7168], P(None, 'tensor'), may hold values from -6 to 6
Outputs:
- input_grad: bfloat16 [8192, 4096], P(('dp', 'tensor'))
- new_error: bfloat16 [16, 4096, 7168], P('dp', None, 'tensor')
- p_factor: float32 [64, 4096], replicated
- q_factor: float32 [64, 7168], P(None, 'tensor')
All inputs are finite; a program needn't handle non-finite values.
Results may differ from a plain program's by a relative error of at most 0.001.
Values sent between devices are 32-bit elements; how exact they have to be, the bound alone decides.
No kernel may reach another device: no remote copies, remote signals or barrier semaphores. Data moves between devices by JAX's collectives and lax.ppermute only.
A program may use at most 128 MiB of HBM per device.

v0:
```python
import jax
import jax.numpy as jnp
from jax import lax
from jax.sharding import PartitionSpec as P


def body(acts, up_cot, up_weight, error_buf, q_init):
    highest = lax.Precision.HIGHEST
    n_replicas = lax.axis_size("dp")
    input_grad = lax.psum_scatter(
        lax.dot_general(
            up_cot, up_weight, (((1,), (1,)), ((), ())), preferred_element_type=jnp.float32
        ),
        "tensor",
        scatter_dimension=0,
        tiled=True,
    ).astype(jnp.bfloat16)
    grad = lax.dot_general(
        acts, up_cot, (((0,), (0,)), ((), ())), preferred_element_type=jnp.float32
    )
    merged = grad + error_buf[0].astype(jnp.float32)
    left_term = lax.dot_general(q_init, merged, (((1,), (1,)), ((), ())), precision=highest)
    left = lax.psum(left_term, ("dp", "tensor"))
    gram = jnp.dot(left, left.T, precision=highest)
    chol = jnp.linalg.cholesky(gram)
    basis = lax.linalg.triangular_solve(chol, left, left_side=True, lower=True)
    right_term = jnp.dot(basis, merged, precision=highest)
    q_factor = lax.psum(right_term, "dp") / n_replicas
    approx = lax.dot_general(basis, q_factor, (((0,), (0,)), ((), ())), precision=highest)
    new_error = (merged - approx).astype(jnp.bfloat16)[None]
    return (input_grad, new_error, basis, q_factor)


def solution(mesh):
    return jax.shard_map(
        body,
        mesh=mesh,
        in_specs=(
            P("dp", None),
            P("dp", "tensor"),
            P(None, "tensor"),
            P("dp", None, "tensor"),
            P(None, "tensor"),
        ),
        out_specs=(P(("dp", "tensor"), None), P("dp", None, "tensor"), P(), P(None, "tensor")),
        check_vma=False,
    )
```

profile of v0, /device:TPU:0, one launch (start us, length us, event | category | flops | bytes accessed | tf_op | source)
XLA Modules:
  0.0 329.4 jit_solution(1678615541551362874)
XLA Ops:
  8.0 0.0 copy-start
  8.0 0.0 copy-start.4
  8.0 0.0 all-reduce.3.cloned.1.call-start
  8.1 1.1 copy-done
  9.2 10.4 %convert_add_fusion = f32[4096,896]{1,0:T(8,128)S(1)} fusion(bf16[1,4096,896]{2,1,0:T(8,128)(2,1)} %param.8, bf16[512,4096]{1,0:T(8,128)(2,1)} %param.5, bf16[512,896]{1,0:T(8,128)(2,1)S(1)} %copy-done), kind=kOutput, calls=%fused_computation | convolution fusion | flops 3765436416 | bytes 27131904 | tf_op jit(solution)/shard_map/dot_general | solution.py:18
  19.6 0.0 copy-start.1
  19.6 5.2 %copy-done.1 = f32[4096,896]{1,0:T(8,128)} copy-done((f32[4096,896]{1,0:T(8,128)}, f32[4096,896]{1,0:T(8,128)S(1)}, u32[]{:S(2)}) %copy-start.1) | copy-done | bytes 14680088
  24.8 0.0 copy-done.4
  24.8 15.5 %convolution_bitcast_fusion = f32[64,4096]{1,0:T(8,128)} fusion(f32[4096,896]{1,0:T(8,128)S(1)} %convert_add_fusion, f32[64,896]{1,0:T(8,128)S(1)} %copy-done.4), kind=kOutput, calls=%fused_computation.3 | convolution fusion | flops 2818572288 | bytes 15958016 | tf_op jit(solution)/shard_map/dot_general | solution.py:22
  40.3 0.0 all-reduce.3.cloned.1.call-update
  40.3 0.3 all-reduce.5.cloned.1.call-start
  40.5 149.0 %all-reduce.3.cloned.1.call-done = f32[64,4096]{1,0:T(8,128)} async-done(((f32[64,4096]{1,0:T(8,128)}), f32[64,4096]{1,0:T(8,128)}) %all-reduce.3.cloned.1.call-update) | async-done | bytes 1048592 | tf_op jit(solution)/shard_map/psum | solution.py:23
  189.6 2.5 fusion.6
  192.1 0.1 copy.9
  192.2 5.8 %cholesky.16 = f32[64,64]{1,0:T(8,128)S(1)} custom-call(f32[64,64]{1,0:T(8,128)S(1)} %fusion.4), custom_call_target="Cholesky" | custom-call | tf_op jit(solution)/shard_map/jit(cholesky)/cholesky | solution.py:25
  198.1 0.6 compare_reduce_fusion
  198.7 0.7 fusion.1
  199.4 4.9 %custom-call.6 = f32[1,64,64]{1,2,0:T(8,128)S(1)} custom-call(f32[1,64,64]{2,1,0:T(8,128)S(1)} %fusion.1), custom_call_target="InvertDiagBlocksLowerTriangular" | custom-call | tf_op jit(solution)/shard_map/triangular_solve | solution.py:26
  204.3 2.3 fusion.2
  206.5 0.0 copy-start.2
  206.6 12.7 %fusion.7 = f32[64,896]{1,0:T(8,128)} fusion(f32[64,4096]{1,0:T(8,128)S(1)} %fusion.2, f32[4096,896]{1,0:T(8,128)} %copy-done.1), kind=kOutput, calls=%fused_computation.17 | convolution fusion | flops 2818572288 | bytes 15958016 | tf_op jit(solution)/shard_map/dot_general | solution.py:27
  219.3 0.0 all-reduce.5.cloned.1.call-update
  219.3 0.3 reduce-scatter.2.cloned.1.call-start
  219.6 9.9 %fusion.5 = f32[512,4096]{1,0:T(8,128)} fusion(bf16[512,896]{1,0:T(8,128)(2,1)S(1)} %copy-done, bf16[4096,896]{1,0:T(8,128)(2,1)} %param.7), kind=kOutput, calls=%fused_computation.15 | convolution fusion | flops 3758096384 | bytes 16646144 | tf_op jit(solution)/shard_map/dot_general | solution.py:11
  229.5 0.0 reduce-scatter.2.cloned.1.call-update
  229.5 73.6 %all-reduce.5.cloned.1.call-done = f32[64,896]{1,0:T(8,128)} async-done(((f32[64,896]{1,0:T(8,128)}), f32[64,896]{1,0:T(8,128)}) %all-reduce.5.cloned.1.call-update) | async-done | bytes 229392 | tf_op jit(solution)/shard_map/psum | solution.py:28
  303.1 1.0 broadcast_multiply_fusion
  304.1 0.0 copy-done.2
  304.1 0.0 copy-start.3
  304.1 15.8 %fusion = bf16[1,4096,896]{2,1,0:T(8,128)(2,1)} fusion(f32[4096,896]{1,0:T(8,128)} %copy-done.1, f32[64,4096]{1,0:T(8,128)S(1)} %fusion.2, f32[64,896]{1,0:T(8,128)S(1)} %broadcast_multiply_fusion), kind=kOutput, calls=%fused_computation.2 | convolution fusion | flops 2825912320 | bytes 23298048 | tf_op jit(solution)/shard_map/dot_general | solution.py:29
  319.9 0.0 copy-done.3
  319.9 0.0 reduce-scatter.2.cloned.1.call-done
  319.9 2.1 convert_element_type.12
  (2 shorter events, 0.0 us)
Async XLA Ops:
  8.0 1.2 copy-start
  8.0 16.8 %copy-start.4 = (f32[64,896]{1,0:T(8,128)S(1)}, f32[64,896]{1,0:T(8,128)}, u32[]{:S(2)}) copy-start(f32[64,896]{1,0:T(8,128)} %param.9) | copy-start | bytes 688132
  8.0 181.5 %all-reduce.3.cloned.1.call-start = ((), (), s32[]{:S(2)}) async-start(), calls=%async_computation.2 | async-start | bytes 2097152 | tf_op jit(solution)/shard_map/psum | solution.py:23
  19.6 5.2 %copy-start.1 = (f32[4096,896]{1,0:T(8,128)}, f32[4096,896]{1,0:T(8,128)S(1)}, u32[]{:S(2)}) copy-start(f32[4096,896]{1,0:T(8,128)S(1)} %convert_add_fusion) | copy-start | bytes 44040196
  40.3 262.9 %all-reduce.5.cloned.1.call-start = ((), (), s32[]{:S(2)}) async-start(), calls=%async_computation.3 | async-start | bytes 458752 | tf_op jit(solution)/shard_map/psum | solution.py:28
  206.5 97.6 %copy-start.2 = (f32[64,4096]{1,0:T(8,128)}, f32[64,4096]{1,0:T(8,128)S(1)}, u32[]{:S(2)}) copy-start(f32[64,4096]{1,0:T(8,128)S(1)} %fusion.2) | copy-start | bytes 3145732
  219.3 100.6 %reduce-scatter.2.cloned.1.call-start = ((), (), s32[]{:S(2)}) async-start(), calls=%async_computation.1 | async-start | bytes 9437184 | tf_op jit(solution)/shard_map/reduce_scatter | solution.py:10
  304.1 15.8 %copy-start.3 = (f32[64,896]{1,0:T(8,128)}, f32[64,896]{1,0:T(8,128)S(1)}, u32[]{:S(2)}) copy-start(f32[64,896]{1,0:T(8,128)S(1)} %broadcast_multiply_fusion) | copy-start | bytes 688132
Sparse Core Ops, SparseCore 0:
  40.4 149.1 all-reduce.2
  219.4 83.6 all-reduce.4
Sparse Core Ops, SparseCore 1:
  229.6 51.5 reduce-scatter.1
where the time goes:
time: 330 us; the launch traced here: 329 us
  waiting for transfers between devices  223 us (68%)
  matrix products  69 us (21%)
  between operations  15.6 us (5%)
  other arithmetic  15.1 us (5%)
  local copies, waits for them, and re-layouts  6.42 us (2%)
    psum x1, waiting for transfers between devices, body(): left = lax.psum(left_term, ('dp', 'tensor'))  149 us
    psum x1, waiting for transfers between devices, body(): q_factor = lax.psum(right_term, 'dp') / n_replicas  73.6 us
    dot_general x1, matrix products, body(): lax.dot_general(basis, q_factor, (((0,), (0,)), ((), ())), precision=high...  15.8 us
    dot_general x1, matrix products, body(): lax.dot_general(q_init, merged, (((1,), (1,)), ((), ())), precision=highest)  15.5 us
    dot_general x1, matrix products, body(): right_term = jnp.dot(basis, merged, precision=highest)  12.7 us
    dot_general x1, matrix products, body(): lax.dot_general(acts, up_cot, (((0,), (0,)), ((), ())), preferred_element...  10.4 us
    dot_general x1, matrix products, body(): lax.dot_general(up_cot, up_weight, (((1,), (1,)), ((), ())), preferred_el...  9.87 us
  transfers between devices with their start and end apart: 3, of which 2 were waited for; matrix products, arithmetic and copies ran while one was open for 8% of the time, Pallas kernels for 0%

commit v1 on v0

v1 whole, which is shorter than its diff:
```python
import jax
import jax.numpy as jnp
from jax import lax
from jax.experimental import pallas as pl
from jax.experimental.pallas import tpu as pltpu
from jax.sharding import PartitionSpec as P

F32 = jnp.float32
BF16 = jnp.bfloat16
HIGHEST = lax.Precision.HIGHEST
RANK = 64
LANES = 128
VMEM = pl.BlockSpec(memory_space=pltpu.VMEM)
NT = (((1,), (1,)), ((), ()))
TN = (((0,), (0,)), ((), ()))


def params(mib):
    return pltpu.CompilerParams(vmem_limit_bytes=mib << 20)


def cost(flops, nbytes):
    return pl.CostEstimate(flops=flops, bytes_accessed=nbytes, transcendentals=0)


def split3(x):
    high = x.astype(BF16)
    rest = x - high.astype(F32)
    mid = rest.astype(BF16)
    low = (rest - mid.astype(F32)).astype(BF16)
    return jnp.concatenate([high, mid, low], axis=0)


def sum3(y):
    return (y[2 * RANK : 3 * RANK] + y[RANK : 2 * RANK]) + y[:RANK]


def dot(a, b, dims=(((1,), (0,)), ((), ()))):
    return lax.dot_general(a, b, dims, preferred_element_type=F32)


def left_kernel(half_ref, q_ref, cot_ref, acts_ref, error_ref, out_ref, q3_ref, p3_ref):
    @pl.when(pl.program_id(0) == 0)
    def _():
        q3_ref[...] = split3(q_ref[...])
        p3_ref[...] = split3(sum3(dot(q3_ref[...], cot_ref[...], NT)))

    term = dot(q3_ref[...], error_ref[...], NT) + dot(p3_ref[...], acts_ref[...])
    left = sum3(term)
    for j in range(left.shape[1] // LANES):
        for g in range(4):
            out_ref[4 * j + g] = left[16 * g : 16 * g + 16, LANES * j : LANES * (j + 1)]


def left_half(half, q, cot, acts, error, tile=512):
    tokens, d = acts.shape
    ff = cot.shape[1]
    steps = d // 2 // tile
    return pl.pallas_call(
        left_kernel,
        grid_spec=pltpu.PrefetchScalarGridSpec(
            num_scalar_prefetch=1,
            grid=(steps,),
            in_specs=[
                pl.BlockSpec((RANK, ff), lambda i, h: (0, 0)),
                pl.BlockSpec((tokens, ff), lambda i, h: (0, 0)),
                pl.BlockSpec((tokens, tile), lambda i, h: (0, h[0] * steps + i)),
                pl.BlockSpec((tile, ff), lambda i, h: (h[0] * steps + i, 0)),
            ],
            out_specs=pl.BlockSpec((tile // 32, 16, LANES), lambda i, h: (i, 0, 0)),
            scratch_shapes=[
                pltpu.VMEM((3 * RANK, ff), BF16),
                pltpu.VMEM((3 * RANK, tokens), BF16),
            ],
        ),
        out_shape=jax.ShapeDtypeStruct((d // 64, 16, LANES), F32),
        compiler_params=params(24),
        cost_estimate=cost(4 * 10**9, 6 << 20),
    )(half, q, cot, acts, error)


def spread_kernel(scale, in_ref, out_ref):
    n = in_ref.shape[0]
    total = in_ref[0]
    for i in range(1, n):
        total = total + in_ref[i]
    if scale != 1.0:
        total = total * scale
    for i in range(n):
        out_ref[i] = total


def spread(x, scale):
    return pl.pallas_call(
        lambda i, o: spread_kernel(scale, i, o),
        in_specs=[VMEM],
        out_specs=VMEM,
        out_shape=jax.ShapeDtypeStruct(x.shape, F32),
        compiler_params=params(8),
        cost_estimate=cost(10**6, 2 << 20),
    )(x)


def inverse_factor(gram):
    groups = RANK // 8
    a = [gram[8 * i : 8 * i + 8] for i in range(groups)]
    row = lax.broadcasted_iota(jnp.int32, (8, RANK), 0)
    col = lax.broadcasted_iota(jnp.int32, (8, RANK), 1)
    b = [jnp.where(row + 8 * i == col, 1.0, 0.0).astype(F32) for i in range(groups)]
    scale = []
    for k in range(groups):
        cols = [
            [jnp.broadcast_to(a[i][:, 8 * k + j : 8 * k + j + 1], (8, RANK)) if i >= k else None for i in range(groups)]
            for j in range(8)
        ]
        block_scale = jnp.zeros((8, RANK), F32)
        for j in range(8):
            pivot = jnp.broadcast_to(cols[j][k][j : j + 1], (8, RANK))
            inverse = 1.0 / pivot
            block_scale = jnp.where(row == j, lax.rsqrt(pivot), block_scale)
            row_a = jnp.broadcast_to(a[k][j : j + 1], (8, RANK))
            row_b = jnp.broadcast_to(b[k][j : j + 1], (8, RANK))
            entries = [jnp.broadcast_to(cols[m][k][j : j + 1], (8, RANK)) for m in range(j + 1, 8)]
            for i in range(k, groups):
                factor = cols[j][i] * inverse
                if i == k:
                    factor = jnp.where(row > j, factor, 0.0)
                a[i] = a[i] - factor * row_a
                b[i] = b[i] - factor * row_b
                for m in range(j + 1, 8):
                    cols[m][i] = cols[m][i] - factor * entries[m - j - 1]
        scale.append(block_scale)
    return jnp.concatenate([b[i] * scale[i] for i in range(groups)], axis=0)


def middle_kernel(half_ref, mine_ref, other_ref, error_ref, acts_ref, cot_ref, basis_ref, right_ref, left_ref):
    h = half_ref[0]
    width = left_ref.shape[2]
    for ref, place in ((mine_ref, h), (other_ref, 1 - h)):
        for j in range(width // LANES):
            for g in range(4):
                left_ref[place, 16 * g : 16 * g + 16, LANES * j : LANES * (j + 1)] = ref[4 * j + g]
    gram = jnp.zeros((RANK, RANK), F32)
    for p in range(2):
        part = left_ref[p]
        gram = gram + lax.dot_general(part, part, NT, precision=HIGHEST, preferred_element_type=F32)
    factor = inverse_factor(gram)
    term = None
    proj = None
    for p in range(2):
        part = lax.dot_general(factor, left_ref[p], (((1,), (0,)), ((), ())), precision=HIGHEST, preferred_element_type=F32)
        basis_ref[:, p * width : (p + 1) * width] = part
        part3 = split3(part)
        t = dot(part3, error_ref[p * width : (p + 1) * width])
        s = dot(part3, acts_ref[:, p * width : (p + 1) * width], NT)
        term = t if term is None else term + t
        proj = s if proj is None else proj + s
    right = sum3(term + dot(split3(sum3(proj)), cot_ref[...]))
    tiles = right.shape[1] // LANES
    for g in range(8):
        for j in range(tiles):
            v = g * tiles + j
            right_ref[v // 4, 8 * (v % 4) : 8 * (v % 4) + 8] = right[8 * g : 8 * g + 8, LANES * j : LANES * (j + 1)]
    for v in range(8 * tiles, 64):
        right_ref[v // 4, 8 * (v % 4) : 8 * (v % 4) + 8] = jnp.zeros((8, LANES), F32)


def middle(half, mine, other, error, acts, cot):
    d = error.shape[0]
    return pl.pallas_call(
        middle_kernel,
        in_specs=[pl.BlockSpec(memory_space=pltpu.SMEM)] + [VMEM] * 5,
        out_specs=[VMEM, VMEM],
        out_shape=[
            jax.ShapeDtypeStruct((RANK, d), F32),
            jax.ShapeDtypeStruct((16, 32, LANES), F32),
        ],
        scratch_shapes=[pltpu.VMEM((2, RANK, d // 2), F32)],
        compiler_params=params(32),
        cost_estimate=cost(4 * 10**9, 13 << 20),
    )(half, mine, other, error, acts, cot)


def merged_kernel(acts_ref, cot_ref, error_ref, out_ref):
    grad = lax.dot_general(acts_ref[...], cot_ref[...], TN, preferred_element_type=F32)
    out_ref[...] = grad + error_ref[...].astype(F32)


def merge(acts, cot, error, tile=512):
    tokens, d = acts.shape
    ff = cot.shape[1]
    return pl.pallas_call(
        merged_kernel,
        grid=(d // tile,),
        in_specs=[
            pl.BlockSpec((tokens, tile), lambda i: (0, i)),
            pl.BlockSpec((tokens, ff), lambda i: (0, 0)),
            pl.BlockSpec((tile, ff), lambda i: (i, 0)),
        ],
        out_specs=pl.BlockSpec((tile, ff), lambda i: (i, 0)),
        out_shape=jax.ShapeDtypeStruct((d, ff), F32),
        compiler_params=params(24),
        cost_estimate=cost(4 * 10**9, 27 << 20),
    )(acts, cot, error)


def prep_kernel(basis_ref, out_ref):
    x = basis_ref[...]
    high = x.astype(BF16)
    low = (x - high.astype(F32)).astype(BF16)
    both = jnp.concatenate([high, low], axis=0).T
    out_ref[:, : 2 * RANK] = both
    out_ref[:, 2 * RANK :] = both


def prep(basis, tile=1024):
    d = basis.shape[1]
    return pl.pallas_call(
        prep_kernel,
        grid=(d // tile,),
        in_specs=[pl.BlockSpec((RANK, tile), lambda i: (0, i))],
        out_specs=pl.BlockSpec((tile, 4 * RANK), lambda i: (i, 0)),
        out_shape=jax.ShapeDtypeStruct((d, 4 * RANK), BF16),
        compiler_params=params(16),
        cost_estimate=cost(10**7, 4 << 20),
    )(basis)


def final_kernel(chunks_ref, basis_ref, merged_ref, error_ref, q_ref, q4_ref):
    @pl.when(pl.program_id(0) == 0)
    def _():
        tiles = q_ref.shape[1] // LANES
        for g in range(8):
            for j in range(tiles):
                v = g * tiles + j
                q_ref[8 * g : 8 * g + 8, LANES * j : LANES * (j + 1)] = chunks_ref[v // 4, 8 * (v % 4) : 8 * (v % 4) + 8]
        q = q_ref[...]
        high = q.astype(BF16)
        low = (q - high.astype(F32)).astype(BF16)
        q4_ref[...] = jnp.concatenate([high, high, low, low], axis=0)

    error_ref[...] = (merged_ref[...] - dot(basis_ref[...], q4_ref[...])).astype(BF16)


def final(chunks, basis4, merged, tile=512):
    d, ff = merged.shape
    return pl.pallas_call(
        final_kernel,
        grid=(d // tile,),
        in_specs=[
            pl.BlockSpec(chunks.shape, lambda i: (0, 0, 0)),
            pl.BlockSpec((tile, 4 * RANK), lambda i: (i, 0)),
            pl.BlockSpec((tile, ff), lambda i: (i, 0)),
        ],
        out_specs=[
            pl.BlockSpec((tile, ff), lambda i: (i, 0)),
            pl.BlockSpec((RANK, ff), lambda i: (0, 0)),
        ],
        out_shape=[
            jax.ShapeDtypeStruct((d, ff), BF16),
            jax.ShapeDtypeStruct((RANK, ff), F32),
        ],
        scratch_shapes=[pltpu.VMEM((4 * RANK, ff), BF16)],
        compiler_params=params(24),
        cost_estimate=cost(2 * 10**9, 24 << 20),
    )(chunks, basis4, merged)


def body(acts, up_cot, up_weight, error_buf, q_init):
    n_dp = lax.axis_size("dp")
    n_tensor = lax.axis_size("tensor")
    both = ("dp", "tensor")
    groups = [[2 * i + c for i in range(n_dp * n_tensor // 2)] for c in range(2)]
    pairs = [(i, i ^ 1) for i in range(n_tensor)]
    error = error_buf[0]
    core = lax.rem(lax.axis_index("tensor"), 2).astype(jnp.int32).reshape(1)

    send = left_half(1 - core, q_init, up_cot, acts, error)
    received = lax.ppermute(send, "tensor", pairs)
    keep = left_half(core, q_init, up_cot, acts, error)
    chunks = lax.all_to_all(keep + received, both, 0, 0, axis_index_groups=groups)

    partial = lax.dot_general(up_cot, up_weight, NT, preferred_element_type=F32)
    input_grad = lax.psum_scatter(partial, "tensor", scatter_dimension=0, tiled=True)
    merged = merge(acts, up_cot, error)

    mine = lax.all_to_all(spread(chunks, 1.0), both, 0, 0, axis_index_groups=groups)
    other = lax.ppermute(mine, "tensor", pairs)
    basis, right = middle(core, mine, other, error, acts, up_cot)

    right = lax.all_to_all(right, "dp", 0, 0)
    basis4 = prep(basis)
    right = lax.all_to_all(spread(right, 1.0 / n_dp), "dp", 0, 0)
    new_error, q_factor = final(right, basis4, merged)
    return (input_grad.astype(BF16), new_error[None], basis, q_factor)


def solution(mesh):
    return jax.shard_map(
        body,
        mesh=mesh,
        in_specs=(
            P("dp", None),
            P("dp", "tensor"),
            P(None, "tensor"),
            P("dp", None, "tensor"),
            P(None, "tensor"),
        ),
        out_specs=(P(("dp", "tensor"), None), P("dp", None, "tensor"), P(), P(None, "tensor")),
        check_vma=False,
    )
```

time: 330 us -> 148 us (0.45)
  waiting for transfers between devices: 223 us -> 1.93 us
  blocking collectives: 0 us -> 61.4 us
  matrix products: 69 us -> 11.2 us
  Pallas kernels: 0 us -> 28.4 us
  local copies, waits for them, and re-layouts: 6.42 us -> 24.8 us
  other arithmetic: 15.1 us -> 2.14 us
    psum x2 -> x0, waiting for transfers between devices: 223 us -> none  [the longest x1 149 us: body(): left = lax.psum(left_term, ('dp', 'tensor'))]
    all_to_all x0 -> x3, blocking collectives: none -> 61.4 us  [the longest x1 28.9 us: body(): lax.all_to_all(keep + received, both, 0, 0, axis_index_groups=groups)]
    dot_general x6 -> x1, matrix products: 66.7 us -> 11.2 us  [body(): partial = lax.dot_general(up_cot, up_weight, NT, preferred_element_type=F32)]
    pallas_call x0 -> x8, Pallas kernels: none -> 28.4 us  [the longest x1 8.58 us: middle(): pl.pallas_call(middle_kernel, in_specs=[pl.BlockSpec(memory_space=pltpu.S...]
    unnamed x10 -> x28, local copies, waits for them, and re-layouts: 6.35 us -> 24.8 us
    another operation x5 -> x0, other arithmetic: 12.1 us -> none  [the longest x3 6.52 us: body(): chol = jnp.linalg.cholesky(gram)]
    all_to_all x0 -> x1, starting transfers between devices: none -> 3.53 us  [body(): right = lax.all_to_all(spread(right, 1.0 / n_dp), 'dp', 0, 0)]
  transfers between devices with their start and end apart: 3 -> 4, of which waited for: 2 -> 1; matrix products, arithmetic and copies ran while one was open for 8% -> 0% of each run, Pallas kernels for 0% -> 19%
where the time goes in v1:
time: 148 us
  blocking collectives  61.4 us (41%)
  Pallas kernels  28.4 us (19%)
  local copies, waits for them, and re-layouts  24.8 us (17%)
  between operations  14.2 us (10%)
  matrix products  11.2 us (8%)
  starting transfers between devices  3.66 us (2%)
  other arithmetic  2.14 us (1%)
  waiting for transfers between devices  1.93 us (1%)
    all_to_all x1, blocking collectives, body(): lax.all_to_all(keep + received, both, 0, 0, axis_index_groups=groups)  28.9 us
    unnamed x28, local copies, waits for them, and re-layouts  24.8 us
    all_to_all x1, blocking collectives, body(): lax.all_to_all(spread(chunks, 1.0), both, 0, 0, axis_index_groups=groups)  20.6 us
    all_to_all x1, blocking collectives, body(): right = lax.all_to_all(right, 'dp', 0, 0)  11.9 us
    dot_general x1, matrix products, body(): partial = lax.dot_general(up_cot, up_weight, NT, preferred_element_type=F32)  11.2 us
    pallas_call x1, Pallas kernels, middle(): pl.pallas_call(middle_kernel, in_specs=[pl.BlockSpec(memory_space=pltpu.S...  8.58 us
    pallas_call x1, Pallas kernels, merge(): pl.pallas_call(merged_kernel, grid=(d // tile,), in_specs=[pl.BlockSpec((...  6.33 us
    pallas_call x2, Pallas kernels, left_half(): pl.pallas_call(left_kernel, grid_spec=pltpu.PrefetchScalarGridSpec(num_sc...  5.99 us
  transfers between devices with their start and end apart: 4, of which 1 were waited for; matrix products, arithmetic and copies ran while one was open for 0% of the time, Pallas kernels for 19%

profile of v1, /device:TPU:0, one launch (start us, length us, event | category | flops | bytes accessed | tf_op | source)
XLA Modules:
  0.0 147.6 jit_solution(13258251628962180608)
XLA Ops:
  7.2 0.0 reduce-scatter.2.cloned.1.call-start
  7.2 11.2 %fusion = f32[512,4096]{1,0:T(8,128)} fusion(bf16[512,896]{1,0:T(8,128)(2,1)} %cot_ref.7, bf16[4096,896]{1,0:T(8,128)(2,1)} %param.7), kind=kOutput, calls=%fused_computation | convolution fusion | flops 3758096384 | bytes 16646144 | tf_op jit(solution)/shard_map/dot_general | solution.py:283
  18.4 0.0 copy-start.11
  18.4 0.0 slice-start
  18.4 0.0 reduce-scatter.2.cloned.1.call-update
  18.4 0.9 copy-done.11
  19.3 0.0 copy-start.2
  19.3 3.2 %copy-done.2 = bf16[1,4096,896]{2,1,0:T(8,128)(2,1)S(1)} copy-done((bf16[1,4096,896]{2,1,0:T(8,128)(2,1)S(1)}, bf16[1,4096,896]{2,1,0:T(8,128)(2,1)}, u32[]{:S(2)}) %copy-start.2) | copy-done | bytes 7340056
  22.5 0.0 copy-start.4
  22.5 2.2 %copy-done.4 = bf16[512,4096]{1,0:T(8,128)(2,1)S(1)} copy-done((bf16[512,4096]{1,0:T(8,128)(2,1)S(1)}, bf16[512,4096]{1,0:T(8,128)(2,1)}, u32[]{:S(2)}) %copy-start.4) | copy-done | bytes 4194328
  24.7 0.0 copy-start.8
  24.7 1.2 copy-done.8
  25.9 0.0 slice-start.1
  25.9 0.0 copy-start.5
  25.9 0.0 copy-start.9
  25.9 3.0 %shard_map.85 = f32[64,16,128]{2,1,0:T(8,128)S(1)} custom-call(s32[1]{0:T(128)S(6)} %sub.3.half_ref, f32[64,896]{1,0:T(8,128)S(1)} %copy-done.11, bf16[512,896]{1,0:T(8,128)(2,1)S(1)} %copy-done.8, bf16[512,4096]{1,0:T(8,128)(2,1)S(1)} %copy-done.4, bf16[4096,896]{1,0:T(8,128)(2,1)S(1)} %bitcast.5), custom_call_target="tpu_custom_call" | custom-call | flops 4000000000 | bytes 6291456 | tf_op jit(solution)/shard_map/pallas_call | solution.py:59
  28.9 0.1 collective-permute-start
  29.0 0.0 slice-done
  29.0 0.0 slice-done.1
  29.0 0.3 copy-done.5
  29.4 0.2 copy-done.9
  29.5 3.0 %shard_map.84 = f32[64,16,128]{2,1,0:T(8,128)S(1)} custom-call(s32[1]{0:T(128)} %bitcast.half_ref, f32[64,896]{1,0:T(8,128)S(1)} %copy-done.11, bf16[512,896]{1,0:T(8,128)(2,1)S(1)} %copy-done.9, bf16[512,4096]{1,0:T(8,128)(2,1)S(1)} %copy-done.5, bf16[4096,896]{1,0:T(8,128)(2,1)S(1)} %bitcast.8), custom_call_target="tpu_custom_call" | custom-call | flops 4000000000 | bytes 6291456 | tf_op jit(solution)/shard_map/pallas_call | solution.py:59
  32.6 0.0 collective-permute-done
  32.6 0.1 add.5
  32.6 28.9 %all_to_all.20.i = f32[64,16,128]{2,1,0:T(8,128)S(1)} all-to-all(f32[64,16,128]{2,1,0:T(8,128)S(1)} %add.5), channel_id=1, replica_groups={{0,2,4,6,8,10,12,14,16,18,20,22,24,26,28,30,32,34,36,38,40,42,44,46,48,..., dimensions={0} | all-to-all | bytes 1048576 | tf_op jit(solution)/shard_map/all_to_all | solution.py:281
  61.6 0.1 shard_map.86
  61.7 20.6 %all_to_all.21.mine_ref = f32[64,16,128]{2,1,0:T(8,128)S(1)} all-to-all(f32[64,16,128]{2,1,0:T(8,128)S(1)} %shard_map.86), channel_id=1, replica_groups={{0,2,4,6,8,10,12,14,16,18,20,22,24,26,28,30,32,34,36,38,40,42,44,46,48,..., dimensions={0} | all-to-all | bytes 1048576 | tf_op jit(solution)/shard_map/all_to_all | solution.py:287
  82.3 0.0 collective-permute-start.1
  82.3 1.9 %collective-permute-done.1.other_ref = f32[64,16,128]{2,1,0:T(8,128)S(1)} collective-permute-done((f32[64,16,128]{2,1,0:T(8,128)S(1)}, f32[64,16,128]{2,1,0:T(8,128)S(1)}, u32[]{:S(2)}, u32[]{:S(2)}) %collective-permute-start.1) | collective-permute-done | bytes 524320 | tf_op jit(solution)/shard_map/ppermute | solution.py:288
  84.2 8.6 %shard_map.87 = (f32[64,4096]{1,0:T(8,128)}, f32[16,32,128]{2,1,0:T(8,128)S(1)}) custom-call(s32[1]{0:T(128)} %bitcast.half_ref, f32[64,16,128]{2,1,0:T(8,128)S(1)} %all_to_all.21.mine_ref, f32[64,16,128]{2,1,0:T(8,128)S(1)} %collective-permute-done.1.other_ref, bf16[4096,896]{1,0:T(8,128)(2,1)S(1)} %bitcast.9, bf16[512,4096]{1,0:T(8,128)(2,1)S(1)} %copy-done.5, ...), custom_call_target="tpu_custom_call" | custom-call | flops 4000000000 | bytes 13631488 | tf_op jit(solution)/shard_map/pallas_call | solution.py:170
  92.8 11.9 %all_to_all.22.i = f32[16,32,128]{2,1,0:T(8,128)S(1)} all-to-all(f32[16,32,128]{2,1,0:T(8,128)S(1)} %get-tuple-element.8), channel_id=1, replica_groups=mesh['dp'=16,'tensor'=8] {'dp'}, dimensions={0} | all-to-all | bytes 524288 | tf_op jit(solution)/shard_map/all_to_all | solution.py:291
  104.6 0.7 shard_map.88
  105.4 3.5 %all-to-all-start.3 = ((f32[16,32,128]{2,1,0:T(8,128)}), f32[16,32,128]{2,1,0:T(8,128)S(1)}, u32[]{:S(2)}, u32[]{:S(2)}) async-start(f32[16,32,128]{2,1,0:T(8,128)} %shard_map.88), calls=%async_computation.4 | async-start | bytes 524288 | tf_op jit(solution)/shard_map/all_to_all | solution.py:293
  108.9 0.0 copy-start.3
  108.9 3.1 %copy-done.3 = bf16[1,4096,896]{2,1,0:T(8,128)(2,1)S(1)} copy-done((bf16[1,4096,896]{2,1,0:T(8,128)(2,1)S(1)}, bf16[1,4096,896]{2,1,0:T(8,128)(2,1)}, u32[]{:S(2)}) %copy-start.3) | copy-done | bytes 7340056
  112.0 0.0 copy-start.6
  112.0 2.2 %copy-done.6 = bf16[512,4096]{1,0:T(8,128)(2,1)S(1)} copy-done((bf16[512,4096]{1,0:T(8,128)(2,1)S(1)}, bf16[512,4096]{1,0:T(8,128)(2,1)}, u32[]{:S(2)}) %copy-start.6) | copy-done | bytes 4194328
  114.2 0.0 copy-start.10
  114.2 1.2 copy-done.10
  115.4 0.0 copy-start.7
  115.4 6.3 %shard_map.90.merged_ref = f32[4096,896]{1,0:T(8,128)S(1)} custom-call(bf16[512,4096]{1,0:T(8,128)(2,1)S(1)} %copy-done.6, bf16[512,896]{1,0:T(8,128)(2,1)S(1)} %copy-done.10, bf16[4096,896]{1,0:T(8,128)(2,1)S(1)} %bitcast.10), custom_call_target="tpu_custom_call" | custom-call | flops 4000000000 | bytes 28311552 | tf_op jit(solution)/shard_map/pallas_call | solution.py:192
  121.7 0.0 copy-start
  121.7 5.2 %copy-done = f32[4096,896]{1,0:T(8,128)} copy-done((f32[4096,896]{1,0:T(8,128)}, f32[4096,896]{1,0:T(8,128)S(1)}, u32[]{:S(2)}) %copy-start) | copy-done | bytes 14680088
  126.9 0.0 copy-done.7
  126.9 0.6 shard_map.89.basis_ref
  127.6 0.0 all-to-all-done.3.chunks_ref
  127.6 0.0 copy-start.1
  127.6 5.2 %copy-done.1 = f32[4096,896]{1,0:T(8,128)S(1)} copy-done((f32[4096,896]{1,0:T(8,128)S(1)}, f32[4096,896]{1,0:T(8,128)}, u32[]{:S(2)}) %copy-start.1) | copy-done | bytes 14680088
  132.7 6.0 %shard_map.91 = (bf16[4096,896]{1,0:T(8,128)(2,1)}, f32[64,896]{1,0:T(8,128)}) custom-call(f32[16,32,128]{2,1,0:T(8,128)S(1)} %all-to-all-done.3.chunks_ref, bf16[4096,256]{1,0:T(8,128)(2,1)S(1)} %shard_map.89.basis_ref, f32[4096,896]{1,0:T(8,128)S(1)} %copy-done.1), custom_call_target="tpu_custom_call" | custom-call | flops 2000000000 | bytes 25165824 | tf_op jit(solution)/shard_map/pallas_call | solution.py:247
  138.7 0.0 reduce-scatter.2.cloned.1.call-done
  138.7 2.1 %convert_element_type.3 = bf16[64,4096]{1,0:T(8,128)(2,1)} convert(f32[64,4096]{1,0:T(8,128)} %reduce-scatter.2.cloned.1.call-done) | non-fusion elementwise | flops 262144 | bytes 1572864 | tf_op jit(solution)/shard_map/convert_element_type | solution.py:295
  (1 shorter events, 0.0 us)
Async XLA Ops:
  7.2 131.6 %reduce-scatter.2.cloned.1.call-start = ((), (), s32[]{:S(2)}) async-start(), calls=%async_computation.5 | async-start | bytes 9437184 | tf_op jit(solution)/shard_map/reduce_scatter | solution.py:284
  18.4 0.9 copy-start.11
  18.4 10.6 %slice-start = ((s8[7340032]{0:T(1024)(128)(4,1)}), s8[3145728]{0:T(1024)(128)(4,1)S(1)}, s32[]{:S(2)}) async-start(s8[7340032]{0:T(1024)(128)(4,1)} %bitcast.6), calls=%async_computation.6 | async-start | bytes 6291456
  19.3 3.2 %copy-start.2 = (bf16[1,4096,896]{2,1,0:T(8,128)(2,1)S(1)}, bf16[1,4096,896]{2,1,0:T(8,128)(2,1)}, u32[]{:S(2)}) copy-start(bf16[1,4096,896]{2,1,0:T(8,128)(2,1)} %param.8) | copy-start | bytes 22020100
  22.5 2.2 %copy-start.4 = (bf16[512,4096]{1,0:T(8,128)(2,1)S(1)}, bf16[512,4096]{1,0:T(8,128)(2,1)}, u32[]{:S(2)}) copy-start(bf16[512,4096]{1,0:T(8,128)(2,1)} %acts_ref.7) | copy-start | bytes 12582916
  24.7 1.2 copy-start.8
  25.9 3.1 %slice-start.1 = ((s8[7340032]{0:T(1024)(128)(4,1)}), s8[4194304]{0:T(1024)(128)(4,1)S(1)}, s32[]{:S(2)}) async-start(s8[7340032]{0:T(1024)(128)(4,1)} %bitcast.6), calls=%async_computation.7 | async-start | bytes 8388608
  25.9 3.5 %copy-start.5 = (bf16[512,4096]{1,0:T(8,128)(2,1)S(1)}, bf16[512,4096]{1,0:T(8,128)(2,1)}, u32[]{:S(2)}) copy-start(bf16[512,4096]{1,0:T(8,128)(2,1)} %acts_ref.7) | copy-start | bytes 12582916
  25.9 3.6 %copy-start.9 = (bf16[512,896]{1,0:T(8,128)(2,1)S(1)}, bf16[512,896]{1,0:T(8,128)(2,1)}, u32[]{:S(2)}) copy-start(bf16[512,896]{1,0:T(8,128)(2,1)} %cot_ref.7) | copy-start | bytes 2752516
  28.9 3.6 %collective-permute-start = (f32[64,16,128]{2,1,0:T(8,128)S(1)}, f32[64,16,128]{2,1,0:T(8,128)S(1)}, u32[]{:S(2)}, u32[]{:S(2)}) collective-permute-start(f32[64,16,128]{2,1,0:T(8,128)S(1)} %shard_map.85), channel_id=1, source_target_pairs={{0,1},{1,0},{2,3},{3,2},{4,5},{5,4},{6,7},{7,6},{8,9},{9,8},{10,11... | collective-permute-start | bytes 1572872 | tf_op jit(solution)/shard_map/ppermute | solution.py:279
  82.3 1.9 %collective-permute-start.1 = (f32[64,16,128]{2,1,0:T(8,128)S(1)}, f32[64,16,128]{2,1,0:T(8,128)S(1)}, u32[]{:S(2)}, u32[]{:S(2)}) collective-permute-start(f32[64,16,128]{2,1,0:T(8,128)S(1)} %all_to_all.21.mine_ref), channel_id=1, source_target_pairs={{0,1},{1,0},{2,3},{3,2},{4,5},{5,4},{6,7},{7,6},{8,9},{9,8},{10,11... | collective-permute-start | bytes 1572872 | tf_op jit(solution)/shard_map/ppermute | solution.py:288
  105.4 22.2 %all-to-all-start.3 = ((f32[16,32,128]{2,1,0:T(8,128)}), f32[16,32,128]{2,1,0:T(8,128)S(1)}, u32[]{:S(2)}, u32[]{:S(2)}) async-start(f32[16,32,128]{2,1,0:T(8,128)} %shard_map.88), calls=%async_computation.4 | async-start | bytes 524288 | tf_op jit(solution)/shard_map/all_to_all | solution.py:293
  108.9 3.1 %copy-start.3 = (bf16[1,4096,896]{2,1,0:T(8,128)(2,1)S(1)}, bf16[1,4096,896]{2,1,0:T(8,128)(2,1)}, u32[]{:S(2)}) copy-start(bf16[1,4096,896]{2,1,0:T(8,128)(2,1)} %param.8) | copy-start | bytes 22020100
  112.0 2.2 %copy-start.6 = (bf16[512,4096]{1,0:T(8,128)(2,1)S(1)}, bf16[512,4096]{1,0:T(8,128)(2,1)}, u32[]{:S(2)}) copy-start(bf16[512,4096]{1,0:T(8,128)(2,1)} %acts_ref.7) | copy-start | bytes 12582916
  114.2 1.2 copy-start.10
  115.4 11.6 %copy-start.7 = (f32[64,4096]{1,0:T(8,128)S(1)}, f32[64,4096]{1,0:T(8,128)}, u32[]{:S(2)}) copy-start(f32[64,4096]{1,0:T(8,128)} %get-tuple-element.6.basis_ref) | copy-start | bytes 3145732
  121.7 5.2 %copy-start = (f32[4096,896]{1,0:T(8,128)}, f32[4096,896]{1,0:T(8,128)S(1)}, u32[]{:S(2)}) copy-start(f32[4096,896]{1,0:T(8,128)S(1)} %shard_map.90.merged_ref) | copy-start | bytes 44040196
  127.6 5.2 %copy-start.1 = (f32[4096,896]{1,0:T(8,128)S(1)}, f32[4096,896]{1,0:T(8,128)}, u32[]{:S(2)}) copy-start(f32[4096,896]{1,0:T(8,128)} %copy-done) | copy-start | bytes 44040196
Sparse Core Ops, SparseCore 0:
  18.6 66.0 reduce-scatter.1

commit v2 on v0

v2 whole, which is shorter than its diff:
```python
import jax
import jax.numpy as jnp
from jax import lax
from jax.experimental import pallas as pl
from jax.experimental.pallas import tpu as pltpu
from jax.sharding import PartitionSpec as P

F32 = jnp.float32
BF16 = jnp.bfloat16
HIGHEST = lax.Precision.HIGHEST
RANK = 64
LANES = 128
VMEM = pl.BlockSpec(memory_space=pltpu.VMEM)
HBM = pl.BlockSpec(memory_space=pltpu.HBM)
NN = (((1,), (0,)), ((), ()))
NT = (((1,), (1,)), ((), ()))
TN = (((0,), (0,)), ((), ()))


def shape(dims, dtype=F32):
    return jax.ShapeDtypeStruct(dims, dtype)


def call(kernel, args, specs, outs, out_specs, scratch, n_sems, limit=56 << 20):
    return pl.pallas_call(
        kernel,
        in_specs=specs,
        out_specs=out_specs,
        out_shape=outs,
        scratch_shapes=[pltpu.VMEM(dims, dtype) for dims, dtype in scratch] + [pltpu.SemaphoreType.DMA((n_sems,))],
        compiler_params=pltpu.CompilerParams(vmem_limit_bytes=limit),
        cost_estimate=pl.CostEstimate(flops=10**6, bytes_accessed=10**5, transcendentals=0),
    )(*args)


class Copies:
    def __init__(self, sems):
        self.sems = sems
        self.all = []

    def start(self, src, dst):
        copy = pltpu.make_async_copy(src, dst, self.sems.at[len(self.all)])
        copy.start()
        self.all.append(copy)
        return copy


def split3(x):
    high = x.astype(BF16)
    rest = x - high.astype(F32)
    mid = rest.astype(BF16)
    low = (rest - mid.astype(F32)).astype(BF16)
    return jnp.concatenate([high, mid, low], axis=0)


def sum3(y):
    return (y[2 * RANK : 3 * RANK] + y[RANK : 2 * RANK]) + y[:RANK]


def dot(a, b, dims=NN):
    return lax.dot_general(a, b, dims, preferred_element_type=F32)


def dot_highest(a, b):
    return lax.dot_general(a, b, NN, precision=HIGHEST, preferred_element_type=F32)


def my_core():
    return lax.rem(lax.axis_index("tensor"), 2)


def part_of(place, width, i, parts):
    step = width // parts
    return pl.ds(pl.multiple_of(place * width + i * step, step), step)


PARTS = 4


def left_part(q3t, p3, error, acts):
    y = dot(error, q3t)
    by_error = (y[:, 2 * RANK :] + y[:, RANK : 2 * RANK]) + y[:, :RANK]
    return by_error.T + sum3(dot(p3, acts))


def store_left(out_ref, i, left):
    tiles = left.shape[1] // LANES
    for j in range(tiles):
        for g in range(4):
            out_ref[4 * (i * tiles + j) + g] = left[16 * g : 16 * g + 16, LANES * j : LANES * (j + 1)]


def half_shapes(tokens, d, ff, parts):
    step = d // 2 // parts
    return [(parts, step, ff), (parts, tokens, step)]


def fetch_half(copies, place, error_hbm, acts_hbm, error_ref, acts_ref):
    width = error_hbm.shape[0] // 2
    parts = error_ref.shape[0]
    started = []
    for i in range(parts):
        at = part_of(place, width, i, parts)
        started.append(
            (copies.start(error_hbm.at[at, :], error_ref.at[i]), copies.start(acts_hbm.at[:, at], acts_ref.at[i]))
        )
    return started


def left_send_kernel(
    q_hbm,
    cot_hbm,
    acts_hbm,
    error_hbm,
    out_ref,
    q3t_ref,
    p3_ref,
    error_keep_ref,
    acts_keep_ref,
    q_ref,
    cot_ref,
    error_ref,
    acts_ref,
    sems,
):
    core = my_core()
    copies = Copies(sems)
    q_copy = copies.start(q_hbm, q_ref)
    cot_copy = copies.start(cot_hbm, cot_ref)
    now = fetch_half(copies, 1 - core, error_hbm, acts_hbm, error_ref, acts_ref)
    later = fetch_half(copies, core, error_hbm, acts_hbm, error_keep_ref, acts_keep_ref)
    q_copy.wait()
    q3 = split3(q_ref[...])
    q3t = q3.T
    q3t_ref[...] = q3t
    cot_copy.wait()
    p3 = split3(sum3(dot(q3, cot_ref[...], NT)))
    p3_ref[...] = p3
    for i, pair in enumerate(now):
        for copy in pair:
            copy.wait()
        store_left(out_ref, i, left_part(q3t, p3, error_ref[i], acts_ref[i]))
    for pair in later:
        for copy in pair:
            copy.wait()


def left_send(q, cot, acts, error):
    tokens, d = acts.shape
    ff = cot.shape[1]
    halves = half_shapes(tokens, d, ff, PARTS)
    return call(
        left_send_kernel,
        (q, cot, acts, error),
        [HBM] * 4,
        [shape((d // 64, 16, LANES)), shape((ff, 3 * RANK), BF16), shape((3 * RANK, tokens), BF16)]
        + [shape(s, BF16) for s in halves],
        [VMEM] * 5,
        [((RANK, ff), F32), ((tokens, ff), BF16)] + [(s, BF16) for s in halves],
        2 + 4 * PARTS,
        limit=44 << 20,
    )


def left_keep_kernel(q3t_ref, p3_ref, error_ref, acts_ref, out_ref):
    for i in range(error_ref.shape[0]):
        store_left(out_ref, i, left_part(q3t_ref[...], p3_ref[...], error_ref[i], acts_ref[i]))


def left_keep(held, dims):
    return pl.pallas_call(
        left_keep_kernel,
        in_specs=[VMEM] * 4,
        out_specs=VMEM,
        out_shape=shape(dims),
        compiler_params=pltpu.CompilerParams(vmem_limit_bytes=10 << 20),
        cost_estimate=pl.CostEstimate(flops=10**6, bytes_accessed=10**5, transcendentals=0),
    )(*held)


def spread_kernel(scale, in_ref, out_ref):
    n = in_ref.shape[0]
    total = in_ref[0]
    for i in range(1, n):
        total = total + in_ref[i]
    if scale != 1.0:
        total = total * scale
    for i in range(n):
        out_ref[i] = total


def spread(x, scale):
    return pl.pallas_call(
        lambda i, o: spread_kernel(scale, i, o),
        in_specs=[VMEM],
        out_specs=VMEM,
        out_shape=shape(x.shape),
        compiler_params=pltpu.CompilerParams(vmem_limit_bytes=8 << 20),
        cost_estimate=pl.CostEstimate(flops=10**6, bytes_accessed=10**5, transcendentals=0),
    )(x)


def inverse_factor(gram):
    groups = RANK // 8
    a = [gram[8 * i : 8 * i + 8] for i in range(groups)]
    row = lax.broadcasted_iota(jnp.int32, (8, RANK), 0)
    col = lax.broadcasted_iota(jnp.int32, (8, RANK), 1)
    b = [jnp.where(row + 8 * i == col, 1.0, 0.0).astype(F32) for i in range(groups)]
    scale = []
    for k in range(groups):
        cols = [
            [jnp.broadcast_to(a[i][:, 8 * k + j : 8 * k + j + 1], (8, RANK)) if i >= k else None for i in range(groups)]
            for j in range(8)
        ]
        block_scale = jnp.zeros((8, RANK), F32)
        for j in range(8):
            pivot = jnp.broadcast_to(cols[j][k][j : j + 1], (8, RANK))
            inverse = 1.0 / pivot
            block_scale = jnp.where(row == j, lax.rsqrt(pivot), block_scale)
            row_a = jnp.broadcast_to(a[k][j : j + 1], (8, RANK))
            row_b = jnp.broadcast_to(b[k][j : j + 1], (8, RANK))
            entries = [jnp.broadcast_to(cols[m][k][j : j + 1], (8, RANK)) for m in range(j + 1, 8)]
            for i in range(k, groups):
                factor = cols[j][i] * inverse
                if i == k:
                    factor = jnp.where(row > j, factor, 0.0)
                a[i] = a[i] - factor * row_a
                b[i] = b[i] - factor * row_b
                for m in range(j + 1, 8):
                    cols[m][i] = cols[m][i] - factor * entries[m - j - 1]
        scale.append(block_scale)
    return jnp.concatenate([b[i] * scale[i] for i in range(groups)], axis=0)


def half_of(chunks_ref):
    n = chunks_ref.shape[0] // 4
    return jnp.concatenate(
        [jnp.concatenate([chunks_ref[4 * j + g] for j in range(n)], axis=1) for g in range(4)], axis=0
    )


def half_terms(left, error_ref, acts_ref, ready=None):
    parts, step = error_ref.shape[:2]
    left3 = split3(left)
    gram = [sum3(dot(left3, left3[RANK * i : RANK * (i + 1)], NT)) for i in range(3)]
    with_error = with_acts = None
    for i in range(parts):
        part = left3[:, i * step : (i + 1) * step]
        if ready is not None:
            for copy in ready[i]:
                copy.wait()
        e = dot(part, error_ref[i])
        a = dot(part, acts_ref[i], NT)
        with_error = e if i == 0 else with_error + e
        with_acts = a if i == 0 else with_acts + a
    return (gram[2] + gram[1]) + gram[0], sum3(with_error), sum3(with_acts)


def first_kernel(
    mine_hbm,
    cot_hbm,
    acts_hbm,
    error_hbm,
    gram_ref,
    with_error_ref,
    with_acts_ref,
    cot_ref,
    error_other_ref,
    acts_other_ref,
    mine_ref,
    error_ref,
    acts_ref,
    sems,
):
    core = my_core()
    copies = Copies(sems)
    mine_copy = copies.start(mine_hbm, mine_ref)
    now = fetch_half(copies, core, error_hbm, acts_hbm, error_ref, acts_ref)
    later = fetch_half(copies, 1 - core, error_hbm, acts_hbm, error_other_ref, acts_other_ref)
    cot_copy = copies.start(cot_hbm, cot_ref)
    mine_copy.wait()
    gram, with_error, with_acts = half_terms(half_of(mine_ref), error_ref, acts_ref, now)
    gram_ref[...] = gram
    with_error_ref[...] = with_error
    with_acts_ref[...] = with_acts
    for pair in later:
        for copy in pair:
            copy.wait()
    cot_copy.wait()


def first(mine, cot, acts, error, parts=1):
    tokens, d = acts.shape
    ff = cot.shape[1]
    halves = half_shapes(tokens, d, ff, parts)
    return call(
        first_kernel,
        (mine, cot, acts, error),
        [HBM] * 4,
        [shape((RANK, RANK)), shape((RANK, ff)), shape((RANK, tokens)), shape((tokens, ff), BF16)]
        + [shape(s, BF16) for s in halves],
        [VMEM] * 6,
        [(mine.shape, F32)] + [(s, BF16) for s in halves],
        2 + 4 * parts,
        limit=44 << 20,
    )


def second_kernel(
    other_ref, gram_ref, with_error_ref, with_acts_ref, cot_ref, error_ref, acts_ref, factor_ref, right_ref
):
    gram, with_error, with_acts = half_terms(half_of(other_ref), error_ref, acts_ref)
    factor = inverse_factor(gram + gram_ref[...])
    factor_ref[...] = factor
    with_acts = with_acts + with_acts_ref[...]
    merged_term = (with_error + with_error_ref[...]) + sum3(dot(split3(with_acts), cot_ref[...]))
    right = dot_highest(factor, merged_term)
    tiles = right.shape[1] // LANES
    for g in range(8):
        for j in range(tiles):
            v = g * tiles + j
            right_ref[v // 4, 8 * (v % 4) : 8 * (v % 4) + 8] = right[8 * g : 8 * g + 8, LANES * j : LANES * (j + 1)]
    for v in range(8 * tiles, 64):
        right_ref[v // 4, 8 * (v % 4) : 8 * (v % 4) + 8] = jnp.zeros((8, LANES), F32)


def second(other, terms):
    return pl.pallas_call(
        second_kernel,
        in_specs=[VMEM] * 7,
        out_specs=[VMEM, VMEM],
        out_shape=[shape((RANK, RANK)), shape((16, 32, LANES))],
        compiler_params=pltpu.CompilerParams(vmem_limit_bytes=12 << 20),
        cost_estimate=pl.CostEstimate(flops=10**6, bytes_accessed=10**5, transcendentals=0),
    )(other, *terms)


def merged_kernel(acts_hbm, cot_hbm, error_hbm, out_hbm, cot_ref, acts_ref, error_ref, out_ref, sems):
    parts, step = error_ref.shape[:2]
    copies = Copies(sems)
    cot_copy = copies.start(cot_hbm, cot_ref)
    waits = []
    for i in range(parts):
        at = slice(i * step, (i + 1) * step)
        waits.append((copies.start(acts_hbm.at[:, at], acts_ref.at[i]), copies.start(error_hbm.at[at, :], error_ref.at[i])))
    cot_copy.wait()
    stores = []
    for i in range(parts):
        waits[i][0].wait()
        waits[i][1].wait()
        out_ref[i] = dot(acts_ref[i], cot_ref[...], TN) + error_ref[i].astype(F32)
        stores.append(copies.start(out_ref.at[i], out_hbm.at[i * step : (i + 1) * step, :]))
    for store in stores:
        store.wait()


def merge(acts, cot, error, parts=4):
    tokens, d = acts.shape
    ff = cot.shape[1]
    step = d // parts
    return call(
        merged_kernel,
        (acts, cot, error),
        [HBM] * 3,
        shape((d, ff)),
        HBM,
        [((tokens, ff), BF16), ((parts, tokens, step), BF16), ((parts, step, ff), BF16), ((parts, step, ff), F32)],
        1 + 3 * parts,
    )


def prep_kernel(factor_ref, mine_ref, other_ref, basis_ref, out_ref):
    core = my_core()
    for ref, place in ((mine_ref, core), (other_ref, 1 - core)):
        width = ref.shape[0] // 4 * LANES
        at = pl.ds(pl.multiple_of(place * width, width), width)
        x = dot_highest(factor_ref[...], half_of(ref))
        basis_ref[:, at] = x
        high = x.astype(BF16)
        low = (x - high.astype(F32)).astype(BF16)
        both = jnp.concatenate([high, low], axis=0).T
        out_ref[at, : 2 * RANK] = both
        out_ref[at, 2 * RANK :] = both


def prep(factor, mine, other):
    d = 2 * (mine.shape[0] // 4 * LANES)
    return pl.pallas_call(
        prep_kernel,
        in_specs=[VMEM] * 3,
        out_specs=[VMEM, VMEM],
        out_shape=[shape((RANK, d)), shape((d, 4 * RANK), BF16)],
        compiler_params=pltpu.CompilerParams(vmem_limit_bytes=12 << 20),
        cost_estimate=pl.CostEstimate(flops=10**6, bytes_accessed=10**5, transcendentals=0),
    )(factor, mine, other)


def final_kernel(chunks_hbm, basis_hbm, merged_hbm, error_hbm, q_ref, chunks_ref, q4_ref, basis_ref, merged_ref, out_ref, sems):
    parts, step = merged_ref.shape[:2]
    copies = Copies(sems)
    chunks_copy = copies.start(chunks_hbm, chunks_ref)
    waits = []
    for i in range(parts):
        at = slice(i * step, (i + 1) * step)
        waits.append(
            (copies.start(basis_hbm.at[at, :], basis_ref.at[i]), copies.start(merged_hbm.at[at, :], merged_ref.at[i]))
        )
    chunks_copy.wait()
    tiles = q_ref.shape[1] // LANES
    for g in range(8):
        for j in range(tiles):
            v = g * tiles + j
            q_ref[8 * g : 8 * g + 8, LANES * j : LANES * (j + 1)] = chunks_ref[v // 4, 8 * (v % 4) : 8 * (v % 4) + 8]
    q = q_ref[...]
    high = q.astype(BF16)
    low = (q - high.astype(F32)).astype(BF16)
    q4_ref[...] = jnp.concatenate([high, high, low, low], axis=0)
    stores = []
    for i in range(parts):
        waits[i][0].wait()
        waits[i][1].wait()
        out_ref[i] = (merged_ref[i] - dot(basis_ref[i], q4_ref[...])).astype(BF16)
        stores.append(copies.start(out_ref.at[i], error_hbm.at[i * step : (i + 1) * step, :]))
    for store in stores:
        store.wait()


def final(chunks, basis4, merged, parts=4):
    d, ff = merged.shape
    step = d // parts
    return call(
        final_kernel,
        (chunks, basis4, merged),
        [HBM] * 3,
        [shape((d, ff), BF16), shape((RANK, ff))],
        [HBM, VMEM],
        [
            (chunks.shape, F32),
            ((4 * RANK, ff), BF16),
            ((parts, step, 4 * RANK), BF16),
            ((parts, step, ff), F32),
            ((parts, step, ff), BF16),
        ],
        1 + 3 * parts,
    )


def partial_kernel(
    cot_hbm,
    weight_hbm,
    far_send_hbm,
    near_send_hbm,
    far_keep_hbm,
    near_keep_hbm,
    cot_ref,
    weight_ref,
    out_ref,
    sems,
):
    parts, step = weight_ref.shape[:2]
    core = my_core()
    x = lax.div(lax.axis_index("tensor"), 2)
    n = cot_ref.shape[0] // 8
    copies = Copies(sems)
    waits = []
    for side, h in enumerate((1 - core, core)):
        for k, hop in enumerate((2, 1, 3, 0)):
            at = pl.multiple_of((lax.rem(x + hop, 4) * 2 + h) * n, n)
            to = (side * 4 + k) * n
            waits.append(copies.start(cot_hbm.at[pl.ds(at, n), :], cot_ref.at[to : to + n, :]))
    weight_copies = [
        copies.start(weight_hbm.at[i * step : (i + 1) * step, :], weight_ref.at[i]) for i in range(parts)
    ]
    for copy in waits:
        copy.wait()
    stores = []
    targets = ((far_send_hbm, 0, n), (near_send_hbm, n, 4 * n), (far_keep_hbm, 4 * n, 5 * n), (near_keep_hbm, 5 * n, 8 * n))
    for i in range(parts):
        weight_copies[i].wait()
        out_ref[i] = dot(cot_ref[...], weight_ref[i], NT)
        for hbm, lo, hi in targets:
            stores.append(copies.start(out_ref.at[i, lo:hi, :], hbm.at[:, i * step : (i + 1) * step]))
    for store in stores:
        store.wait()


def partials(cot, weight, parts=4):
    tokens, ff = cot.shape
    d = weight.shape[0]
    n = tokens // 8
    step = d // parts
    return call(
        partial_kernel,
        (cot, weight),
        [HBM, HBM],
        [shape((r, d)) for r in (n, 3 * n, n, 3 * n)],
        [HBM] * 4,
        [((tokens, ff), BF16), ((parts, step, ff), BF16), ((parts, tokens, step), F32)],
        8 + 5 * parts,
    )


def ring_kernel(takes, ins, outs, bufs, sems):
    copies = Copies(sems)
    loads = []
    slot = 0
    for take in takes:
        started = []
        for which, rows, cols in take:
            started.append(copies.start(ins[which].at[rows, cols], bufs.at[slot]))
            slot += 1
        loads.append(started)
    stores = []
    slot = 0
    for started, out in zip(loads, outs):
        for copy in started:
            copy.wait()
        total = bufs[slot]
        for k in range(1, len(started)):
            total = total + bufs[slot + k]
        bufs[slot] = total
        stores.append(copies.start(bufs.at[slot], out))
        slot += len(started)
    for store in stores:
        store.wait()


def ring_sums(ins, takes, n, w):
    slots = sum(len(take) for take in takes)
    count = len(ins)

    def kernel(*refs):
        ring_kernel(takes, refs[:count], refs[count : count + len(takes)], *refs[count + len(takes) :])

    return call(
        kernel,
        ins,
        [HBM] * count,
        [shape((n, w))] * len(takes),
        [HBM] * len(takes),
        [((slots, n, w), F32)],
        slots + len(takes),
    )


def close_kernel(keep_hbm, got_hbm, low_right, high_right, low_left, high_left, out_hbm, own_ref, in_ref, out_ref, sems):
    copies = Copies(sems)
    n, d = out_ref.shape
    w = d // 2
    own = slice(2 * n, 3 * n)
    loads = [copies.start(src.at[own, :], own_ref.at[i]) for i, src in enumerate((keep_hbm, got_hbm))]
    loads += [copies.start(src, in_ref.at[i]) for i, src in enumerate((low_right, low_left, high_right, high_left))]
    for copy in loads:
        copy.wait()
    for k, cols in enumerate((slice(0, w), slice(w, d))):
        own_sum = own_ref[0, :, cols] + own_ref[1, :, cols]
        out_ref[:, cols] = (own_sum + (in_ref[2 * k] + in_ref[2 * k + 1])).astype(BF16)
    copies.start(out_ref, out_hbm).wait()


def close(keep, got, low_right, high_right, low_left, high_left):
    n, w = low_right.shape
    return call(
        close_kernel,
        (keep, got, low_right, high_right, low_left, high_left),
        [HBM] * 6,
        shape((n, 2 * w), BF16),
        HBM,
        [((2, n, 2 * w), F32), ((4, n, w), F32), ((n, 2 * w), BF16)],
        7,
    )


def body(acts, up_cot, up_weight, error_buf, q_init):
    n_dp = lax.axis_size("dp")
    n_tensor = lax.axis_size("tensor")
    both = ("dp", "tensor")
    groups = [[2 * i + c for i in range(n_dp * n_tensor // 2)] for c in range(2)]
    pairs = [(i, i ^ 1) for i in range(n_tensor)]
    right_ring = [(i, (i + 2) % n_tensor) for i in range(n_tensor)]
    left_ring = [(i, (i - 2) % n_tensor) for i in range(n_tensor)]
    error = error_buf[0]

    send, *held = left_send(q_init, up_cot, acts, error)
    received = lax.ppermute(send, "tensor", pairs)
    total = left_keep(held, send.shape) + received
    chunks = lax.all_to_all(total, both, 0, 0, axis_index_groups=groups)

    up_weight, _ = lax.optimization_barrier((up_weight, total))
    far_send, near_send, far_keep, near_keep = partials(up_cot, up_weight)
    acts_late, _ = lax.optimization_barrier((acts, far_keep))
    merged = merge(acts_late, up_cot, error)
    chunks, merged, far_send, near_send = lax.optimization_barrier((chunks, merged, far_send, near_send))

    spread_left = spread(chunks, 1.0)
    mine = lax.all_to_all(spread_left, both, 0, 0, axis_index_groups=groups)
    far_send, near_send, _ = lax.optimization_barrier((far_send, near_send, spread_left))
    far_got = lax.ppermute(far_send, "tensor", pairs)
    near_got = lax.ppermute(near_send, "tensor", pairs)
    n, w = far_keep.shape[0], far_keep.shape[1] // 2
    low, high = slice(0, w), slice(w, 2 * w)
    plus, minus = slice(0, n), slice(n, 2 * n)
    far_low, far_high = ring_sums(
        (far_keep, far_got), (((0, plus, low), (1, plus, low)), ((0, plus, high), (1, plus, high))), n, w
    )
    low_relay = lax.ppermute(far_low, "tensor", right_ring)
    high_relay = lax.ppermute(far_high, "tensor", left_ring)
    plus_high, minus_low = ring_sums(
        (near_keep, near_got), (((0, plus, high), (1, plus, high)), ((0, minus, low), (1, minus, low))), n, w
    )
    high_right = lax.ppermute(plus_high, "tensor", right_ring)
    low_left = lax.ppermute(minus_low, "tensor", left_ring)
    mine, _, _ = lax.optimization_barrier((mine, far_low, plus_high))

    other = lax.ppermute(mine, "tensor", pairs)
    factor, right = second(other, first(mine, up_cot, acts, error))

    right_parts = lax.all_to_all(right, "dp", 0, 0)
    basis, basis4 = prep(factor, mine, other)
    near_keep, low_relay, high_relay, _ = lax.optimization_barrier((near_keep, low_relay, high_relay, factor))
    plus_low, minus_high = ring_sums(
        (near_keep, near_got, low_relay, high_relay),
        (
            ((0, plus, low), (1, plus, low), (2, plus, slice(0, w))),
            ((0, minus, high), (1, minus, high), (3, plus, slice(0, w))),
        ),
        n,
        w,
    )
    low_right = lax.ppermute(plus_low, "tensor", right_ring)
    high_left = lax.ppermute(minus_high, "tensor", left_ring)
    right_parts, basis4, _ = lax.optimization_barrier((right_parts, basis4, plus_low))

    spread_right = spread(right_parts, 1.0 / n_dp)
    q_chunks = lax.all_to_all(spread_right, "dp", 0, 0)
    near_keep, low_right, high_left, high_right, low_left, _ = lax.optimization_barrier(
        (near_keep, low_right, high_left, high_right, low_left, spread_right)
    )
    input_grad = close(near_keep, near_got, low_right, high_right, low_left, high_left)
    q_chunks, input_grad = lax.optimization_barrier((q_chunks, input_grad))
    new_error, q_factor = final(q_chunks, basis4, merged)
    return (input_grad, new_error[None], basis, q_factor)


def solution(mesh):
    return jax.shard_map(
        body,
        mesh=mesh,
        in_specs=(
            P("dp", None),
            P("dp", "tensor"),
            P(None, "tensor"),
            P("dp", None, "tensor"),
            P(None, "tensor"),
        ),
        out_specs=(P(("dp", "tensor"), None), P("dp", None, "tensor"), P(), P(None, "tensor")),
        check_vma=False,
    )
```

time: 330 us -> 125 us (0.38)
  waiting for transfers between devices: 223 us -> 19.5 us
  matrix products: 69 us -> 0 us
  Pallas kernels: 0 us -> 58.6 us
  starting transfers between devices: 0.6 us -> 36.9 us
  between operations: 15.6 us -> 1.07 us
  other arithmetic: 15.1 us -> 0.86 us
    psum x2 -> x0, waiting for transfers between devices: 223 us -> none  [the longest x1 149 us: body(): left = lax.psum(left_term, ('dp', 'tensor'))]
    dot_general x6 -> x0, matrix products: 66.7 us -> none  [the longest x1 15.8 us: body(): lax.dot_general(basis, q_factor, (((0,), (0,)), ((), ())), precision=high...]
    pallas_call x0 -> x14, Pallas kernels: none -> 58.6 us  [the longest x9 49.3 us: call(): pl.pallas_call(kernel, in_specs=specs, out_specs=out_specs, out_shape=out...]
    all_to_all x0 -> x4, starting transfers between devices: none -> 28.9 us  [the longest x1 11.7 us: body(): chunks = lax.all_to_all(total, both, 0, 0, axis_index_groups=groups)]
    all_to_all x0 -> x4, waiting for transfers between devices: none -> 16.4 us  [the longest x1 7.63 us: body(): mine = lax.all_to_all(spread_left, both, 0, 0, axis_index_groups=groups)]
    another operation x5 -> x0, other arithmetic: 12.1 us -> none  [the longest x3 6.52 us: body(): chol = jnp.linalg.cholesky(gram)]
    ppermute x0 -> x10, starting transfers between devices: none -> 7.96 us  [the longest x1 2.67 us: body(): low_left = lax.ppermute(minus_low, 'tensor', left_ring)]
    unnamed x10 -> x26, local copies, waits for them, and re-layouts: 6.35 us -> 7.87 us
  transfers between devices with their start and end apart: 3 -> 14, of which waited for: 2 -> 5; matrix products, arithmetic and copies ran while one was open for 8% -> 0% of each run, Pallas kernels for 0% -> 34%
where the time goes in v2:
time: 125 us
  Pallas kernels  58.6 us (47%)
  starting transfers between devices  36.9 us (30%)
  waiting for transfers between devices  19.5 us (16%)
  local copies, waits for them, and re-layouts  7.87 us (6%)
    pallas_call x9, Pallas kernels, call(): pl.pallas_call(kernel, in_specs=specs, out_specs=out_specs, out_shape=out...  49.3 us
    all_to_all x1, starting transfers between devices, body(): chunks = lax.all_to_all(total, both, 0, 0, axis_index_groups=groups)  11.7 us
    all_to_all x1, starting transfers between devices, body(): mine = lax.all_to_all(spread_left, both, 0, 0, axis_index_groups=groups)  10.2 us
    unnamed x26, local copies, waits for them, and re-layouts  7.87 us
    all_to_all x1, waiting for transfers between devices, body(): mine = lax.all_to_all(spread_left, both, 0, 0, axis_index_groups=groups)  7.63 us
    all_to_all x1, waiting for transfers between devices, body(): right_parts = lax.all_to_all(right, 'dp', 0, 0)  5.32 us
    pallas_call x1, Pallas kernels, second(): pl.pallas_call(second_kernel, in_specs=[VMEM] * 7, out_specs=[VMEM, VMEM]...  3.75 us
    all_to_all x1, starting transfers between devices, body(): right_parts = lax.all_to_all(right, 'dp', 0, 0)  3.53 us
  transfers between devices with their start and end apart: 14, of which 5 were waited for; matrix products, arithmetic and copies ran while one was open for 0% of the time, Pallas kernels for 34%

profile of v2, /device:TPU:0, one launch (start us, length us, event | category | flops | bytes accessed | tf_op | source)
XLA Modules:
  0.0 124.8 jit_solution(6660530936771972043)
XLA Ops:
  0.6 0.0 copy-start
  0.6 1.2 copy-done
  1.8 0.0 copy-start.3
  1.8 0.9 copy-done.3
  2.8 5.5 %shard_map.84 = (f32[64,16,128]{2,1,0:T(8,128)S(1)}, bf16[896,192]{1,0:T(8,128)(2,1)S(1)}, bf16[192,512]{1,0:T(8,128)(2,1)S(1)}, bf16[4,512,896]{2,1,0:T(8,128)(2,1)S(1)}, bf16[4,512,512]{2,1,0:T(8,128)(2,1)S(1)}) custom-call(f32[64,896]{1,0:T(8,128)S(1)} %copy-done.3, bf16[512,896]{1,0:T(8,128)(2,1)S(1)} %copy-done, bf16[512,4096]{1,0:T(8,128)(2,1)} %acts_hbm.4, ...), custom_call_target="tpu_custom_call" | custom-call | flops 1000000 | bytes 100000 | tf_op jit(solution)/shard_map/pallas_call | solution.py:25
  8.3 0.1 collective-permute-start
  8.3 1.9 %shard_map.85 = f32[64,16,128]{2,1,0:T(8,128)S(1)} custom-call(bf16[896,192]{1,0:T(8,128)(2,1)S(1)} %get-tuple-element.52.q3t_ref, bf16[192,512]{1,0:T(8,128)(2,1)S(1)} %get-tuple-element.53.p3_ref, bf16[4,512,896]{2,1,0:T(8,128)(2,1)S(1)} %get-tuple-element.54.error_ref, bf16[4,512,512]{2,1,0:T(8,128)(2,1)S(1)} %get-tuple-element.55.acts_ref), custom_call_target="tpu_custom_call" | custom-call | flops 1000000 | bytes 100000 | tf_op jit(solution)/shard_map/pallas_call | solution.py:171
  10.2 0.0 collective-permute-done
  10.3 0.9 add.3
  11.1 11.7 %all-to-all-start = ((f32[64,16,128]{2,1,0:T(8,128)}), f32[64,16,128]{2,1,0:T(8,128)S(1)}, u32[]{:S(2)}, u32[]{:S(2)}) async-start(f32[64,16,128]{2,1,0:T(8,128)} %add.3), calls=%async_computation | async-start | bytes 1048576 | tf_op jit(solution)/shard_map/all_to_all | solution.py:587
  22.8 8.6 %shard_map.86 = (f32[64,4096]{1,0:T(8,128)}, f32[192,4096]{1,0:T(8,128)}, f32[64,4096]{1,0:T(8,128)}, f32[192,4096]{1,0:T(8,128)}) custom-call(bf16[512,896]{1,0:T(8,128)(2,1)} %cot_hbm.7, bf16[4096,896]{1,0:T(8,128)(2,1)} %weight_hbm), custom_call_target="tpu_custom_call" | custom-call | flops 1000000 | bytes 100000 | tf_op jit(solution)/shard_map/pallas_call | solution.py:25
  31.4 0.0 copy-start.12
  31.4 9.3 %shard_map.87.merged_hbm = f32[4096,896]{1,0:T(8,128)} custom-call(bf16[512,4096]{1,0:T(8,128)(2,1)} %acts_hbm.4, bf16[512,896]{1,0:T(8,128)(2,1)} %cot_hbm.7, bf16[4096,896]{1,0:T(8,128)(2,1)} %bitcast.3), custom_call_target="tpu_custom_call" | custom-call | flops 1000000 | bytes 100000 | tf_op jit(solution)/shard_map/pallas_call | solution.py:25
  40.8 0.0 all-to-all-done.i
  40.8 0.9 shard_map.88
  41.7 0.2 collective-permute-start.2
  41.9 0.0 copy-done.12
  41.9 0.3 collective-permute-start.1
  42.2 10.2 %all-to-all-start.1 = ((f32[64,16,128]{2,1,0:T(8,128)}), f32[64,16,128]{2,1,0:T(8,128)S(1)}, u32[]{:S(2)}, u32[]{:S(2)}) async-start(f32[64,16,128]{2,1,0:T(8,128)} %shard_map.88), calls=%async_computation.1 | async-start | bytes 1048576 | tf_op jit(solution)/shard_map/all_to_all | solution.py:596
  52.4 0.0 collective-permute-done.1.refs_1_
  52.4 0.0 copy-start.5
  52.4 1.0 copy-done.5
  53.4 2.4 %shard_map.89 = (f32[64,2048]{1,0:T(8,128)}, f32[64,2048]{1,0:T(8,128)}) custom-call(f32[64,4096]{1,0:T(8,128)} %get-tuple-element.58.refs_0_, f32[64,4096]{1,0:T(8,128)} %copy-done.5), custom_call_target="tpu_custom_call" | custom-call | flops 1000000 | bytes 100000 | tf_op jit(solution)/shard_map/pallas_call | solution.py:25
  55.8 0.0 copy-start.1
  55.8 0.0 collective-permute-done.2.refs_1_.got_hbm
  55.8 2.5 %shard_map.90 = (f32[64,2048]{1,0:T(8,128)}, f32[64,2048]{1,0:T(8,128)}) custom-call(f32[192,4096]{1,0:T(8,128)} %get-tuple-element.88.refs_0_.keep_hbm, f32[192,4096]{1,0:T(8,128)} %collective-permute-done.2.refs_1_.got_hbm), custom_call_target="tpu_custom_call" | custom-call | flops 1000000 | bytes 100000 | tf_op jit(solution)/shard_map/pallas_call | solution.py:25
  58.3 7.6 %all-to-all-done.1.mine_hbm.mine_ref = f32[64,16,128]{2,1,0:T(8,128)S(1)} async-done(((f32[64,16,128]{2,1,0:T(8,128)}), f32[64,16,128]{2,1,0:T(8,128)S(1)}, u32[]{:S(2)}, u32[]{:S(2)}) %all-to-all-start.1) | async-done | bytes 524320 | tf_op jit(solution)/shard_map/all_to_all | solution.py:596
  65.9 0.0 collective-permute-start.3
  65.9 0.9 collective-permute-start.5
  66.8 1.1 collective-permute-start.4
  68.0 0.6 collective-permute-start.8
  68.5 2.7 %collective-permute-start.9 = (f32[64,2048]{1,0:T(8,128)}, f32[64,2048]{1,0:T(8,128)S(1)}, u32[]{:S(2)}, u32[]{:S(2)}) collective-permute-start(f32[64,2048]{1,0:T(8,128)} %get-tuple-element.87), channel_id=1, source_target_pairs={{0,6},{1,7},{2,0},{3,1},{4,2},{5,3},{6,4},{7,5},{8,14},{9,15},{10,... | collective-permute-start | bytes 1572872 | tf_op jit(solution)/shard_map/ppermute | solution.py:612
  71.2 0.0 copy-done.1
  71.2 5.0 %shard_map.91 = (f32[64,64]{1,0:T(8,128)S(1)}, f32[64,896]{1,0:T(8,128)S(1)}, f32[64,512]{1,0:T(8,128)S(1)}, bf16[512,896]{1,0:T(8,128)(2,1)S(1)}, bf16[1,2048,8...) custom-call(f32[64,16,128]{2,1,0:T(8,128)S(1)} %all-to-all-done.1.mine_hbm.mine_ref, ...), custom_call_target="tpu_custom_call" | custom-call | flops 1000000 | bytes 100000 | tf_op jit(solution)/shard_map/pallas_call | solution.py:25
  76.2 0.0 collective-permute-done.3.other_ref
  76.2 3.8 %shard_map.92 = (f32[64,64]{1,0:T(8,128)S(1)}, f32[16,32,128]{2,1,0:T(8,128)}) custom-call(f32[64,16,128]{2,1,0:T(8,128)S(1)} %collective-permute-done.3.other_ref, f32[64,64]{1,0:T(8,128)S(1)} %get-tuple-element.71.gram_ref, f32[64,896]{1,0:T(8,128)S(1)} %get-tuple-element.72.with_error_ref, f32[64,512]{1,0:T(8,128)S(1)} %get-tuple-element.73.with_acts_ref, ...), custom_call_target="tpu_custom_call" | custom-call | flops 1000000 | bytes 100000 | tf_op jit(solution)/shard_map/pallas_call | solution.py:328
  79.9 0.9 collective-permute-done.5.refs_3_
  80.9 2.1 %collective-permute-done.4.refs_2_ = f32[64,2048]{1,0:T(8,128)S(1)} collective-permute-done((f32[64,2048]{1,0:T(8,128)}, f32[64,2048]{1,0:T(8,128)S(1)}, u32[]{:S(2)}, u32[]{:S(2)}) %collective-permute-start.4) | collective-permute-done | bytes 524320 | tf_op jit(solution)/shard_map/ppermute | solution.py:606
  83.0 0.0 copy-done.6
  83.0 0.8 copy-done.7
  83.8 2.8 %shard_map.94 = (f32[64,2048]{1,0:T(8,128)}, f32[64,2048]{1,0:T(8,128)}) custom-call(f32[192,4096]{1,0:T(8,128)} %get-tuple-element.88.refs_0_.keep_hbm, f32[192,4096]{1,0:T(8,128)} %collective-permute-done.2.refs_1_.got_hbm, f32[64,2048]{1,0:T(8,128)} %copy-done.7, f32[64,2048]{1,0:T(8,128)} %copy-done.6), custom_call_target="tpu_custom_call" | custom-call | flops 1000000 | bytes 100000 | tf_op jit(solution)/shard_map/pallas_call | solution.py:25
  86.6 0.2 collective-permute-start.7
  86.8 1.9 %collective-permute-start.6 = (f32[64,2048]{1,0:T(8,128)}, f32[64,2048]{1,0:T(8,128)S(1)}, u32[]{:S(2)}, u32[]{:S(2)}) collective-permute-start(f32[64,2048]{1,0:T(8,128)} %get-tuple-element.84), channel_id=1, source_target_pairs={{0,2},{1,3},{2,4},{3,5},{4,6},{5,7},{6,0},{7,1},{8,10},{9,11},{10,... | collective-permute-start | bytes 1572872 | tf_op jit(solution)/shard_map/ppermute | solution.py:630
  88.7 3.5 %all-to-all-start.2 = ((f32[16,32,128]{2,1,0:T(8,128)}), f32[16,32,128]{2,1,0:T(8,128)S(1)}, u32[]{:S(2)}, u32[]{:S(2)}) async-start(f32[16,32,128]{2,1,0:T(8,128)} %get-tuple-element.77), calls=%async_computation.2 | async-start | bytes 524288 | tf_op jit(solution)/shard_map/all_to_all | solution.py:618
  92.2 1.9 %shard_map.93 = (f32[64,4096]{1,0:T(8,128)}, bf16[4096,256]{1,0:T(8,128)(2,1)S(1)}) custom-call(f32[64,64]{1,0:T(8,128)S(1)} %get-tuple-element.78.factor_ref, f32[64,16,128]{2,1,0:T(8,128)S(1)} %all-to-all-done.1.mine_hbm.mine_ref, f32[64,16,128]{2,1,0:T(8,128)S(1)} %collective-permute-done.3.other_ref), custom_call_target="tpu_custom_call" | custom-call | flops 1000000 | bytes 100000 | tf_op jit(solution)/shard_map/pallas_call | solution.py:388
  94.2 1.4 %copy-done.2 = bf16[4096,256]{1,0:T(8,128)(2,1)} copy-done((bf16[4096,256]{1,0:T(8,128)(2,1)}, bf16[4096,256]{1,0:T(8,128)(2,1)S(1)}, u32[]{:S(2)}) %copy-start.2) | copy-done | bytes 2097176
  95.6 5.3 %all-to-all-done.2.i = f32[16,32,128]{2,1,0:T(8,128)S(1)} async-done(((f32[16,32,128]{2,1,0:T(8,128)}), f32[16,32,128]{2,1,0:T(8,128)S(1)}, u32[]{:S(2)}, u32[]{:S(2)}) %all-to-all-start.2) | async-done | bytes 262176 | tf_op jit(solution)/shard_map/all_to_all | solution.py:618
  100.9 0.8 shard_map.95
  101.7 3.5 %all-to-all-start.3 = ((f32[16,32,128]{2,1,0:T(8,128)}), f32[16,32,128]{2,1,0:T(8,128)S(1)}, u32[]{:S(2)}, u32[]{:S(2)}) async-start(f32[16,32,128]{2,1,0:T(8,128)} %shard_map.95), calls=%async_computation.3 | async-start | bytes 524288 | tf_op jit(solution)/shard_map/all_to_all | solution.py:635
  105.2 0.0 collective-permute-done.9.low_left
  105.2 0.0 copy-start.9
  105.2 0.0 collective-permute-done.8.high_right
  105.2 0.0 copy-start.8
  105.3 0.0 collective-permute-done.7.high_left
  105.3 0.0 copy-start.10
  105.3 0.0 collective-permute-done.6.low_right
  105.3 0.7 copy-done.9
  106.0 0.2 copy-done.8
  106.2 0.2 copy-done.10
  106.4 0.8 copy-done.11
  107.2 3.2 %shard_map.96 = bf16[64,4096]{1,0:T(8,128)(2,1)} custom-call(f32[192,4096]{1,0:T(8,128)} %get-tuple-element.88.refs_0_.keep_hbm, f32[192,4096]{1,0:T(8,128)} %collective-permute-done.2.refs_1_.got_hbm, f32[64,2048]{1,0:T(8,128)} %copy-done.11, f32[64,2048]{1,0:T(8,128)} %copy-done.8, f32[64,2048]{1,0:T(8,128)} %copy-done.9, f32[64,2048]{1,0:T(8,128)} %copy-done.10), custom_call_target="tpu_custom_call" | custom-call | flops 1000000 | bytes 100000 | tf_op jit(solution)/shard_map/pallas_call | solution.py:25
  110.4 3.5 %all-to-all-done.3.chunks_hbm = f32[16,32,128]{2,1,0:T(8,128)S(1)} async-done(((f32[16,32,128]{2,1,0:T(8,128)}), f32[16,32,128]{2,1,0:T(8,128)S(1)}, u32[]{:S(2)}, u32[]{:S(2)}) %all-to-all-start.3) | async-done | bytes 262176 | tf_op jit(solution)/shard_map/all_to_all | solution.py:635
  113.9 0.7 copy-done.4
  114.6 10.0 %shard_map.97 = (bf16[4096,896]{1,0:T(8,128)(2,1)}, f32[64,896]{1,0:T(8,128)}) custom-call(f32[16,32,128]{2,1,0:T(8,128)} %copy-done.4, bf16[4096,256]{1,0:T(8,128)(2,1)} %copy-done.2, f32[4096,896]{1,0:T(8,128)} %shard_map.87.merged_hbm), custom_call_target="tpu_custom_call" | custom-call | flops 1000000 | bytes 100000 | tf_op jit(solution)/shard_map/pallas_call | solution.py:25
  (5 shorter events, 0.0 us)
Async XLA Ops:
  0.6 1.2 copy-start
  1.8 0.9 copy-start.3
  8.3 2.0 %collective-permute-start = (f32[64,16,128]{2,1,0:T(8,128)S(1)}, f32[64,16,128]{2,1,0:T(8,128)S(1)}, u32[]{:S(2)}, u32[]{:S(2)}) collective-permute-start(f32[64,16,128]{2,1,0:T(8,128)S(1)} %get-tuple-element.56), channel_id=1, source_target_pairs={{0,1},{1,0},{2,3},{3,2},{4,5},{5,4},{6,7},{7,6},{8,9},{9,8},{10,11... | collective-permute-start | bytes 1572872 | tf_op jit(solution)/shard_map/ppermute | solution.py:585
  11.1 29.7 %all-to-all-start = ((f32[64,16,128]{2,1,0:T(8,128)}), f32[64,16,128]{2,1,0:T(8,128)S(1)}, u32[]{:S(2)}, u32[]{:S(2)}) async-start(f32[64,16,128]{2,1,0:T(8,128)} %add.3), calls=%async_computation | async-start | bytes 1048576 | tf_op jit(solution)/shard_map/all_to_all | solution.py:587
  31.4 10.5 %copy-start.12 = (f32[64,4096]{1,0:T(8,128)S(1)}, f32[64,4096]{1,0:T(8,128)}, u32[]{:S(2)}) copy-start(f32[64,4096]{1,0:T(8,128)} %get-tuple-element.65) | copy-start | bytes 3145732
  41.7 14.1 %collective-permute-start.2 = (f32[192,4096]{1,0:T(8,128)}, f32[192,4096]{1,0:T(8,128)}, u32[]{:S(2)}, u32[]{:S(2)}) collective-permute-start(f32[192,4096]{1,0:T(8,128)} %get-tuple-element.68), channel_id=1, source_target_pairs={{0,1},{1,0},{2,3},{3,2},{4,5},{5,4},{6,7},{7,6},{8,9},{9,8},{10,11... | collective-permute-start | bytes 9437192 | tf_op jit(solution)/shard_map/ppermute | solution.py:599
  41.9 10.5 %collective-permute-start.1 = (f32[64,4096]{1,0:T(8,128)S(1)}, f32[64,4096]{1,0:T(8,128)S(1)}, u32[]{:S(2)}, u32[]{:S(2)}) collective-permute-start(f32[64,4096]{1,0:T(8,128)S(1)} %copy-done.12), channel_id=1, source_target_pairs={{0,1},{1,0},{2,3},{3,2},{4,5},{5,4},{6,7},{7,6},{8,9},{9,8},{10,11... | collective-permute-start | bytes 3145736 | tf_op jit(solution)/shard_map/ppermute | solution.py:598
  42.2 23.7 %all-to-all-start.1 = ((f32[64,16,128]{2,1,0:T(8,128)}), f32[64,16,128]{2,1,0:T(8,128)S(1)}, u32[]{:S(2)}, u32[]{:S(2)}) async-start(f32[64,16,128]{2,1,0:T(8,128)} %shard_map.88), calls=%async_computation.1 | async-start | bytes 1048576 | tf_op jit(solution)/shard_map/all_to_all | solution.py:596
  52.4 1.0 copy-start.5
  55.8 15.4 %copy-start.1 = (bf16[512,896]{1,0:T(8,128)(2,1)S(1)}, bf16[512,896]{1,0:T(8,128)(2,1)}, u32[]{:S(2)}) copy-start(bf16[512,896]{1,0:T(8,128)(2,1)} %cot_hbm.7) | copy-start | bytes 2752516
  65.9 10.2 %collective-permute-start.3 = (f32[64,16,128]{2,1,0:T(8,128)S(1)}, f32[64,16,128]{2,1,0:T(8,128)S(1)}, u32[]{:S(2)}, u32[]{:S(2)}) collective-permute-start(f32[64,16,128]{2,1,0:T(8,128)S(1)} %all-to-all-done.1.mine_hbm.mine_ref), channel_id=1, source_target_pairs={{0,1},{1,0},{2,3},{3,2},{4,5},{5,4},{6,7},{7,6},{8,9},{9,8},{10,11... | collective-permute-start | bytes 1572872 | tf_op jit(solution)/shard_map/ppermute | solution.py:615
  65.9 14.9 %collective-permute-start.5 = (f32[64,2048]{1,0:T(8,128)}, f32[64,2048]{1,0:T(8,128)S(1)}, u32[]{:S(2)}, u32[]{:S(2)}) collective-permute-start(f32[64,2048]{1,0:T(8,128)} %get-tuple-element.80), channel_id=1, source_target_pairs={{0,6},{1,7},{2,0},{3,1},{4,2},{5,3},{6,4},{7,5},{8,14},{9,15},{10,... | collective-permute-start | bytes 1572872 | tf_op jit(solution)/shard_map/ppermute | solution.py:607
  66.8 16.2 %collective-permute-start.4 = (f32[64,2048]{1,0:T(8,128)}, f32[64,2048]{1,0:T(8,128)S(1)}, u32[]{:S(2)}, u32[]{:S(2)}) collective-permute-start(f32[64,2048]{1,0:T(8,128)} %get-tuple-element.66), channel_id=1, source_target_pairs={{0,2},{1,3},{2,4},{3,5},{4,6},{5,7},{6,0},{7,1},{8,10},{9,11},{10,... | collective-permute-start | bytes 1572872 | tf_op jit(solution)/shard_map/ppermute | solution.py:606
  68.0 37.3 %collective-permute-start.8 = (f32[64,2048]{1,0:T(8,128)}, f32[64,2048]{1,0:T(8,128)S(1)}, u32[]{:S(2)}, u32[]{:S(2)}) collective-permute-start(f32[64,2048]{1,0:T(8,128)} %get-tuple-element.69), channel_id=1, source_target_pairs={{0,2},{1,3},{2,4},{3,5},{4,6},{5,7},{6,0},{7,1},{8,10},{9,11},{10,... | collective-permute-start | bytes 1572872 | tf_op jit(solution)/shard_map/ppermute | solution.py:611
  68.5 36.7 %collective-permute-start.9 = (f32[64,2048]{1,0:T(8,128)}, f32[64,2048]{1,0:T(8,128)S(1)}, u32[]{:S(2)}, u32[]{:S(2)}) collective-permute-start(f32[64,2048]{1,0:T(8,128)} %get-tuple-element.87), channel_id=1, source_target_pairs={{0,6},{1,7},{2,0},{3,1},{4,2},{5,3},{6,4},{7,5},{8,14},{9,15},{10,... | collective-permute-start | bytes 1572872 | tf_op jit(solution)/shard_map/ppermute | solution.py:612
  80.9 2.1 %copy-start.6 = (f32[64,2048]{1,0:T(8,128)}, f32[64,2048]{1,0:T(8,128)S(1)}, u32[]{:S(2)}) copy-start(f32[64,2048]{1,0:T(8,128)S(1)} %collective-permute-done.5.refs_3_) | copy-start | bytes 1572868
  83.0 0.8 copy-start.7
  86.6 18.6 %collective-permute-start.7 = (f32[64,2048]{1,0:T(8,128)}, f32[64,2048]{1,0:T(8,128)S(1)}, u32[]{:S(2)}, u32[]{:S(2)}) collective-permute-start(f32[64,2048]{1,0:T(8,128)} %get-tuple-element.86), channel_id=1, source_target_pairs={{0,6},{1,7},{2,0},{3,1},{4,2},{5,3},{6,4},{7,5},{8,14},{9,15},{10,... | collective-permute-start | bytes 1572872 | tf_op jit(solution)/shard_map/ppermute | solution.py:631
  86.8 18.5 %collective-permute-start.6 = (f32[64,2048]{1,0:T(8,128)}, f32[64,2048]{1,0:T(8,128)S(1)}, u32[]{:S(2)}, u32[]{:S(2)}) collective-permute-start(f32[64,2048]{1,0:T(8,128)} %get-tuple-element.84), channel_id=1, source_target_pairs={{0,2},{1,3},{2,4},{3,5},{4,6},{5,7},{6,0},{7,1},{8,10},{9,11},{10,... | collective-permute-start | bytes 1572872 | tf_op jit(solution)/shard_map/ppermute | solution.py:630
  88.7 12.2 %all-to-all-start.2 = ((f32[16,32,128]{2,1,0:T(8,128)}), f32[16,32,128]{2,1,0:T(8,128)S(1)}, u32[]{:S(2)}, u32[]{:S(2)}) async-start(f32[16,32,128]{2,1,0:T(8,128)} %get-tuple-element.77), calls=%async_computation.2 | async-start | bytes 524288 | tf_op jit(solution)/shard_map/all_to_all | solution.py:618
  94.2 1.4 %copy-start.2 = (bf16[4096,256]{1,0:T(8,128)(2,1)}, bf16[4096,256]{1,0:T(8,128)(2,1)S(1)}, u32[]{:S(2)}) copy-start(bf16[4096,256]{1,0:T(8,128)(2,1)S(1)} %get-tuple-element.95.basis_hbm) | copy-start | bytes 6291460
  101.7 12.2 %all-to-all-start.3 = ((f32[16,32,128]{2,1,0:T(8,128)}), f32[16,32,128]{2,1,0:T(8,128)S(1)}, u32[]{:S(2)}, u32[]{:S(2)}) async-start(f32[16,32,128]{2,1,0:T(8,128)} %shard_map.95), calls=%async_computation.3 | async-start | bytes 524288 | tf_op jit(solution)/shard_map/all_to_all | solution.py:635
  105.2 0.8 copy-start.9
  105.2 0.9 copy-start.8
  105.3 1.1 copy-start.10
  106.4 0.8 copy-start.11
  113.9 0.7 copy-start.4

commit v3 on v2

--- a/solution.py
+++ b/solution.py
@@ -335,40 +335,6 @@
     )(other, *terms)
 
 
-def merged_kernel(acts_hbm, cot_hbm, error_hbm, out_hbm, cot_ref, acts_ref, error_ref, out_ref, sems):
-    parts, step = error_ref.shape[:2]
-    copies = Copies(sems)
-    cot_copy = copies.start(cot_hbm, cot_ref)
-    waits = []
-    for i in range(parts):
-        at = slice(i * step, (i + 1) * step)
-        waits.append((copies.start(acts_hbm.at[:, at], acts_ref.at[i]), copies.start(error_hbm.at[at, :], error_ref.at[i])))
-    cot_copy.wait()
-    stores = []
-    for i in range(parts):
-        waits[i][0].wait()
-        waits[i][1].wait()
-        out_ref[i] = dot(acts_ref[i], cot_ref[...], TN) + error_ref[i].astype(F32)
-        stores.append(copies.start(out_ref.at[i], out_hbm.at[i * step : (i + 1) * step, :]))
-    for store in stores:
-        store.wait()
-
-
-def merge(acts, cot, error, parts=4):
-    tokens, d = acts.shape
-    ff = cot.shape[1]
-    step = d // parts
-    return call(
-        merged_kernel,
-        (acts, cot, error),
-        [HBM] * 3,
-        shape((d, ff)),
-        HBM,
-        [((tokens, ff), BF16), ((parts, tokens, step), BF16), ((parts, step, ff), BF16), ((parts, step, ff), F32)],
-        1 + 3 * parts,
-    )
-
-
 def prep_kernel(factor_ref, mine_ref, other_ref, basis_ref, out_ref):
     core = my_core()
     for ref, place in ((mine_ref, core), (other_ref, 1 - core)):
@@ -395,15 +361,36 @@
     )(factor, mine, other)
 
 
-def final_kernel(chunks_hbm, basis_hbm, merged_hbm, error_hbm, q_ref, chunks_ref, q4_ref, basis_ref, merged_ref, out_ref, sems):
-    parts, step = merged_ref.shape[:2]
+def final_kernel(
+    chunks_hbm,
+    basis_hbm,
+    cot_hbm,
+    acts_hbm,
+    error_hbm,
+    out_hbm,
+    q_ref,
+    chunks_ref,
+    q4_ref,
+    basis_ref,
+    cot_ref,
+    acts_ref,
+    error_ref,
+    out_ref,
+    sems,
+):
+    parts, step = error_ref.shape[:2]
     copies = Copies(sems)
     chunks_copy = copies.start(chunks_hbm, chunks_ref)
+    cot_copy = copies.start(cot_hbm, cot_ref)
     waits = []
     for i in range(parts):
         at = slice(i * step, (i + 1) * step)
         waits.append(
-            (copies.start(basis_hbm.at[at, :], basis_ref.at[i]), copies.start(merged_hbm.at[at, :], merged_ref.at[i]))
+            (
+                copies.start(acts_hbm.at[:, at], acts_ref.at[i]),
+                copies.start(basis_hbm.at[at, :], basis_ref.at[i]),
+                copies.start(error_hbm.at[at, :], error_ref.at[i]),
+            )
         )
     chunks_copy.wait()
     tiles = q_ref.shape[1] // LANES
@@ -411,37 +398,42 @@
         for j in range(tiles):
             v = g * tiles + j
             q_ref[8 * g : 8 * g + 8, LANES * j : LANES * (j + 1)] = chunks_ref[v // 4, 8 * (v % 4) : 8 * (v % 4) + 8]
-    q = q_ref[...]
+    q = -q_ref[...]
     high = q.astype(BF16)
     low = (q - high.astype(F32)).astype(BF16)
     q4_ref[...] = jnp.concatenate([high, high, low, low], axis=0)
+    cot_copy.wait()
     stores = []
     for i in range(parts):
-        waits[i][0].wait()
-        waits[i][1].wait()
-        out_ref[i] = (merged_ref[i] - dot(basis_ref[i], q4_ref[...])).astype(BF16)
-        stores.append(copies.start(out_ref.at[i], error_hbm.at[i * step : (i + 1) * step, :]))
+        for copy in waits[i]:
+            copy.wait()
+        merged = dot(acts_ref[i], cot_ref[...], TN) + error_ref[i].astype(F32)
+        out_ref[i] = (merged + dot(basis_ref[i], q4_ref[...])).astype(BF16)
+        stores.append(copies.start(out_ref.at[i], out_hbm.at[i * step : (i + 1) * step, :]))
     for store in stores:
         store.wait()
 
 
-def final(chunks, basis4, merged, parts=4):
-    d, ff = merged.shape
+def final(chunks, basis4, cot, acts, error, parts=8):
+    tokens, d = acts.shape
+    ff = cot.shape[1]
     step = d // parts
     return call(
         final_kernel,
-        (chunks, basis4, merged),
-        [HBM] * 3,
+        (chunks, basis4, cot, acts, error),
+        [HBM] * 5,
         [shape((d, ff), BF16), shape((RANK, ff))],
         [HBM, VMEM],
         [
             (chunks.shape, F32),
             ((4 * RANK, ff), BF16),
             ((parts, step, 4 * RANK), BF16),
-            ((parts, step, ff), F32),
+            ((tokens, ff), BF16),
+            ((parts, tokens, step), BF16),
+            ((parts, step, ff), BF16),
             ((parts, step, ff), BF16),
         ],
-        1 + 3 * parts,
+        2 + 4 * parts,
     )
 
 
@@ -543,31 +535,61 @@
     )
 
 
-def close_kernel(keep_hbm, got_hbm, low_right, high_right, low_left, high_left, out_hbm, own_ref, in_ref, out_ref, sems):
+def near_kernel(keep_hbm, got_hbm, low_hbm, high_hbm, plus_hbm, minus_hbm, keep_ref, got_ref, relay_ref, sems):
     copies = Copies(sems)
-    n, d = out_ref.shape
+    n, d = plus_hbm.shape
     w = d // 2
-    own = slice(2 * n, 3 * n)
-    loads = [copies.start(src.at[own, :], own_ref.at[i]) for i, src in enumerate((keep_hbm, got_hbm))]
-    loads += [copies.start(src, in_ref.at[i]) for i, src in enumerate((low_right, low_left, high_right, high_left))]
+    loads = [copies.start(low_hbm, relay_ref.at[0]), copies.start(high_hbm, relay_ref.at[1])]
+    loads += [copies.start(src.at[: 2 * n, :], dst) for src, dst in ((keep_hbm, keep_ref), (got_hbm, got_ref))]
     for copy in loads:
         copy.wait()
-    for k, cols in enumerate((slice(0, w), slice(w, d))):
-        own_sum = own_ref[0, :, cols] + own_ref[1, :, cols]
-        out_ref[:, cols] = (own_sum + (in_ref[2 * k] + in_ref[2 * k + 1])).astype(BF16)
+    keep_ref[:n, w:] += got_ref[:n, w:]
+    keep_ref[:n, :w] = (keep_ref[:n, :w] + got_ref[:n, :w]) + relay_ref[0]
+    plus = copies.start(keep_ref.at[:n, :], plus_hbm)
+    keep_ref[n:, :w] += got_ref[n:, :w]
+    keep_ref[n:, w:] = (keep_ref[n:, w:] + got_ref[n:, w:]) + relay_ref[1]
+    minus = copies.start(keep_ref.at[n:, :], minus_hbm)
+    plus.wait()
+    minus.wait()
+
+
+def near_sums(keep, got, low, high):
+    n, d = low.shape[0], keep.shape[1]
+    return call(
+        near_kernel,
+        (keep, got, low, high),
+        [HBM] * 4,
+        [shape((n, d))] * 2,
+        [HBM] * 2,
+        [((2 * n, d), F32), ((2 * n, d), F32), ((2, n, d // 2), F32)],
+        6,
+    )
+
+
+def close_kernel(keep_hbm, got_hbm, right_hbm, left_hbm, out_hbm, in_ref, out_ref, sems):
+    copies = Copies(sems)
+    n = out_ref.shape[0]
+    own = slice(2 * n, 3 * n)
+    loads = [
+        copies.start(src, in_ref.at[i])
+        for i, src in enumerate((keep_hbm.at[own, :], got_hbm.at[own, :], right_hbm, left_hbm))
+    ]
+    for copy in loads:
+        copy.wait()
+    out_ref[...] = ((in_ref[0] + in_ref[1]) + (in_ref[2] + in_ref[3])).astype(BF16)
     copies.start(out_ref, out_hbm).wait()
 
 
-def close(keep, got, low_right, high_right, low_left, high_left):
-    n, w = low_right.shape
+def close(keep, got, right, left):
+    n, d = right.shape
     return call(
         close_kernel,
-        (keep, got, low_right, high_right, low_left, high_left),
-        [HBM] * 6,
-        shape((n, 2 * w), BF16),
+        (keep, got, right, left),
+        [HBM] * 4,
+        shape((n, d), BF16),
         HBM,
-        [((2, n, 2 * w), F32), ((4, n, w), F32), ((n, 2 * w), BF16)],
-        7,
+        [((4, n, d), F32), ((n, d), BF16)],
+        5,
     )
 
 
@@ -588,9 +610,7 @@
 
     up_weight, _ = lax.optimization_barrier((up_weight, total))
     far_send, near_send, far_keep, near_keep = partials(up_cot, up_weight)
-    acts_late, _ = lax.optimization_barrier((acts, far_keep))
-    merged = merge(acts_late, up_cot, error)
-    chunks, merged, far_send, near_send = lax.optimization_barrier((chunks, merged, far_send, near_send))
+    chunks, far_send, near_send = lax.optimization_barrier((chunks, far_send, near_send))
 
     spread_left = spread(chunks, 1.0)
     mine = lax.all_to_all(spread_left, both, 0, 0, axis_index_groups=groups)
@@ -599,46 +619,32 @@
     near_got = lax.ppermute(near_send, "tensor", pairs)
     n, w = far_keep.shape[0], far_keep.shape[1] // 2
     low, high = slice(0, w), slice(w, 2 * w)
-    plus, minus = slice(0, n), slice(n, 2 * n)
     far_low, far_high = ring_sums(
-        (far_keep, far_got), (((0, plus, low), (1, plus, low)), ((0, plus, high), (1, plus, high))), n, w
+        (far_keep, far_got), (((0, slice(0, n), low), (1, slice(0, n), low)), ((0, slice(0, n), high), (1, slice(0, n), high))), n, w
     )
     low_relay = lax.ppermute(far_low, "tensor", right_ring)
     high_relay = lax.ppermute(far_high, "tensor", left_ring)
-    plus_high, minus_low = ring_sums(
-        (near_keep, near_got), (((0, plus, high), (1, plus, high)), ((0, minus, low), (1, minus, low))), n, w
-    )
-    high_right = lax.ppermute(plus_high, "tensor", right_ring)
-    low_left = lax.ppermute(minus_low, "tensor", left_ring)
-    mine, _, _ = lax.optimization_barrier((mine, far_low, plus_high))
+    mine, _ = lax.optimization_barrier((mine, far_low))
 
     other = lax.ppermute(mine, "tensor", pairs)
-    factor, right = second(other, first(mine, up_cot, acts, error))
-
+    terms = first(mine, up_cot, acts, error)
+    gram, low_relay, high_relay = lax.optimization_barrier((terms[0], low_relay, high_relay))
+    factor, right = second(other, [gram, *terms[1:]])
+
+    near_keep, _ = lax.optimization_barrier((near_keep, factor))
+    plus, minus = near_sums(near_keep, near_got, low_relay, high_relay)
+    from_left = lax.ppermute(plus, "tensor", right_ring)
+    from_right = lax.ppermute(minus, "tensor", left_ring)
     right_parts = lax.all_to_all(right, "dp", 0, 0)
     basis, basis4 = prep(factor, mine, other)
-    near_keep, low_relay, high_relay, _ = lax.optimization_barrier((near_keep, low_relay, high_relay, factor))
-    plus_low, minus_high = ring_sums(
-        (near_keep, near_got, low_relay, high_relay),
-        (
-            ((0, plus, low), (1, plus, low), (2, plus, slice(0, w))),
-            ((0, minus, high), (1, minus, high), (3, plus, slice(0, w))),
-        ),
-        n,
-        w,
-    )
-    low_right = lax.ppermute(plus_low, "tensor", right_ring)
-    high_left = lax.ppermute(minus_high, "tensor", left_ring)
-    right_parts, basis4, _ = lax.optimization_barrier((right_parts, basis4, plus_low))
+    right_parts, basis4, _ = lax.optimization_barrier((right_parts, basis4, plus))
 
     spread_right = spread(right_parts, 1.0 / n_dp)
     q_chunks = lax.all_to_all(spread_right, "dp", 0, 0)
-    near_keep, low_right, high_left, high_right, low_left, _ = lax.optimization_barrier(
-        (near_keep, low_right, high_left, high_right, low_left, spread_right)
-    )
-    input_grad = close(near_keep, near_got, low_right, high_right, low_left, high_left)
+    near_keep, from_left, from_right, _ = lax.optimization_barrier((near_keep, from_left, from_right, spread_right))
+    input_grad = close(near_keep, near_got, from_left, from_right)
     q_chunks, input_grad = lax.optimization_barrier((q_chunks, input_grad))
-    new_error, q_factor = final(q_chunks, basis4, merged)
+    new_error, q_factor = final(q_chunks, basis4, up_cot, acts, error)
     return (input_grad, new_error[None], basis, q_factor)
 
 

time: 125 us -> 115 us (0.920)
  Pallas kernels: 58.6 us -> 49.8 us
  waiting for transfers between devices: 19.5 us -> 26.7 us
  starting transfers between devices: 36.9 us -> 31.4 us
  local copies, waits for them, and re-layouts: 7.87 us -> 5.18 us
    pallas_call x9 -> x7, Pallas kernels: 49.3 us -> 40.6 us  [call(): pl.pallas_call(kernel, in_specs=specs, out_specs=out_specs, out_shape=out...]
    all_to_all x1, waiting for transfers between devices: 0.01 us -> 5.38 us  [body(): chunks = lax.all_to_all(total, both, 0, 0, axis_index_groups=groups)]
    all_to_all x1, starting transfers between devices: 10.2 us -> 4.96 us  [body(): mine = lax.all_to_all(spread_left, both, 0, 0, axis_index_groups=groups)]
    ppermute x4 -> x2, waiting for transfers between devices: 0.01 us -> 4.57 us  [the longest x1 2.49 us: body(): from_right = lax.ppermute(minus, 'tensor', left_ring)]
    ppermute x4 -> x2, starting transfers between devices: 5.33 us -> 2.09 us  [the longest x1 1.73 us: body(): from_left = lax.ppermute(plus, 'tensor', right_ring)]
    all_to_all x1, starting transfers between devices: 3.53 us -> 6.38 us  [body(): right_parts = lax.all_to_all(right, 'dp', 0, 0)]
    all_to_all x1, waiting for transfers between devices: 3.5 us -> 0.66 us  [body(): q_chunks = lax.all_to_all(spread_right, 'dp', 0, 0)]
    unnamed x26 -> x18, local copies, waits for them, and re-layouts: 7.87 us -> 5.18 us
  transfers between devices with their start and end apart: 14 -> 12, of which waited for: 5 -> 9; matrix products, arithmetic and copies ran while one was open for 0% -> 0% of each run, Pallas kernels for 34% -> 24%
where the time goes in v3:
time: 115 us
  Pallas kernels  49.8 us (43%)
  starting transfers between devices  31.4 us (27%)
  waiting for transfers between devices  26.7 us (23%)
  local copies, waits for them, and re-layouts  5.18 us (5%)
    pallas_call x7, Pallas kernels, call(): pl.pallas_call(kernel, in_specs=specs, out_specs=out_specs, out_shape=out...  40.6 us
    all_to_all x1, starting transfers between devices, body(): chunks = lax.all_to_all(total, both, 0, 0, axis_index_groups=groups)  11.5 us
    all_to_all x1, waiting for transfers between devices, body(): mine = lax.all_to_all(spread_left, both, 0, 0, axis_index_groups=groups)  6.56 us
    all_to_all x1, starting transfers between devices, body(): right_parts = lax.all_to_all(right, 'dp', 0, 0)  6.38 us
    all_to_all x1, waiting for transfers between devices, body(): chunks = lax.all_to_all(total, both, 0, 0, axis_index_groups=groups)  5.38 us
    all_to_all x1, waiting for transfers between devices, body(): right_parts = lax.all_to_all(right, 'dp', 0, 0)  5.36 us
    unnamed x18, local copies, waits for them, and re-layouts  5.18 us
    all_to_all x1, starting transfers between devices, body(): mine = lax.all_to_all(spread_left, both, 0, 0, axis_index_groups=groups)  4.96 us
  transfers between devices with their start and end apart: 12, of which 9 were waited for; matrix products, arithmetic and copies ran while one was open for 0% of the time, Pallas kernels for 24%

profile of v3, /device:TPU:0, one launch (start us, length us, event | category | flops | bytes accessed | tf_op | source)
XLA Modules:
  0.0 114.9 jit_solution(5498861563090944786)
XLA Ops:
  0.6 0.0 copy-start
  0.6 1.2 %copy-done = bf16[512,896]{1,0:T(8,128)(2,1)S(1)} copy-done((bf16[512,896]{1,0:T(8,128)(2,1)S(1)}, bf16[512,896]{1,0:T(8,128)(2,1)}, u32[]{:S(2)}) %copy-start) | copy-done | bytes 917528
  1.8 0.0 copy-start.3
  1.8 0.9 copy-done.3
  2.8 5.5 %shard_map.84 = (f32[64,16,128]{2,1,0:T(8,128)S(1)}, bf16[896,192]{1,0:T(8,128)(2,1)S(1)}, bf16[192,512]{1,0:T(8,128)(2,1)S(1)}, bf16[4,512,896]{2,1,0:T(8,128)(2,1)S(1)}, bf16[4,512,512]{2,1,0:T(8,128)(2,1)S(1)}) custom-call(f32[64,896]{1,0:T(8,128)S(1)} %copy-done.3, bf16[512,896]{1,0:T(8,128)(2,1)S(1)} %copy-done, bf16[512,4096]{1,0:T(8,128)(2,1)} %acts_hbm.5, ...), custom_call_target="tpu_custom_call" | custom-call | flops 1000000 | bytes 100000 | tf_op jit(solution)/shard_map/pallas_call | solution.py:25
  8.3 0.1 collective-permute-start
  8.3 1.9 %shard_map.85 = f32[64,16,128]{2,1,0:T(8,128)S(1)} custom-call(bf16[896,192]{1,0:T(8,128)(2,1)S(1)} %get-tuple-element.47.q3t_ref, bf16[192,512]{1,0:T(8,128)(2,1)S(1)} %get-tuple-element.48.p3_ref, bf16[4,512,896]{2,1,0:T(8,128)(2,1)S(1)} %get-tuple-element.49.error_ref, bf16[4,512,512]{2,1,0:T(8,128)(2,1)S(1)} %get-tuple-element.50.acts_ref), custom_call_target="tpu_custom_call" | custom-call | flops 1000000 | bytes 100000 | tf_op jit(solution)/shard_map/pallas_call | solution.py:171
  10.2 0.0 collective-permute-done
  10.3 0.9 add.3
  11.1 11.5 %all-to-all-start = ((f32[64,16,128]{2,1,0:T(8,128)}), f32[64,16,128]{2,1,0:T(8,128)S(1)}, u32[]{:S(2)}, u32[]{:S(2)}) async-start(f32[64,16,128]{2,1,0:T(8,128)} %add.3), calls=%async_computation | async-start | bytes 1048576 | tf_op jit(solution)/shard_map/all_to_all | solution.py:609
  22.6 8.6 %shard_map.86 = (f32[64,4096]{1,0:T(8,128)}, f32[192,4096]{1,0:T(8,128)}, f32[64,4096]{1,0:T(8,128)}, f32[192,4096]{1,0:T(8,128)}) custom-call(bf16[512,896]{1,0:T(8,128)(2,1)} %cot_hbm.7, bf16[4096,896]{1,0:T(8,128)(2,1)} %weight_hbm), custom_call_target="tpu_custom_call" | custom-call | flops 1000000 | bytes 100000 | tf_op jit(solution)/shard_map/pallas_call | solution.py:25
  31.2 0.0 copy-start.1
  31.2 5.4 %all-to-all-done.i = f32[64,16,128]{2,1,0:T(8,128)S(1)} async-done(((f32[64,16,128]{2,1,0:T(8,128)}), f32[64,16,128]{2,1,0:T(8,128)S(1)}, u32[]{:S(2)}, u32[]{:S(2)}) %all-to-all-start) | async-done | bytes 524320 | tf_op jit(solution)/shard_map/all_to_all | solution.py:609
  36.6 0.9 shard_map.87
  37.6 0.0 collective-permute-start.5
  37.6 0.5 collective-permute-start.1
  38.1 5.0 %all-to-all-start.1 = ((f32[64,16,128]{2,1,0:T(8,128)}), f32[64,16,128]{2,1,0:T(8,128)S(1)}, u32[]{:S(2)}, u32[]{:S(2)}) async-start(f32[64,16,128]{2,1,0:T(8,128)} %shard_map.87), calls=%async_computation.1 | async-start | bytes 1048576 | tf_op jit(solution)/shard_map/all_to_all | solution.py:616
  43.0 1.5 %collective-permute-done.1.refs_1_ = f32[64,4096]{1,0:T(8,128)S(1)} collective-permute-done((f32[64,4096]{1,0:T(8,128)}, f32[64,4096]{1,0:T(8,128)S(1)}, u32[]{:S(2)}, u32[]{:S(2)}) %collective-permute-start.1) | collective-permute-done | bytes 1048608 | tf_op jit(solution)/shard_map/ppermute | solution.py:618
  44.6 0.0 copy-start.6
  44.6 1.0 copy-done.6
  45.5 2.5 %shard_map.88 = (f32[64,2048]{1,0:T(8,128)}, f32[64,2048]{1,0:T(8,128)}) custom-call(f32[64,4096]{1,0:T(8,128)} %get-tuple-element.56.refs_0_, f32[64,4096]{1,0:T(8,128)} %copy-done.6), custom_call_target="tpu_custom_call" | custom-call | flops 1000000 | bytes 100000 | tf_op jit(solution)/shard_map/pallas_call | solution.py:25
  48.0 1.3 %collective-permute-start.4 = (f32[64,2048]{1,0:T(8,128)}, f32[64,2048]{1,0:T(8,128)S(1)}, u32[]{:S(2)}, u32[]{:S(2)}) collective-permute-start(f32[64,2048]{1,0:T(8,128)} %get-tuple-element.63), channel_id=1, source_target_pairs={{0,6},{1,7},{2,0},{3,1},{4,2},{5,3},{6,4},{7,5},{8,14},{9,15},{10,... | collective-permute-start | bytes 1572872 | tf_op jit(solution)/shard_map/ppermute | solution.py:626
  49.3 0.8 collective-permute-start.3
  50.1 6.6 %all-to-all-done.1.mine_hbm.mine_ref = f32[64,16,128]{2,1,0:T(8,128)S(1)} async-done(((f32[64,16,128]{2,1,0:T(8,128)}), f32[64,16,128]{2,1,0:T(8,128)S(1)}, u32[]{:S(2)}, u32[]{:S(2)}) %all-to-all-start.1) | async-done | bytes 524320 | tf_op jit(solution)/shard_map/all_to_all | solution.py:616
  56.7 0.0 collective-permute-start.2
  56.7 0.0 copy-done.1
  56.7 5.0 %shard_map.89 = (f32[64,64]{1,0:T(8,128)S(1)}, f32[64,896]{1,0:T(8,128)S(1)}, f32[64,512]{1,0:T(8,128)S(1)}, bf16[512,896]{1,0:T(8,128)(2,1)S(1)}, bf16[1,2048,8...) custom-call(f32[64,16,128]{2,1,0:T(8,128)S(1)} %all-to-all-done.1.mine_hbm.mine_ref, ...), custom_call_target="tpu_custom_call" | custom-call | flops 1000000 | bytes 100000 | tf_op jit(solution)/shard_map/pallas_call | solution.py:25
  61.6 0.8 collective-permute-done.4.high_hbm
  62.5 0.0 copy-start.7
  62.5 1.8 %collective-permute-done.3.low_hbm = f32[64,2048]{1,0:T(8,128)S(1)} collective-permute-done((f32[64,2048]{1,0:T(8,128)}, f32[64,2048]{1,0:T(8,128)S(1)}, u32[]{:S(2)}, u32[]{:S(2)}) %collective-permute-start.3) | collective-permute-done | bytes 524320 | tf_op jit(solution)/shard_map/ppermute | solution.py:625
  64.3 0.0 copy-start.8
  64.3 0.0 collective-permute-done.2.other_ref
  64.3 3.7 %shard_map.90 = (f32[64,64]{1,0:T(8,128)S(1)}, f32[16,32,128]{2,1,0:T(8,128)}) custom-call(f32[64,16,128]{2,1,0:T(8,128)S(1)} %collective-permute-done.2.other_ref, f32[64,64]{1,0:T(8,128)S(1)} %get-tuple-element.64.gram_ref, f32[64,896]{1,0:T(8,128)S(1)} %get-tuple-element.65.with_error_ref, f32[64,512]{1,0:T(8,128)S(1)} %get-tuple-element.66.with_acts_ref, ...), custom_call_target="tpu_custom_call" | custom-call | flops 1000000 | bytes 100000 | tf_op jit(solution)/shard_map/pallas_call | solution.py:328
  68.1 0.0 copy-done.7
  68.1 0.0 copy-done.8
  68.1 0.0 collective-permute-done.5.got_hbm
  68.1 4.1 %shard_map.92 = (f32[64,4096]{1,0:T(8,128)}, f32[64,4096]{1,0:T(8,128)}) custom-call(f32[192,4096]{1,0:T(8,128)} %get-tuple-element.81.keep_hbm, f32[192,4096]{1,0:T(8,128)} %collective-permute-done.5.got_hbm, f32[64,2048]{1,0:T(8,128)} %copy-done.8, f32[64,2048]{1,0:T(8,128)} %copy-done.7), custom_call_target="tpu_custom_call" | custom-call | flops 1000000 | bytes 100000 | tf_op jit(solution)/shard_map/pallas_call | solution.py:25
  72.2 0.4 collective-permute-start.7
  72.5 1.7 %collective-permute-start.6 = (f32[64,4096]{1,0:T(8,128)}, f32[64,4096]{1,0:T(8,128)}, u32[]{:S(2)}, u32[]{:S(2)}) collective-permute-start(f32[64,4096]{1,0:T(8,128)} %get-tuple-element.78), channel_id=1, source_target_pairs={{0,2},{1,3},{2,4},{3,5},{4,6},{5,7},{6,0},{7,1},{8,10},{9,11},{10,... | collective-permute-start | bytes 3145736 | tf_op jit(solution)/shard_map/ppermute | solution.py:636
  74.2 6.4 %all-to-all-start.2 = ((f32[16,32,128]{2,1,0:T(8,128)}), f32[16,32,128]{2,1,0:T(8,128)S(1)}, u32[]{:S(2)}, u32[]{:S(2)}) async-start(f32[16,32,128]{2,1,0:T(8,128)} %get-tuple-element.70), calls=%async_computation.2 | async-start | bytes 524288 | tf_op jit(solution)/shard_map/all_to_all | solution.py:638
  80.6 1.9 %shard_map.91 = (f32[64,4096]{1,0:T(8,128)}, bf16[4096,256]{1,0:T(8,128)(2,1)S(1)}) custom-call(f32[64,64]{1,0:T(8,128)S(1)} %get-tuple-element.71.factor_ref, f32[64,16,128]{2,1,0:T(8,128)S(1)} %all-to-all-done.1.mine_hbm.mine_ref, f32[64,16,128]{2,1,0:T(8,128)S(1)} %collective-permute-done.2.other_ref), custom_call_target="tpu_custom_call" | custom-call | flops 1000000 | bytes 100000 | tf_op jit(solution)/shard_map/pallas_call | solution.py:354
  82.6 0.0 copy-start.2
  82.6 1.4 %copy-done.2 = bf16[4096,256]{1,0:T(8,128)(2,1)} copy-done((bf16[4096,256]{1,0:T(8,128)(2,1)}, bf16[4096,256]{1,0:T(8,128)(2,1)S(1)}, u32[]{:S(2)}) %copy-start.2) | copy-done | bytes 2097176
  84.0 5.4 %all-to-all-done.2.i = f32[16,32,128]{2,1,0:T(8,128)S(1)} async-done(((f32[16,32,128]{2,1,0:T(8,128)}), f32[16,32,128]{2,1,0:T(8,128)S(1)}, u32[]{:S(2)}, u32[]{:S(2)}) %all-to-all-start.2) | async-done | bytes 262176 | tf_op jit(solution)/shard_map/all_to_all | solution.py:638
  89.3 0.8 shard_map.93
  90.1 3.8 %all-to-all-start.3 = ((f32[16,32,128]{2,1,0:T(8,128)}), f32[16,32,128]{2,1,0:T(8,128)S(1)}, u32[]{:S(2)}, u32[]{:S(2)}) async-start(f32[16,32,128]{2,1,0:T(8,128)} %shard_map.93), calls=%async_computation.3 | async-start | bytes 524288 | tf_op jit(solution)/shard_map/all_to_all | solution.py:643
  93.8 2.5 %collective-permute-done.7.left_hbm = f32[64,4096]{1,0:T(8,128)S(1)} collective-permute-done((f32[64,4096]{1,0:T(8,128)}, f32[64,4096]{1,0:T(8,128)S(1)}, u32[]{:S(2)}, u32[]{:S(2)}) %collective-permute-start.7) | collective-permute-done | bytes 1048608 | tf_op jit(solution)/shard_map/ppermute | solution.py:637
  96.3 0.0 copy-start.5
  96.3 2.1 %collective-permute-done.6.right_hbm = f32[64,4096]{1,0:T(8,128)} collective-permute-done((f32[64,4096]{1,0:T(8,128)}, f32[64,4096]{1,0:T(8,128)}, u32[]{:S(2)}, u32[]{:S(2)}) %collective-permute-start.6) | collective-permute-done | bytes 1048608 | tf_op jit(solution)/shard_map/ppermute | solution.py:636
  98.4 0.0 copy-done.5
  98.4 3.2 %shard_map.94 = bf16[64,4096]{1,0:T(8,128)(2,1)} custom-call(f32[192,4096]{1,0:T(8,128)} %get-tuple-element.81.keep_hbm, f32[192,4096]{1,0:T(8,128)} %collective-permute-done.5.got_hbm, f32[64,4096]{1,0:T(8,128)} %collective-permute-done.6.right_hbm, f32[64,4096]{1,0:T(8,128)} %copy-done.5), custom_call_target="tpu_custom_call" | custom-call | flops 1000000 | bytes 100000 | tf_op jit(solution)/shard_map/pallas_call | solution.py:25
  101.6 0.7 all-to-all-done.3.chunks_hbm
  102.3 0.0 copy-start.4
  102.3 0.7 copy-done.4
  103.0 11.8 %shard_map.95 = (bf16[4096,896]{1,0:T(8,128)(2,1)}, f32[64,896]{1,0:T(8,128)}) custom-call(f32[16,32,128]{2,1,0:T(8,128)} %copy-done.4, bf16[4096,256]{1,0:T(8,128)(2,1)} %copy-done.2, bf16[512,896]{1,0:T(8,128)(2,1)} %cot_hbm.7, bf16[512,4096]{1,0:T(8,128)(2,1)} %acts_hbm.5, bf16[4096,896]{1,0:T(8,128)(2,1)} %bitcast.4), custom_call_target="tpu_custom_call" | custom-call | flops 1000000 | bytes 100000 | tf_op jit(solution)/shard_map/pallas_call | solution.py:25
Async XLA Ops:
  0.6 1.2 %copy-start = (bf16[512,896]{1,0:T(8,128)(2,1)S(1)}, bf16[512,896]{1,0:T(8,128)(2,1)}, u32[]{:S(2)}) copy-start(bf16[512,896]{1,0:T(8,128)(2,1)} %cot_hbm.7) | copy-start | bytes 2752516
  1.8 0.9 copy-start.3
  8.3 2.0 %collective-permute-start = (f32[64,16,128]{2,1,0:T(8,128)S(1)}, f32[64,16,128]{2,1,0:T(8,128)S(1)}, u32[]{:S(2)}, u32[]{:S(2)}) collective-permute-start(f32[64,16,128]{2,1,0:T(8,128)S(1)} %get-tuple-element.51), channel_id=1, source_target_pairs={{0,1},{1,0},{2,3},{3,2},{4,5},{5,4},{6,7},{7,6},{8,9},{9,8},{10,11... | collective-permute-start | bytes 1572872 | tf_op jit(solution)/shard_map/ppermute | solution.py:607
  11.1 25.5 %all-to-all-start = ((f32[64,16,128]{2,1,0:T(8,128)}), f32[64,16,128]{2,1,0:T(8,128)S(1)}, u32[]{:S(2)}, u32[]{:S(2)}) async-start(f32[64,16,128]{2,1,0:T(8,128)} %add.3), calls=%async_computation | async-start | bytes 1048576 | tf_op jit(solution)/shard_map/all_to_all | solution.py:609
  31.2 25.4 %copy-start.1 = (bf16[512,896]{1,0:T(8,128)(2,1)S(1)}, bf16[512,896]{1,0:T(8,128)(2,1)}, u32[]{:S(2)}) copy-start(bf16[512,896]{1,0:T(8,128)(2,1)} %cot_hbm.7) | copy-start | bytes 2752516
  37.6 30.5 %collective-permute-start.5 = (f32[192,4096]{1,0:T(8,128)}, f32[192,4096]{1,0:T(8,128)}, u32[]{:S(2)}, u32[]{:S(2)}) collective-permute-start(f32[192,4096]{1,0:T(8,128)} %get-tuple-element.75), channel_id=1, source_target_pairs={{0,1},{1,0},{2,3},{3,2},{4,5},{5,4},{6,7},{7,6},{8,9},{9,8},{10,11... | collective-permute-start | bytes 9437192 | tf_op jit(solution)/shard_map/ppermute | solution.py:619
  37.6 7.0 %collective-permute-start.1 = (f32[64,4096]{1,0:T(8,128)}, f32[64,4096]{1,0:T(8,128)S(1)}, u32[]{:S(2)}, u32[]{:S(2)}) collective-permute-start(f32[64,4096]{1,0:T(8,128)} %get-tuple-element.59), channel_id=1, source_target_pairs={{0,1},{1,0},{2,3},{3,2},{4,5},{5,4},{6,7},{7,6},{8,9},{9,8},{10,11... | collective-permute-start | bytes 3145736 | tf_op jit(solution)/shard_map/ppermute | solution.py:618
  38.1 18.6 %all-to-all-start.1 = ((f32[64,16,128]{2,1,0:T(8,128)}), f32[64,16,128]{2,1,0:T(8,128)S(1)}, u32[]{:S(2)}, u32[]{:S(2)}) async-start(f32[64,16,128]{2,1,0:T(8,128)} %shard_map.87), calls=%async_computation.1 | async-start | bytes 1048576 | tf_op jit(solution)/shard_map/all_to_all | solution.py:616
  44.6 1.0 copy-start.6
  48.0 14.5 %collective-permute-start.4 = (f32[64,2048]{1,0:T(8,128)}, f32[64,2048]{1,0:T(8,128)S(1)}, u32[]{:S(2)}, u32[]{:S(2)}) collective-permute-start(f32[64,2048]{1,0:T(8,128)} %get-tuple-element.63), channel_id=1, source_target_pairs={{0,6},{1,7},{2,0},{3,1},{4,2},{5,3},{6,4},{7,5},{8,14},{9,15},{10,... | collective-permute-start | bytes 1572872 | tf_op jit(solution)/shard_map/ppermute | solution.py:626
  49.3 15.0 %collective-permute-start.3 = (f32[64,2048]{1,0:T(8,128)}, f32[64,2048]{1,0:T(8,128)S(1)}, u32[]{:S(2)}, u32[]{:S(2)}) collective-permute-start(f32[64,2048]{1,0:T(8,128)} %get-tuple-element.60), channel_id=1, source_target_pairs={{0,2},{1,3},{2,4},{3,5},{4,6},{5,7},{6,0},{7,1},{8,10},{9,11},{10,... | collective-permute-start | bytes 1572872 | tf_op jit(solution)/shard_map/ppermute | solution.py:625
  56.7 7.6 %collective-permute-start.2 = (f32[64,16,128]{2,1,0:T(8,128)S(1)}, f32[64,16,128]{2,1,0:T(8,128)S(1)}, u32[]{:S(2)}, u32[]{:S(2)}) collective-permute-start(f32[64,16,128]{2,1,0:T(8,128)S(1)} %all-to-all-done.1.mine_hbm.mine_ref), channel_id=1, source_target_pairs={{0,1},{1,0},{2,3},{3,2},{4,5},{5,4},{6,7},{7,6},{8,9},{9,8},{10,11... | collective-permute-start | bytes 1572872 | tf_op jit(solution)/shard_map/ppermute | solution.py:629
  62.5 5.6 %copy-start.7 = (f32[64,2048]{1,0:T(8,128)}, f32[64,2048]{1,0:T(8,128)S(1)}, u32[]{:S(2)}) copy-start(f32[64,2048]{1,0:T(8,128)S(1)} %collective-permute-done.4.high_hbm) | copy-start | bytes 1572868
  64.3 3.7 %copy-start.8 = (f32[64,2048]{1,0:T(8,128)}, f32[64,2048]{1,0:T(8,128)S(1)}, u32[]{:S(2)}) copy-start(f32[64,2048]{1,0:T(8,128)S(1)} %collective-permute-done.3.low_hbm) | copy-start | bytes 1572868
  72.2 24.2 %collective-permute-start.7 = (f32[64,4096]{1,0:T(8,128)}, f32[64,4096]{1,0:T(8,128)S(1)}, u32[]{:S(2)}, u32[]{:S(2)}) collective-permute-start(f32[64,4096]{1,0:T(8,128)} %get-tuple-element.80), channel_id=1, source_target_pairs={{0,6},{1,7},{2,0},{3,1},{4,2},{5,3},{6,4},{7,5},{8,14},{9,15},{10,... | collective-permute-start | bytes 3145736 | tf_op jit(solution)/shard_map/ppermute | solution.py:637
  72.5 25.9 %collective-permute-start.6 = (f32[64,4096]{1,0:T(8,128)}, f32[64,4096]{1,0:T(8,128)}, u32[]{:S(2)}, u32[]{:S(2)}) collective-permute-start(f32[64,4096]{1,0:T(8,128)} %get-tuple-element.78), channel_id=1, source_target_pairs={{0,2},{1,3},{2,4},{3,5},{4,6},{5,7},{6,0},{7,1},{8,10},{9,11},{10,... | collective-permute-start | bytes 3145736 | tf_op jit(solution)/shard_map/ppermute | solution.py:636
  74.2 15.1 %all-to-all-start.2 = ((f32[16,32,128]{2,1,0:T(8,128)}), f32[16,32,128]{2,1,0:T(8,128)S(1)}, u32[]{:S(2)}, u32[]{:S(2)}) async-start(f32[16,32,128]{2,1,0:T(8,128)} %get-tuple-element.70), calls=%async_computation.2 | async-start | bytes 524288 | tf_op jit(solution)/shard_map/all_to_all | solution.py:638
  82.6 1.4 %copy-start.2 = (bf16[4096,256]{1,0:T(8,128)(2,1)}, bf16[4096,256]{1,0:T(8,128)(2,1)S(1)}, u32[]{:S(2)}) copy-start(bf16[4096,256]{1,0:T(8,128)(2,1)S(1)} %get-tuple-element.86.basis_hbm) | copy-start | bytes 6291460
  90.1 12.2 %all-to-all-start.3 = ((f32[16,32,128]{2,1,0:T(8,128)}), f32[16,32,128]{2,1,0:T(8,128)S(1)}, u32[]{:S(2)}, u32[]{:S(2)}) async-start(f32[16,32,128]{2,1,0:T(8,128)} %shard_map.93), calls=%async_computation.3 | async-start | bytes 524288 | tf_op jit(solution)/shard_map/all_to_all | solution.py:643
  96.3 2.1 %copy-start.5 = (f32[64,4096]{1,0:T(8,128)}, f32[64,4096]{1,0:T(8,128)S(1)}, u32[]{:S(2)}) copy-start(f32[64,4096]{1,0:T(8,128)S(1)} %collective-permute-done.7.left_hbm) | copy-start | bytes 3145732
  102.3 0.7 copy-start.4

commit v4 on v3

--- a/solution.py
+++ b/solution.py
@@ -232,10 +232,10 @@
     return jnp.concatenate([b[i] * scale[i] for i in range(groups)], axis=0)
 
 
-def half_of(chunks_ref):
-    n = chunks_ref.shape[0] // 4
+def half_of(*refs):
+    chunks = [ref.at[i] for ref in refs for i in range(ref.shape[0])]
     return jnp.concatenate(
-        [jnp.concatenate([chunks_ref[4 * j + g] for j in range(n)], axis=1) for g in range(4)], axis=0
+        [jnp.concatenate([chunk[...] for chunk in chunks[g::4]], axis=1) for g in range(4)], axis=0
     )
 
 
@@ -337,8 +337,8 @@
 
 def prep_kernel(factor_ref, mine_ref, other_ref, basis_ref, out_ref):
     core = my_core()
+    width = mine_ref.shape[0] // 4 * LANES
     for ref, place in ((mine_ref, core), (other_ref, 1 - core)):
-        width = ref.shape[0] // 4 * LANES
         at = pl.ds(pl.multiple_of(place * width, width), width)
         x = dot_highest(factor_ref[...], half_of(ref))
         basis_ref[:, at] = x
@@ -362,14 +362,13 @@
 
 
 def final_kernel(
-    chunks_hbm,
+    chunks_ref,
     basis_hbm,
     cot_hbm,
     acts_hbm,
     error_hbm,
     out_hbm,
     q_ref,
-    chunks_ref,
     q4_ref,
     basis_ref,
     cot_ref,
@@ -380,7 +379,6 @@
 ):
     parts, step = error_ref.shape[:2]
     copies = Copies(sems)
-    chunks_copy = copies.start(chunks_hbm, chunks_ref)
     cot_copy = copies.start(cot_hbm, cot_ref)
     waits = []
     for i in range(parts):
@@ -392,7 +390,6 @@
                 copies.start(error_hbm.at[at, :], error_ref.at[i]),
             )
         )
-    chunks_copy.wait()
     tiles = q_ref.shape[1] // LANES
     for g in range(8):
         for j in range(tiles):
@@ -421,11 +418,10 @@
     return call(
         final_kernel,
         (chunks, basis4, cot, acts, error),
-        [HBM] * 5,
+        [VMEM] + [HBM] * 4,
         [shape((d, ff), BF16), shape((RANK, ff))],
         [HBM, VMEM],
         [
-            (chunks.shape, F32),
             ((4 * RANK, ff), BF16),
             ((parts, step, 4 * RANK), BF16),
             ((tokens, ff), BF16),
@@ -433,7 +429,7 @@
             ((parts, step, ff), BF16),
             ((parts, step, ff), BF16),
         ],
-        2 + 4 * parts,
+        1 + 4 * parts,
     )
 
 
@@ -492,78 +488,96 @@
     )
 
 
-def ring_kernel(takes, ins, outs, bufs, sems):
+def core_kernel(
+    far_keep_hbm,
+    far_got_hbm,
+    near_keep_hbm,
+    near_got_hbm,
+    far_low_hbm,
+    far_high_hbm,
+    plus_hbm,
+    minus_hbm,
+    keep_ref,
+    got_ref,
+    sems,
+):
     copies = Copies(sems)
-    loads = []
-    slot = 0
-    for take in takes:
-        started = []
-        for which, rows, cols in take:
-            started.append(copies.start(ins[which].at[rows, cols], bufs.at[slot]))
-            slot += 1
-        loads.append(started)
+    n, d = plus_hbm.shape
+    wide = far_low_hbm.shape[1]
+    rows = [slice(i * n, (i + 1) * n) for i in range(3)]
+    loads = [(copies.start(far_keep_hbm, keep_ref.at[rows[0], :]), copies.start(far_got_hbm, got_ref.at[rows[0], :]))]
+    for i in range(2):
+        loads.append(
+            (
+                copies.start(near_keep_hbm.at[rows[i], :], keep_ref.at[rows[i + 1], :]),
+                copies.start(near_got_hbm.at[rows[i], :], got_ref.at[rows[i + 1], :]),
+            )
+        )
     stores = []
-    slot = 0
-    for started, out in zip(loads, outs):
-        for copy in started:
+    for pair, at, outs in zip(loads, rows, ((far_low_hbm, far_high_hbm), (plus_hbm,), (minus_hbm,))):
+        for copy in pair:
             copy.wait()
-        total = bufs[slot]
-        for k in range(1, len(started)):
-            total = total + bufs[slot + k]
-        bufs[slot] = total
-        stores.append(copies.start(bufs.at[slot], out))
-        slot += len(started)
+        keep_ref[at, :] += got_ref[at, :]
+        if len(outs) == 2:
+            stores += [copies.start(keep_ref.at[at, :wide], outs[0]), copies.start(keep_ref.at[at, d - wide :], outs[1])]
+        else:
+            stores.append(copies.start(keep_ref.at[at, :], outs[0]))
     for store in stores:
         store.wait()
 
 
-def ring_sums(ins, takes, n, w):
-    slots = sum(len(take) for take in takes)
-    count = len(ins)
-
-    def kernel(*refs):
-        ring_kernel(takes, refs[:count], refs[count : count + len(takes)], *refs[count + len(takes) :])
-
+def core_sums(far_keep, far_got, near_keep, near_got):
+    n, d = far_keep.shape
     return call(
-        kernel,
-        ins,
-        [HBM] * count,
-        [shape((n, w))] * len(takes),
-        [HBM] * len(takes),
-        [((slots, n, w), F32)],
-        slots + len(takes),
-    )
-
-
-def near_kernel(keep_hbm, got_hbm, low_hbm, high_hbm, plus_hbm, minus_hbm, keep_ref, got_ref, relay_ref, sems):
+        core_kernel,
+        (far_keep, far_got, near_keep, near_got),
+        [HBM] * 4,
+        [shape((n, d // 2 + LANES))] * 2 + [shape((n, d))] * 2,
+        [HBM] * 4,
+        [((3 * n, d), F32)] * 2,
+        10,
+    )
+
+
+def relay_kernel(plus_hbm, minus_hbm, low_hbm, high_hbm, plus_out, minus_out, half_ref, relay_ref, sems):
     copies = Copies(sems)
-    n, d = plus_hbm.shape
+    d = plus_hbm.shape[1]
     w = d // 2
-    loads = [copies.start(low_hbm, relay_ref.at[0]), copies.start(high_hbm, relay_ref.at[1])]
-    loads += [copies.start(src.at[: 2 * n, :], dst) for src, dst in ((keep_hbm, keep_ref), (got_hbm, got_ref))]
-    for copy in loads:
-        copy.wait()
-    keep_ref[:n, w:] += got_ref[:n, w:]
-    keep_ref[:n, :w] = (keep_ref[:n, :w] + got_ref[:n, :w]) + relay_ref[0]
-    plus = copies.start(keep_ref.at[:n, :], plus_hbm)
-    keep_ref[n:, :w] += got_ref[n:, :w]
-    keep_ref[n:, w:] = (keep_ref[n:, w:] + got_ref[n:, w:]) + relay_ref[1]
-    minus = copies.start(keep_ref.at[n:, :], minus_hbm)
-    plus.wait()
-    minus.wait()
-
-
-def near_sums(keep, got, low, high):
-    n, d = low.shape[0], keep.shape[1]
-    return call(
-        near_kernel,
-        (keep, got, low, high),
-        [HBM] * 4,
-        [shape((n, d))] * 2,
-        [HBM] * 2,
-        [((2 * n, d), F32), ((2 * n, d), F32), ((2, n, d // 2), F32)],
-        6,
-    )
+    wide = low_hbm.shape[1]
+    parts = (
+        (plus_hbm, plus_out, low_hbm, slice(0, w), slice(0, w)),
+        (minus_hbm, minus_out, high_hbm, slice(w, d), slice(wide - w, wide)),
+    )
+    loads = [
+        (copies.start(src.at[:, at], half_ref.at[i]), copies.start(relay, relay_ref.at[i]))
+        for i, (src, _, relay, at, _) in enumerate(parts)
+    ]
+    stores = []
+    for i, (_, out, _, at, far) in enumerate(parts):
+        for copy in loads[i]:
+            copy.wait()
+        half_ref[i] += relay_ref[i, :, far]
+        stores.append(copies.start(half_ref.at[i], out.at[:, at]))
+    for store in stores:
+        store.wait()
+
+
+def relay_sums(plus, minus, low, high):
+    n, d = plus.shape
+    return pl.pallas_call(
+        relay_kernel,
+        in_specs=[HBM] * 4,
+        out_specs=[HBM] * 2,
+        out_shape=[shape((n, d))] * 2,
+        input_output_aliases={0: 0, 1: 1},
+        scratch_shapes=[
+            pltpu.VMEM((2, n, d // 2), F32),
+            pltpu.VMEM((2,) + low.shape, F32),
+            pltpu.SemaphoreType.DMA((6,)),
+        ],
+        compiler_params=pltpu.CompilerParams(vmem_limit_bytes=56 << 20),
+        cost_estimate=pl.CostEstimate(flops=10**6, bytes_accessed=10**5, transcendentals=0),
+    )(plus, minus, low, high)
 
 
 def close_kernel(keep_hbm, got_hbm, right_hbm, left_hbm, out_hbm, in_ref, out_ref, sems):
@@ -617,27 +631,22 @@
     far_send, near_send, _ = lax.optimization_barrier((far_send, near_send, spread_left))
     far_got = lax.ppermute(far_send, "tensor", pairs)
     near_got = lax.ppermute(near_send, "tensor", pairs)
-    n, w = far_keep.shape[0], far_keep.shape[1] // 2
-    low, high = slice(0, w), slice(w, 2 * w)
-    far_low, far_high = ring_sums(
-        (far_keep, far_got), (((0, slice(0, n), low), (1, slice(0, n), low)), ((0, slice(0, n), high), (1, slice(0, n), high))), n, w
-    )
+    far_low, far_high, plus, minus = core_sums(far_keep, far_got, near_keep, near_got)
     low_relay = lax.ppermute(far_low, "tensor", right_ring)
     high_relay = lax.ppermute(far_high, "tensor", left_ring)
     mine, _ = lax.optimization_barrier((mine, far_low))
 
     other = lax.ppermute(mine, "tensor", pairs)
     terms = first(mine, up_cot, acts, error)
-    gram, low_relay, high_relay = lax.optimization_barrier((terms[0], low_relay, high_relay))
-    factor, right = second(other, [gram, *terms[1:]])
-
-    near_keep, _ = lax.optimization_barrier((near_keep, factor))
-    plus, minus = near_sums(near_keep, near_got, low_relay, high_relay)
+    factor, right = second(other, terms)
+
+    low_relay, high_relay, right = lax.optimization_barrier((low_relay, high_relay, right))
+    plus, minus = relay_sums(plus, minus, low_relay, high_relay)
     from_left = lax.ppermute(plus, "tensor", right_ring)
     from_right = lax.ppermute(minus, "tensor", left_ring)
     right_parts = lax.all_to_all(right, "dp", 0, 0)
     basis, basis4 = prep(factor, mine, other)
-    right_parts, basis4, _ = lax.optimization_barrier((right_parts, basis4, plus))
+    right_parts, basis4 = lax.optimization_barrier((right_parts, basis4))
 
     spread_right = spread(right_parts, 1.0 / n_dp)
     q_chunks = lax.all_to_all(spread_right, "dp", 0, 0)

time: 115 us -> 116 us (level)
  waiting for transfers between devices: 26.7 us -> 23.2 us
  Pallas kernels: 49.8 us -> 51.1 us
  local copies, waits for them, and re-layouts: 5.18 us -> 6.44 us
  starting transfers between devices: 31.4 us -> 32.6 us
    ppermute x1, starting transfers between devices: 0.36 us -> 3.22 us  [body(): from_right = lax.ppermute(minus, 'tensor', left_ring)]
    ppermute x1, waiting for transfers between devices: 2.49 us -> 0.01 us  [body(): from_right = lax.ppermute(minus, 'tensor', left_ring)]
    pallas_call x0 -> x1, Pallas kernels: none -> 2.48 us  [relay_sums(): pl.pallas_call(relay_kernel, in_specs=[HBM] * 4, out_specs=[HBM] * 2, out...]
    all_to_all x1, waiting for transfers between devices: 6.56 us -> 4.4 us  [body(): mine = lax.all_to_all(spread_left, both, 0, 0, axis_index_groups=groups)]
    ppermute x1, starting transfers between devices: 1.73 us -> 0.07 us  [body(): from_left = lax.ppermute(plus, 'tensor', right_ring)]
    unnamed x18, local copies, waits for them, and re-layouts: 5.18 us -> 6.44 us
    pallas_call x7 -> x6, Pallas kernels: 40.6 us -> 39.4 us  [call(): pl.pallas_call(kernel, in_specs=specs, out_specs=out_specs, out_shape=out...]
  transfers between devices with their start and end apart: 12 -> 12, of which waited for: 9 -> 8; matrix products, arithmetic and copies ran while one was open for 0% -> 0% of each run, Pallas kernels for 24% -> 26%
where the time goes in v4:
time: 116 us; the launch traced here: 115 us
  Pallas kernels  51.1 us (44%)
  starting transfers between devices  32.6 us (28%)
  waiting for transfers between devices  23.2 us (20%)
  local copies, waits for them, and re-layouts  6.44 us (6%)
    pallas_call x6, Pallas kernels, call(): pl.pallas_call(kernel, in_specs=specs, out_specs=out_specs, out_shape=out...  39.4 us
    all_to_all x1, starting transfers between devices, body(): chunks = lax.all_to_all(total, both, 0, 0, axis_index_groups=groups)  11.5 us
    unnamed x18, local copies, waits for them, and re-layouts  6.44 us
    all_to_all x1, starting transfers between devices, body(): right_parts = lax.all_to_all(right, 'dp', 0, 0)  6.36 us
    all_to_all x1, waiting for transfers between devices, body(): chunks = lax.all_to_all(total, both, 0, 0, axis_index_groups=groups)  5.4 us
    all_to_all x1, waiting for transfers between devices, body(): right_parts = lax.all_to_all(right, 'dp', 0, 0)  5.36 us
    all_to_all x1, starting transfers between devices, body(): mine = lax.all_to_all(spread_left, both, 0, 0, axis_index_groups=groups)  4.95 us
    all_to_all x1, waiting for transfers between devices, body(): mine = lax.all_to_all(spread_left, both, 0, 0, axis_index_groups=groups)  4.4 us
  transfers between devices with their start and end apart: 12, of which 8 were waited for; matrix products, arithmetic and copies ran while one was open for 0% of the time, Pallas kernels for 26%

profile of v4, /device:TPU:0, one launch (start us, length us, event | category | flops | bytes accessed | tf_op | source)
XLA Modules:
  0.0 115.1 jit_solution(7015942762997270406)
XLA Ops:
  0.6 0.0 copy-start
  0.6 1.2 %copy-done = bf16[512,896]{1,0:T(8,128)(2,1)S(1)} copy-done((bf16[512,896]{1,0:T(8,128)(2,1)S(1)}, bf16[512,896]{1,0:T(8,128)(2,1)}, u32[]{:S(2)}) %copy-start) | copy-done | bytes 917528
  1.8 0.0 copy-start.3
  1.8 0.9 copy-done.3
  2.8 5.5 %shard_map.84 = (f32[64,16,128]{2,1,0:T(8,128)S(1)}, bf16[896,192]{1,0:T(8,128)(2,1)S(1)}, bf16[192,512]{1,0:T(8,128)(2,1)S(1)}, bf16[4,512,896]{2,1,0:T(8,128)(2,1)S(1)}, bf16[4,512,512]{2,1,0:T(8,128)(2,1)S(1)}) custom-call(f32[64,896]{1,0:T(8,128)S(1)} %copy-done.3, bf16[512,896]{1,0:T(8,128)(2,1)S(1)} %copy-done, bf16[512,4096]{1,0:T(8,128)(2,1)} %acts_hbm.5, ...), custom_call_target="tpu_custom_call" | custom-call | flops 1000000 | bytes 100000 | tf_op jit(solution)/shard_map/pallas_call | solution.py:25
  8.3 0.1 collective-permute-start
  8.3 1.9 %shard_map.85 = f32[64,16,128]{2,1,0:T(8,128)S(1)} custom-call(bf16[896,192]{1,0:T(8,128)(2,1)S(1)} %get-tuple-element.48.q3t_ref, bf16[192,512]{1,0:T(8,128)(2,1)S(1)} %get-tuple-element.49.p3_ref, bf16[4,512,896]{2,1,0:T(8,128)(2,1)S(1)} %get-tuple-element.50.error_ref, bf16[4,512,512]{2,1,0:T(8,128)(2,1)S(1)} %get-tuple-element.51.acts_ref), custom_call_target="tpu_custom_call" | custom-call | flops 1000000 | bytes 100000 | tf_op jit(solution)/shard_map/pallas_call | solution.py:171
  10.2 0.0 collective-permute-done
  10.3 0.9 add.3
  11.1 11.5 %all-to-all-start = ((f32[64,16,128]{2,1,0:T(8,128)}), f32[64,16,128]{2,1,0:T(8,128)S(1)}, u32[]{:S(2)}, u32[]{:S(2)}) async-start(f32[64,16,128]{2,1,0:T(8,128)} %add.3), calls=%async_computation | async-start | bytes 1048576 | tf_op jit(solution)/shard_map/all_to_all | solution.py:623
  22.6 8.6 %shard_map.86 = (f32[64,4096]{1,0:T(8,128)}, f32[192,4096]{1,0:T(8,128)}, f32[64,4096]{1,0:T(8,128)}, f32[192,4096]{1,0:T(8,128)}) custom-call(bf16[512,896]{1,0:T(8,128)(2,1)} %cot_hbm.7, bf16[4096,896]{1,0:T(8,128)(2,1)} %weight_hbm), custom_call_target="tpu_custom_call" | custom-call | flops 1000000 | bytes 100000 | tf_op jit(solution)/shard_map/pallas_call | solution.py:25
  31.2 5.4 %all-to-all-done.i = f32[64,16,128]{2,1,0:T(8,128)S(1)} async-done(((f32[64,16,128]{2,1,0:T(8,128)}), f32[64,16,128]{2,1,0:T(8,128)S(1)}, u32[]{:S(2)}, u32[]{:S(2)}) %all-to-all-start) | async-done | bytes 524320 | tf_op jit(solution)/shard_map/all_to_all | solution.py:623
  36.6 0.9 shard_map.87
  37.5 0.0 collective-permute-start.2
  37.5 0.5 collective-permute-start.1
  38.0 4.9 %all-to-all-start.1 = ((f32[64,16,128]{2,1,0:T(8,128)}), f32[64,16,128]{2,1,0:T(8,128)S(1)}, u32[]{:S(2)}, u32[]{:S(2)}) async-start(f32[64,16,128]{2,1,0:T(8,128)} %shard_map.87), calls=%async_computation.1 | async-start | bytes 1048576 | tf_op jit(solution)/shard_map/all_to_all | solution.py:630
  43.0 1.5 %collective-permute-done.1.far_got_hbm = f32[64,4096]{1,0:T(8,128)S(1)} collective-permute-done((f32[64,4096]{1,0:T(8,128)}, f32[64,4096]{1,0:T(8,128)S(1)}, u32[]{:S(2)}, u32[]{:S(2)}) %collective-permute-start.1) | collective-permute-done | bytes 1048608 | tf_op jit(solution)/shard_map/ppermute | solution.py:632
  44.5 0.0 copy-start.6
  44.5 0.5 collective-permute-done.2.near_got_hbm.got_hbm
  45.0 0.5 copy-done.6
  45.5 0.0 copy-start.1
  45.5 4.5 %shard_map.88 = (f32[64,2176]{1,0:T(8,128)}, f32[64,2176]{1,0:T(8,128)}, f32[64,4096]{1,0:T(8,128)}, f32[64,4096]{1,0:T(8,128)}) custom-call(f32[64,4096]{1,0:T(8,128)} %get-tuple-element.54.far_keep_hbm, f32[64,4096]{1,0:T(8,128)} %copy-done.6, f32[192,4096]{1,0:T(8,128)} %get-tuple-element.83.near_keep_hbm.keep_hbm, ...), custom_call_target="tpu_custom_call" | custom-call | flops 1000000 | bytes 100000 | tf_op jit(solution)/shard_map/pallas_call | solution.py:25
  50.0 1.3 %collective-permute-start.4 = (f32[64,2176]{1,0:T(8,128)}, f32[64,2176]{1,0:T(8,128)S(1)}, u32[]{:S(2)}, u32[]{:S(2)}) collective-permute-start(f32[64,2176]{1,0:T(8,128)} %get-tuple-element.64), channel_id=1, source_target_pairs={{0,6},{1,7},{2,0},{3,1},{4,2},{5,3},{6,4},{7,5},{8,14},{9,15},{10,... | collective-permute-start | bytes 1671176 | tf_op jit(solution)/shard_map/ppermute | solution.py:636
  51.3 0.8 collective-permute-start.3
  52.1 4.4 %all-to-all-done.1.mine_hbm.mine_ref = f32[64,16,128]{2,1,0:T(8,128)S(1)} async-done(((f32[64,16,128]{2,1,0:T(8,128)}), f32[64,16,128]{2,1,0:T(8,128)S(1)}, u32[]{:S(2)}, u32[]{:S(2)}) %all-to-all-start.1) | async-done | bytes 524320 | tf_op jit(solution)/shard_map/all_to_all | solution.py:630
  56.5 0.0 collective-permute-start.5
  56.5 0.0 copy-done.1
  56.5 5.0 %shard_map.89 = (f32[64,64]{1,0:T(8,128)S(1)}, f32[64,896]{1,0:T(8,128)S(1)}, f32[64,512]{1,0:T(8,128)S(1)}, bf16[512,896]{1,0:T(8,128)(2,1)S(1)}, bf16[1,2048,8...) custom-call(f32[64,16,128]{2,1,0:T(8,128)S(1)} %all-to-all-done.1.mine_hbm.mine_ref, ...), custom_call_target="tpu_custom_call" | custom-call | flops 1000000 | bytes 100000 | tf_op jit(solution)/shard_map/pallas_call | solution.py:25
  61.5 0.0 collective-permute-done.5.other_ref
  61.5 3.7 %shard_map.90 = (f32[64,64]{1,0:T(8,128)S(1)}, f32[16,32,128]{2,1,0:T(8,128)}) custom-call(f32[64,16,128]{2,1,0:T(8,128)S(1)} %collective-permute-done.5.other_ref, f32[64,64]{1,0:T(8,128)S(1)} %get-tuple-element.66.gram_ref, f32[64,896]{1,0:T(8,128)S(1)} %get-tuple-element.67.with_error_ref, f32[64,512]{1,0:T(8,128)S(1)} %get-tuple-element.68.with_acts_ref, ...), custom_call_target="tpu_custom_call" | custom-call | flops 1000000 | bytes 100000 | tf_op jit(solution)/shard_map/pallas_call | solution.py:328
  65.2 0.0 collective-permute-done.4.high_hbm
  65.2 0.0 copy-start.7
  65.2 1.8 %collective-permute-done.3.low_hbm = f32[64,2176]{1,0:T(8,128)S(1)} collective-permute-done((f32[64,2176]{1,0:T(8,128)}, f32[64,2176]{1,0:T(8,128)S(1)}, u32[]{:S(2)}, u32[]{:S(2)}) %collective-permute-start.3) | collective-permute-done | bytes 557088 | tf_op jit(solution)/shard_map/ppermute | solution.py:635
  67.0 0.0 copy-start.8
  67.0 0.0 copy-done.7
  67.0 0.8 copy-done.8
  67.8 2.5 %shard_map.93 = (f32[64,4096]{1,0:T(8,128)}, f32[64,4096]{1,0:T(8,128)}) custom-call(f32[64,4096]{1,0:T(8,128)} %get-tuple-element.77.plus_hbm, f32[64,4096]{1,0:T(8,128)} %get-tuple-element.78.minus_hbm, f32[64,2176]{1,0:T(8,128)} %copy-done.8, f32[64,2176]{1,0:T(8,128)} %copy-done.7), custom_call_target="tpu_custom_call", output_to_operand_aliasing={{0}: (0, {}), {1}: (1, {})} | custom-call | flops 1000000 | bytes 100000 | tf_op jit(solution)/shard_map/pallas_call | solution.py:567
  70.3 0.1 collective-permute-start.6
  70.4 3.2 %collective-permute-start.7 = (f32[64,4096]{1,0:T(8,128)}, f32[64,4096]{1,0:T(8,128)}, u32[]{:S(2)}, u32[]{:S(2)}) collective-permute-start(f32[64,4096]{1,0:T(8,128)} %get-tuple-element.82), channel_id=1, source_target_pairs={{0,6},{1,7},{2,0},{3,1},{4,2},{5,3},{6,4},{7,5},{8,14},{9,15},{10,... | collective-permute-start | bytes 3145736 | tf_op jit(solution)/shard_map/ppermute | solution.py:646
  73.6 6.4 %all-to-all-start.2 = ((f32[16,32,128]{2,1,0:T(8,128)}), f32[16,32,128]{2,1,0:T(8,128)S(1)}, u32[]{:S(2)}, u32[]{:S(2)}) async-start(f32[16,32,128]{2,1,0:T(8,128)} %get-tuple-element.73), calls=%async_computation.2 | async-start | bytes 524288 | tf_op jit(solution)/shard_map/all_to_all | solution.py:647
  80.0 1.9 %shard_map.91 = (f32[64,4096]{1,0:T(8,128)}, bf16[4096,256]{1,0:T(8,128)(2,1)S(1)}) custom-call(f32[64,64]{1,0:T(8,128)S(1)} %get-tuple-element.74.factor_ref, f32[64,16,128]{2,1,0:T(8,128)S(1)} %all-to-all-done.1.mine_hbm.mine_ref, f32[64,16,128]{2,1,0:T(8,128)S(1)} %collective-permute-done.5.other_ref), custom_call_target="tpu_custom_call" | custom-call | flops 1000000 | bytes 100000 | tf_op jit(solution)/shard_map/pallas_call | solution.py:354
  81.9 0.0 copy-start.2
  81.9 1.4 %copy-done.2 = bf16[4096,256]{1,0:T(8,128)(2,1)} copy-done((bf16[4096,256]{1,0:T(8,128)(2,1)}, bf16[4096,256]{1,0:T(8,128)(2,1)S(1)}, u32[]{:S(2)}) %copy-start.2) | copy-done | bytes 2097176
  83.3 5.4 %all-to-all-done.2.i = f32[16,32,128]{2,1,0:T(8,128)S(1)} async-done(((f32[16,32,128]{2,1,0:T(8,128)}), f32[16,32,128]{2,1,0:T(8,128)S(1)}, u32[]{:S(2)}, u32[]{:S(2)}) %all-to-all-start.2) | async-done | bytes 262176 | tf_op jit(solution)/shard_map/all_to_all | solution.py:647
  88.7 0.8 shard_map.92
  89.4 3.8 %all-to-all-start.3 = ((f32[16,32,128]{2,1,0:T(8,128)}), f32[16,32,128]{2,1,0:T(8,128)S(1)}, u32[]{:S(2)}, u32[]{:S(2)}) async-start(f32[16,32,128]{2,1,0:T(8,128)} %shard_map.92), calls=%async_computation.3 | async-start | bytes 524288 | tf_op jit(solution)/shard_map/all_to_all | solution.py:652
  93.2 2.6 %collective-permute-done.6.right_hbm = f32[64,4096]{1,0:T(8,128)S(1)} collective-permute-done((f32[64,4096]{1,0:T(8,128)}, f32[64,4096]{1,0:T(8,128)S(1)}, u32[]{:S(2)}, u32[]{:S(2)}) %collective-permute-start.6) | collective-permute-done | bytes 1048608 | tf_op jit(solution)/shard_map/ppermute | solution.py:645
  95.8 0.0 copy-start.5
  95.8 0.0 collective-permute-done.7.left_hbm
  95.8 1.0 copy-done.5
  96.7 3.2 %shard_map.94 = bf16[64,4096]{1,0:T(8,128)(2,1)} custom-call(f32[192,4096]{1,0:T(8,128)} %get-tuple-element.83.near_keep_hbm.keep_hbm, f32[192,4096]{1,0:T(8,128)} %collective-permute-done.2.near_got_hbm.got_hbm, f32[64,4096]{1,0:T(8,128)} %copy-done.5, f32[64,4096]{1,0:T(8,128)} %collective-permute-done.7.left_hbm), custom_call_target="tpu_custom_call" | custom-call | flops 1000000 | bytes 100000 | tf_op jit(solution)/shard_map/pallas_call | solution.py:25
  99.9 1.7 %all-to-all-done.3.chunks_ref = f32[16,32,128]{2,1,0:T(8,128)S(1)} async-done(((f32[16,32,128]{2,1,0:T(8,128)}), f32[16,32,128]{2,1,0:T(8,128)S(1)}, u32[]{:S(2)}, u32[]{:S(2)}) %all-to-all-start.3) | async-done | bytes 262176 | tf_op jit(solution)/shard_map/all_to_all | solution.py:652
  101.6 0.0 copy-start.4
  101.6 0.7 copy-done.4
  102.3 12.6 %shard_map.95 = (bf16[4096,896]{1,0:T(8,128)(2,1)}, f32[64,896]{1,0:T(8,128)}) custom-call(f32[16,32,128]{2,1,0:T(8,128)} %copy-done.4, bf16[4096,256]{1,0:T(8,128)(2,1)} %copy-done.2, bf16[512,896]{1,0:T(8,128)(2,1)} %cot_hbm.7, bf16[512,4096]{1,0:T(8,128)(2,1)} %acts_hbm.5, bf16[4096,896]{1,0:T(8,128)(2,1)} %bitcast.4), custom_call_target="tpu_custom_call" | custom-call | flops 1000000 | bytes 100000 | tf_op jit(solution)/shard_map/pallas_call | solution.py:25
Async XLA Ops:
  0.6 1.2 %copy-start = (bf16[512,896]{1,0:T(8,128)(2,1)S(1)}, bf16[512,896]{1,0:T(8,128)(2,1)}, u32[]{:S(2)}) copy-start(bf16[512,896]{1,0:T(8,128)(2,1)} %cot_hbm.7) | copy-start | bytes 2752516
  1.8 0.9 copy-start.3
  8.3 2.0 %collective-permute-start = (f32[64,16,128]{2,1,0:T(8,128)S(1)}, f32[64,16,128]{2,1,0:T(8,128)S(1)}, u32[]{:S(2)}, u32[]{:S(2)}) collective-permute-start(f32[64,16,128]{2,1,0:T(8,128)S(1)} %get-tuple-element.52), channel_id=1, source_target_pairs={{0,1},{1,0},{2,3},{3,2},{4,5},{5,4},{6,7},{7,6},{8,9},{9,8},{10,11... | collective-permute-start | bytes 1572872 | tf_op jit(solution)/shard_map/ppermute | solution.py:621
  11.1 25.5 %all-to-all-start = ((f32[64,16,128]{2,1,0:T(8,128)}), f32[64,16,128]{2,1,0:T(8,128)S(1)}, u32[]{:S(2)}, u32[]{:S(2)}) async-start(f32[64,16,128]{2,1,0:T(8,128)} %add.3), calls=%async_computation | async-start | bytes 1048576 | tf_op jit(solution)/shard_map/all_to_all | solution.py:623
  37.5 7.5 %collective-permute-start.2 = (f32[192,4096]{1,0:T(8,128)}, f32[192,4096]{1,0:T(8,128)}, u32[]{:S(2)}, u32[]{:S(2)}) collective-permute-start(f32[192,4096]{1,0:T(8,128)} %get-tuple-element.62), channel_id=1, source_target_pairs={{0,1},{1,0},{2,3},{3,2},{4,5},{5,4},{6,7},{7,6},{8,9},{9,8},{10,11... | collective-permute-start | bytes 9437192 | tf_op jit(solution)/shard_map/ppermute | solution.py:633
  37.5 7.0 %collective-permute-start.1 = (f32[64,4096]{1,0:T(8,128)}, f32[64,4096]{1,0:T(8,128)S(1)}, u32[]{:S(2)}, u32[]{:S(2)}) collective-permute-start(f32[64,4096]{1,0:T(8,128)} %get-tuple-element.60), channel_id=1, source_target_pairs={{0,1},{1,0},{2,3},{3,2},{4,5},{5,4},{6,7},{7,6},{8,9},{9,8},{10,11... | collective-permute-start | bytes 3145736 | tf_op jit(solution)/shard_map/ppermute | solution.py:632
  38.0 18.5 %all-to-all-start.1 = ((f32[64,16,128]{2,1,0:T(8,128)}), f32[64,16,128]{2,1,0:T(8,128)S(1)}, u32[]{:S(2)}, u32[]{:S(2)}) async-start(f32[64,16,128]{2,1,0:T(8,128)} %shard_map.87), calls=%async_computation.1 | async-start | bytes 1048576 | tf_op jit(solution)/shard_map/all_to_all | solution.py:630
  44.5 1.0 copy-start.6
  45.5 11.0 %copy-start.1 = (bf16[512,896]{1,0:T(8,128)(2,1)S(1)}, bf16[512,896]{1,0:T(8,128)(2,1)}, u32[]{:S(2)}) copy-start(bf16[512,896]{1,0:T(8,128)(2,1)} %cot_hbm.7) | copy-start | bytes 2752516
  50.0 15.2 %collective-permute-start.4 = (f32[64,2176]{1,0:T(8,128)}, f32[64,2176]{1,0:T(8,128)S(1)}, u32[]{:S(2)}, u32[]{:S(2)}) collective-permute-start(f32[64,2176]{1,0:T(8,128)} %get-tuple-element.64), channel_id=1, source_target_pairs={{0,6},{1,7},{2,0},{3,1},{4,2},{5,3},{6,4},{7,5},{8,14},{9,15},{10,... | collective-permute-start | bytes 1671176 | tf_op jit(solution)/shard_map/ppermute | solution.py:636
  51.3 15.7 %collective-permute-start.3 = (f32[64,2176]{1,0:T(8,128)}, f32[64,2176]{1,0:T(8,128)S(1)}, u32[]{:S(2)}, u32[]{:S(2)}) collective-permute-start(f32[64,2176]{1,0:T(8,128)} %get-tuple-element.63), channel_id=1, source_target_pairs={{0,2},{1,3},{2,4},{3,5},{4,6},{5,7},{6,0},{7,1},{8,10},{9,11},{10,... | collective-permute-start | bytes 1671176 | tf_op jit(solution)/shard_map/ppermute | solution.py:635
  56.5 5.0 %collective-permute-start.5 = (f32[64,16,128]{2,1,0:T(8,128)S(1)}, f32[64,16,128]{2,1,0:T(8,128)S(1)}, u32[]{:S(2)}, u32[]{:S(2)}) collective-permute-start(f32[64,16,128]{2,1,0:T(8,128)S(1)} %all-to-all-done.1.mine_hbm.mine_ref), channel_id=1, source_target_pairs={{0,1},{1,0},{2,3},{3,2},{4,5},{5,4},{6,7},{7,6},{8,9},{9,8},{10,11... | collective-permute-start | bytes 1572872 | tf_op jit(solution)/shard_map/ppermute | solution.py:639
  65.2 1.8 %copy-start.7 = (f32[64,2176]{1,0:T(8,128)}, f32[64,2176]{1,0:T(8,128)S(1)}, u32[]{:S(2)}) copy-start(f32[64,2176]{1,0:T(8,128)S(1)} %collective-permute-done.4.high_hbm) | copy-start | bytes 1671172
  67.0 0.8 copy-start.8
  70.3 25.5 %collective-permute-start.6 = (f32[64,4096]{1,0:T(8,128)}, f32[64,4096]{1,0:T(8,128)S(1)}, u32[]{:S(2)}, u32[]{:S(2)}) collective-permute-start(f32[64,4096]{1,0:T(8,128)} %get-tuple-element.81), channel_id=1, source_target_pairs={{0,2},{1,3},{2,4},{3,5},{4,6},{5,7},{6,0},{7,1},{8,10},{9,11},{10,... | collective-permute-start | bytes 3145736 | tf_op jit(solution)/shard_map/ppermute | solution.py:645
  70.4 25.4 %collective-permute-start.7 = (f32[64,4096]{1,0:T(8,128)}, f32[64,4096]{1,0:T(8,128)}, u32[]{:S(2)}, u32[]{:S(2)}) collective-permute-start(f32[64,4096]{1,0:T(8,128)} %get-tuple-element.82), channel_id=1, source_target_pairs={{0,6},{1,7},{2,0},{3,1},{4,2},{5,3},{6,4},{7,5},{8,14},{9,15},{10,... | collective-permute-start | bytes 3145736 | tf_op jit(solution)/shard_map/ppermute | solution.py:646
  73.6 15.1 %all-to-all-start.2 = ((f32[16,32,128]{2,1,0:T(8,128)}), f32[16,32,128]{2,1,0:T(8,128)S(1)}, u32[]{:S(2)}, u32[]{:S(2)}) async-start(f32[16,32,128]{2,1,0:T(8,128)} %get-tuple-element.73), calls=%async_computation.2 | async-start | bytes 524288 | tf_op jit(solution)/shard_map/all_to_all | solution.py:647
  81.9 1.4 %copy-start.2 = (bf16[4096,256]{1,0:T(8,128)(2,1)}, bf16[4096,256]{1,0:T(8,128)(2,1)S(1)}, u32[]{:S(2)}) copy-start(bf16[4096,256]{1,0:T(8,128)(2,1)S(1)} %get-tuple-element.88.basis_hbm) | copy-start | bytes 6291460
  89.4 12.2 %all-to-all-start.3 = ((f32[16,32,128]{2,1,0:T(8,128)}), f32[16,32,128]{2,1,0:T(8,128)S(1)}, u32[]{:S(2)}, u32[]{:S(2)}) async-start(f32[16,32,128]{2,1,0:T(8,128)} %shard_map.92), calls=%async_computation.3 | async-start | bytes 524288 | tf_op jit(solution)/shard_map/all_to_all | solution.py:652
  95.8 1.0 copy-start.5
  101.6 0.7 copy-start.4

commit v5 on v4

--- a/solution.py
+++ b/solution.py
@@ -86,8 +86,8 @@
 def store_left(out_ref, i, left):
     tiles = left.shape[1] // LANES
     for j in range(tiles):
-        for g in range(4):
-            out_ref[4 * (i * tiles + j) + g] = left[16 * g : 16 * g + 16, LANES * j : LANES * (j + 1)]
+        for g in range(8):
+            out_ref[8 * (i * tiles + j) + g] = left[8 * g : 8 * g + 8, LANES * j : LANES * (j + 1)]
 
 
 def half_shapes(tokens, d, ff, parts):
@@ -153,7 +153,7 @@
         left_send_kernel,
         (q, cot, acts, error),
         [HBM] * 4,
-        [shape((d // 64, 16, LANES)), shape((ff, 3 * RANK), BF16), shape((3 * RANK, tokens), BF16)]
+        [shape((d // 32, 8, LANES)), shape((ff, 3 * RANK), BF16), shape((3 * RANK, tokens), BF16)]
         + [shape(s, BF16) for s in halves],
         [VMEM] * 5,
         [((RANK, ff), F32), ((tokens, ff), BF16)] + [(s, BF16) for s in halves],
@@ -178,20 +178,21 @@
     )(*held)
 
 
-def spread_kernel(scale, in_ref, out_ref):
+def spread_kernel(scale, kinds, in_ref, out_ref):
     n = in_ref.shape[0]
-    total = in_ref[0]
-    for i in range(1, n):
-        total = total + in_ref[i]
-    if scale != 1.0:
-        total = total * scale
-    for i in range(n):
-        out_ref[i] = total
-
-
-def spread(x, scale):
+    for kind in range(kinds):
+        total = in_ref[kind]
+        for i in range(kind + kinds, n, kinds):
+            total = total + in_ref[i]
+        if scale != 1.0:
+            total = total * scale
+        for i in range(kind, n, kinds):
+            out_ref[i] = total
+
+
+def spread(x, scale, kinds=1):
     return pl.pallas_call(
-        lambda i, o: spread_kernel(scale, i, o),
+        lambda i, o: spread_kernel(scale, kinds, i, o),
         in_specs=[VMEM],
         out_specs=VMEM,
         out_shape=shape(x.shape),
@@ -232,10 +233,10 @@
     return jnp.concatenate([b[i] * scale[i] for i in range(groups)], axis=0)
 
 
-def half_of(*refs):
-    chunks = [ref.at[i] for ref in refs for i in range(ref.shape[0])]
+def half_of(tiles_ref):
+    n = tiles_ref.shape[0] // 8
     return jnp.concatenate(
-        [jnp.concatenate([chunk[...] for chunk in chunks[g::4]], axis=1) for g in range(4)], axis=0
+        [jnp.concatenate([tiles_ref[8 * j + g] for j in range(n)], axis=1) for g in range(8)], axis=0
     )
 
 
@@ -337,7 +338,7 @@
 
 def prep_kernel(factor_ref, mine_ref, other_ref, basis_ref, out_ref):
     core = my_core()
-    width = mine_ref.shape[0] // 4 * LANES
+    width = mine_ref.shape[0] // 8 * LANES
     for ref, place in ((mine_ref, core), (other_ref, 1 - core)):
         at = pl.ds(pl.multiple_of(place * width, width), width)
         x = dot_highest(factor_ref[...], half_of(ref))
@@ -350,7 +351,7 @@
 
 
 def prep(factor, mine, other):
-    d = 2 * (mine.shape[0] // 4 * LANES)
+    d = 2 * (mine.shape[0] // 8 * LANES)
     return pl.pallas_call(
         prep_kernel,
         in_specs=[VMEM] * 3,
@@ -362,13 +363,14 @@
 
 
 def final_kernel(
-    chunks_ref,
+    chunks_hbm,
     basis_hbm,
     cot_hbm,
     acts_hbm,
     error_hbm,
     out_hbm,
     q_ref,
+    chunks_ref,
     q4_ref,
     basis_ref,
     cot_ref,
@@ -379,6 +381,7 @@
 ):
     parts, step = error_ref.shape[:2]
     copies = Copies(sems)
+    chunks_copy = copies.start(chunks_hbm, chunks_ref)
     cot_copy = copies.start(cot_hbm, cot_ref)
     waits = []
     for i in range(parts):
@@ -386,10 +389,11 @@
         waits.append(
             (
                 copies.start(acts_hbm.at[:, at], acts_ref.at[i]),
+                copies.start(error_hbm.at[at, :], error_ref.at[i]),
                 copies.start(basis_hbm.at[at, :], basis_ref.at[i]),
-                copies.start(error_hbm.at[at, :], error_ref.at[i]),
             )
         )
+    chunks_copy.wait()
     tiles = q_ref.shape[1] // LANES
     for g in range(8):
         for j in range(tiles):
@@ -418,10 +422,11 @@
     return call(
         final_kernel,
         (chunks, basis4, cot, acts, error),
-        [VMEM] + [HBM] * 4,
+        [HBM] * 5,
         [shape((d, ff), BF16), shape((RANK, ff))],
         [HBM, VMEM],
         [
+            (chunks.shape, F32),
             ((4 * RANK, ff), BF16),
             ((parts, step, 4 * RANK), BF16),
             ((tokens, ff), BF16),
@@ -429,7 +434,7 @@
             ((parts, step, ff), BF16),
             ((parts, step, ff), BF16),
         ],
-        1 + 4 * parts,
+        2 + 4 * parts,
     )
 
 
@@ -539,24 +544,20 @@
     )
 
 
-def relay_kernel(plus_hbm, minus_hbm, low_hbm, high_hbm, plus_out, minus_out, half_ref, relay_ref, sems):
+def relay_kernel(plus_hbm, minus_hbm, low_ref, high_ref, plus_out, minus_out, half_ref, sems):
     copies = Copies(sems)
     d = plus_hbm.shape[1]
     w = d // 2
-    wide = low_hbm.shape[1]
+    wide = low_ref.shape[1]
     parts = (
-        (plus_hbm, plus_out, low_hbm, slice(0, w), slice(0, w)),
-        (minus_hbm, minus_out, high_hbm, slice(w, d), slice(wide - w, wide)),
-    )
-    loads = [
-        (copies.start(src.at[:, at], half_ref.at[i]), copies.start(relay, relay_ref.at[i]))
-        for i, (src, _, relay, at, _) in enumerate(parts)
-    ]
+        (plus_hbm, plus_out, low_ref, slice(0, w), slice(0, w)),
+        (minus_hbm, minus_out, high_ref, slice(w, d), slice(wide - w, wide)),
+    )
+    loads = [copies.start(src.at[:, at], half_ref.at[i]) for i, (src, _, _, at, _) in enumerate(parts)]
     stores = []
-    for i, (_, out, _, at, far) in enumerate(parts):
-        for copy in loads[i]:
-            copy.wait()
-        half_ref[i] += relay_ref[i, :, far]
+    for i, (_, out, relay, at, far) in enumerate(parts):
+        loads[i].wait()
+        half_ref[i] += relay[:, far]
         stores.append(copies.start(half_ref.at[i], out.at[:, at]))
     for store in stores:
         store.wait()
@@ -566,16 +567,15 @@
     n, d = plus.shape
     return pl.pallas_call(
         relay_kernel,
-        in_specs=[HBM] * 4,
+        in_specs=[HBM] * 2 + [VMEM] * 2,
         out_specs=[HBM] * 2,
         out_shape=[shape((n, d))] * 2,
         input_output_aliases={0: 0, 1: 1},
         scratch_shapes=[
             pltpu.VMEM((2, n, d // 2), F32),
-            pltpu.VMEM((2,) + low.shape, F32),
-            pltpu.SemaphoreType.DMA((6,)),
+            pltpu.SemaphoreType.DMA((4,)),
         ],
-        compiler_params=pltpu.CompilerParams(vmem_limit_bytes=56 << 20),
+        compiler_params=pltpu.CompilerParams(vmem_limit_bytes=52 << 20),
         cost_estimate=pl.CostEstimate(flops=10**6, bytes_accessed=10**5, transcendentals=0),
     )(plus, minus, low, high)
 
@@ -611,7 +611,6 @@
     n_dp = lax.axis_size("dp")
     n_tensor = lax.axis_size("tensor")
     both = ("dp", "tensor")
-    groups = [[2 * i + c for i in range(n_dp * n_tensor // 2)] for c in range(2)]
     pairs = [(i, i ^ 1) for i in range(n_tensor)]
     right_ring = [(i, (i + 2) % n_tensor) for i in range(n_tensor)]
     left_ring = [(i, (i - 2) % n_tensor) for i in range(n_tensor)]
@@ -620,14 +619,14 @@
     send, *held = left_send(q_init, up_cot, acts, error)
     received = lax.ppermute(send, "tensor", pairs)
     total = left_keep(held, send.shape) + received
-    chunks = lax.all_to_all(total, both, 0, 0, axis_index_groups=groups)
+    chunks = lax.all_to_all(total, both, 0, 0)
 
     up_weight, _ = lax.optimization_barrier((up_weight, total))
     far_send, near_send, far_keep, near_keep = partials(up_cot, up_weight)
     chunks, far_send, near_send = lax.optimization_barrier((chunks, far_send, near_send))
 
-    spread_left = spread(chunks, 1.0)
-    mine = lax.all_to_all(spread_left, both, 0, 0, axis_index_groups=groups)
+    spread_left = spread(chunks, 1.0, kinds=2)
+    mine = lax.all_to_all(spread_left, both, 0, 0)
     far_send, near_send, _ = lax.optimization_barrier((far_send, near_send, spread_left))
     far_got = lax.ppermute(far_send, "tensor", pairs)
     near_got = lax.ppermute(near_send, "tensor", pairs)

time: 116 us -> 113 us (0.974)
  Pallas kernels: 51.1 us -> 49.8 us
    unnamed x18 -> x14, local copies, waits for them, and re-layouts: 6.44 us -> 5.65 us
where the time goes in v5:
time: 113 us
  Pallas kernels  49.8 us (44%)
  starting transfers between devices  32.7 us (29%)
  waiting for transfers between devices  22.8 us (20%)
  local copies, waits for them, and re-layouts  5.65 us (5%)
    pallas_call x6, Pallas kernels, call(): pl.pallas_call(kernel, in_specs=specs, out_specs=out_specs, out_shape=out...  38.5 us
    all_to_all x1, starting transfers between devices, body(): chunks = lax.all_to_all(total, both, 0, 0)  11.2 us
    all_to_all x1, starting transfers between devices, body(): right_parts = lax.all_to_all(right, 'dp', 0, 0)  6.84 us
    unnamed x14, local copies, waits for them, and re-layouts  5.65 us
    all_to_all x1, waiting for transfers between devices, body(): right_parts = lax.all_to_all(right, 'dp', 0, 0)  5.35 us
    all_to_all x1, waiting for transfers between devices, body(): chunks = lax.all_to_all(total, both, 0, 0)  4.91 us
    all_to_all x1, starting transfers between devices, body(): mine = lax.all_to_all(spread_left, both, 0, 0)  4.86 us
    all_to_all x1, waiting for transfers between devices, body(): mine = lax.all_to_all(spread_left, both, 0, 0)  4.36 us
  transfers between devices with their start and end apart: 12, of which 8 were waited for; matrix products, arithmetic and copies ran while one was open for 0% of the time, Pallas kernels for 26%

profile of v5, /device:TPU:0, one launch (start us, length us, event | category | flops | bytes accessed | tf_op | source)
XLA Modules:
  0.0 112.7 jit_solution(14828872457012778831)
XLA Ops:
  0.6 0.0 copy-start
  0.6 1.2 %copy-done = bf16[512,896]{1,0:T(8,128)(2,1)S(1)} copy-done((bf16[512,896]{1,0:T(8,128)(2,1)S(1)}, bf16[512,896]{1,0:T(8,128)(2,1)}, u32[]{:S(2)}) %copy-start) | copy-done | bytes 917528
  1.8 0.0 copy-start.3
  1.8 0.9 copy-done.3
  2.8 5.5 %shard_map.84 = (f32[128,8,128]{2,1,0:T(8,128)S(1)}, bf16[896,192]{1,0:T(8,128)(2,1)S(1)}, bf16[192,512]{1,0:T(8,128)(2,1)S(1)}, bf16[4,512,896]{2,1,0:T(8,128)(2,1)S(1)}, bf16[4,512,512]{2,1,0:T(8,128)(2,1)S(1)}) custom-call(f32[64,896]{1,0:T(8,128)S(1)} %copy-done.3, bf16[512,896]{1,0:T(8,128)(2,1)S(1)} %copy-done, bf16[512,4096]{1,0:T(8,128)(2,1)} %acts_hbm.5, ...), custom_call_target="tpu_custom_call" | custom-call | flops 1000000 | bytes 100000 | tf_op jit(solution)/shard_map/pallas_call | solution.py:25
  8.3 0.1 collective-permute-start
  8.3 1.9 %shard_map.85 = f32[128,8,128]{2,1,0:T(8,128)S(1)} custom-call(bf16[896,192]{1,0:T(8,128)(2,1)S(1)} %get-tuple-element.48.q3t_ref, bf16[192,512]{1,0:T(8,128)(2,1)S(1)} %get-tuple-element.49.p3_ref, bf16[4,512,896]{2,1,0:T(8,128)(2,1)S(1)} %get-tuple-element.50.error_ref, bf16[4,512,512]{2,1,0:T(8,128)(2,1)S(1)} %get-tuple-element.51.acts_ref), custom_call_target="tpu_custom_call" | custom-call | flops 1000000 | bytes 100000 | tf_op jit(solution)/shard_map/pallas_call | solution.py:171
  10.2 0.0 collective-permute-done
  10.3 0.8 add.3
  11.1 11.2 %all-to-all-start = ((f32[128,8,128]{2,1,0:T(8,128)}), f32[128,8,128]{2,1,0:T(8,128)S(1)}, u32[]{:S(2)}, u32[]{:S(2)}) async-start(f32[128,8,128]{2,1,0:T(8,128)} %add.3), calls=%async_computation | async-start | bytes 1048576 | tf_op jit(solution)/shard_map/all_to_all | solution.py:622
  22.3 8.6 %shard_map.86 = (f32[64,4096]{1,0:T(8,128)}, f32[192,4096]{1,0:T(8,128)}, f32[64,4096]{1,0:T(8,128)}, f32[192,4096]{1,0:T(8,128)}) custom-call(bf16[512,896]{1,0:T(8,128)(2,1)} %cot_hbm.7, bf16[4096,896]{1,0:T(8,128)(2,1)} %weight_hbm), custom_call_target="tpu_custom_call" | custom-call | flops 1000000 | bytes 100000 | tf_op jit(solution)/shard_map/pallas_call | solution.py:25
  31.0 4.9 %all-to-all-done.i = f32[128,8,128]{2,1,0:T(8,128)S(1)} async-done(((f32[128,8,128]{2,1,0:T(8,128)}), f32[128,8,128]{2,1,0:T(8,128)S(1)}, u32[]{:S(2)}, u32[]{:S(2)}) %all-to-all-start) | async-done | bytes 524320 | tf_op jit(solution)/shard_map/all_to_all | solution.py:622
  35.9 0.9 shard_map.87
  36.8 0.0 collective-permute-start.2
  36.8 0.5 collective-permute-start.1
  37.3 4.9 %all-to-all-start.1 = ((f32[128,8,128]{2,1,0:T(8,128)}), f32[128,8,128]{2,1,0:T(8,128)S(1)}, u32[]{:S(2)}, u32[]{:S(2)}) async-start(f32[128,8,128]{2,1,0:T(8,128)} %shard_map.87), calls=%async_computation.1 | async-start | bytes 1048576 | tf_op jit(solution)/shard_map/all_to_all | solution.py:629
  42.2 1.6 %collective-permute-done.1.far_got_hbm = f32[64,4096]{1,0:T(8,128)S(1)} collective-permute-done((f32[64,4096]{1,0:T(8,128)}, f32[64,4096]{1,0:T(8,128)S(1)}, u32[]{:S(2)}, u32[]{:S(2)}) %collective-permute-start.1) | collective-permute-done | bytes 1048608 | tf_op jit(solution)/shard_map/ppermute | solution.py:631
  43.8 0.0 copy-start.6
  43.8 0.5 collective-permute-done.2.near_got_hbm.got_hbm
  44.3 0.5 copy-done.6
  44.7 0.0 copy-start.1
  44.7 4.5 %shard_map.88 = (f32[64,2176]{1,0:T(8,128)}, f32[64,2176]{1,0:T(8,128)}, f32[64,4096]{1,0:T(8,128)}, f32[64,4096]{1,0:T(8,128)}) custom-call(f32[64,4096]{1,0:T(8,128)} %get-tuple-element.54.far_keep_hbm, f32[64,4096]{1,0:T(8,128)} %copy-done.6, f32[192,4096]{1,0:T(8,128)} %get-tuple-element.83.near_keep_hbm.keep_hbm, ...), custom_call_target="tpu_custom_call" | custom-call | flops 1000000 | bytes 100000 | tf_op jit(solution)/shard_map/pallas_call | solution.py:25
  49.2 0.9 collective-permute-start.4
  50.1 1.2 %collective-permute-start.3 = (f32[64,2176]{1,0:T(8,128)}, f32[64,2176]{1,0:T(8,128)S(1)}, u32[]{:S(2)}, u32[]{:S(2)}) collective-permute-start(f32[64,2176]{1,0:T(8,128)} %get-tuple-element.63), channel_id=1, source_target_pairs={{0,2},{1,3},{2,4},{3,5},{4,6},{5,7},{6,0},{7,1},{8,10},{9,11},{10,... | collective-permute-start | bytes 1671176 | tf_op jit(solution)/shard_map/ppermute | solution.py:634
  51.3 4.4 %all-to-all-done.1.mine_hbm.mine_ref = f32[128,8,128]{2,1,0:T(8,128)S(1)} async-done(((f32[128,8,128]{2,1,0:T(8,128)}), f32[128,8,128]{2,1,0:T(8,128)S(1)}, u32[]{:S(2)}, u32[]{:S(2)}) %all-to-all-start.1) | async-done | bytes 524320 | tf_op jit(solution)/shard_map/all_to_all | solution.py:629
  55.7 0.0 collective-permute-start.5
  55.7 0.0 copy-done.1
  55.7 5.0 %shard_map.89 = (f32[64,64]{1,0:T(8,128)S(1)}, f32[64,896]{1,0:T(8,128)S(1)}, f32[64,512]{1,0:T(8,128)S(1)}, bf16[512,896]{1,0:T(8,128)(2,1)S(1)}, bf16[1,2048,8...) custom-call(f32[128,8,128]{2,1,0:T(8,128)S(1)} %all-to-all-done.1.mine_hbm.mine_ref, ...), custom_call_target="tpu_custom_call" | custom-call | flops 1000000 | bytes 100000 | tf_op jit(solution)/shard_map/pallas_call | solution.py:25
  60.7 0.0 collective-permute-done.5.other_ref
  60.7 3.7 %shard_map.90 = (f32[64,64]{1,0:T(8,128)S(1)}, f32[16,32,128]{2,1,0:T(8,128)}) custom-call(f32[128,8,128]{2,1,0:T(8,128)S(1)} %collective-permute-done.5.other_ref, f32[64,64]{1,0:T(8,128)S(1)} %get-tuple-element.66.gram_ref, f32[64,896]{1,0:T(8,128)S(1)} %get-tuple-element.67.with_error_ref, f32[64,512]{1,0:T(8,128)S(1)} %get-tuple-element.68.with_acts_ref, ...), custom_call_target="tpu_custom_call" | custom-call | flops 1000000 | bytes 100000 | tf_op jit(solution)/shard_map/pallas_call | solution.py:329
  64.4 0.0 collective-permute-done.4.high_ref
  64.4 1.8 %collective-permute-done.3.low_ref = f32[64,2176]{1,0:T(8,128)S(1)} collective-permute-done((f32[64,2176]{1,0:T(8,128)}, f32[64,2176]{1,0:T(8,128)S(1)}, u32[]{:S(2)}, u32[]{:S(2)}) %collective-permute-start.3) | collective-permute-done | bytes 557088 | tf_op jit(solution)/shard_map/ppermute | solution.py:634
  66.2 2.1 %shard_map.93 = (f32[64,4096]{1,0:T(8,128)}, f32[64,4096]{1,0:T(8,128)}) custom-call(f32[64,4096]{1,0:T(8,128)} %get-tuple-element.77.plus_hbm, f32[64,4096]{1,0:T(8,128)} %get-tuple-element.78.minus_hbm, f32[64,2176]{1,0:T(8,128)S(1)} %collective-permute-done.3.low_ref, ...), custom_call_target="tpu_custom_call", output_to_operand_aliasing={{0}: (0, {}), {1}: (1, {})} | custom-call | flops 1000000 | bytes 100000 | tf_op jit(solution)/shard_map/pallas_call | solution.py:568
  68.3 0.1 collective-permute-start.6
  68.4 3.2 %collective-permute-start.7 = (f32[64,4096]{1,0:T(8,128)}, f32[64,4096]{1,0:T(8,128)}, u32[]{:S(2)}, u32[]{:S(2)}) collective-permute-start(f32[64,4096]{1,0:T(8,128)} %get-tuple-element.82), channel_id=1, source_target_pairs={{0,6},{1,7},{2,0},{3,1},{4,2},{5,3},{6,4},{7,5},{8,14},{9,15},{10,... | collective-permute-start | bytes 3145736 | tf_op jit(solution)/shard_map/ppermute | solution.py:645
  71.6 6.8 %all-to-all-start.2 = ((f32[16,32,128]{2,1,0:T(8,128)}), f32[16,32,128]{2,1,0:T(8,128)S(1)}, u32[]{:S(2)}, u32[]{:S(2)}) async-start(f32[16,32,128]{2,1,0:T(8,128)} %get-tuple-element.73), calls=%async_computation.2 | async-start | bytes 524288 | tf_op jit(solution)/shard_map/all_to_all | solution.py:646
  78.4 1.9 %shard_map.91 = (f32[64,4096]{1,0:T(8,128)}, bf16[4096,256]{1,0:T(8,128)(2,1)S(1)}) custom-call(f32[64,64]{1,0:T(8,128)S(1)} %get-tuple-element.74.factor_ref, f32[128,8,128]{2,1,0:T(8,128)S(1)} %all-to-all-done.1.mine_hbm.mine_ref, f32[128,8,128]{2,1,0:T(8,128)S(1)} %collective-permute-done.5.other_ref), custom_call_target="tpu_custom_call" | custom-call | flops 1000000 | bytes 100000 | tf_op jit(solution)/shard_map/pallas_call | solution.py:355
  80.4 0.0 copy-start.2
  80.4 1.4 %copy-done.2 = bf16[4096,256]{1,0:T(8,128)(2,1)} copy-done((bf16[4096,256]{1,0:T(8,128)(2,1)}, bf16[4096,256]{1,0:T(8,128)(2,1)S(1)}, u32[]{:S(2)}) %copy-start.2) | copy-done | bytes 2097176
  81.8 5.3 %all-to-all-done.2.i = f32[16,32,128]{2,1,0:T(8,128)S(1)} async-done(((f32[16,32,128]{2,1,0:T(8,128)}), f32[16,32,128]{2,1,0:T(8,128)S(1)}, u32[]{:S(2)}, u32[]{:S(2)}) %all-to-all-start.2) | async-done | bytes 262176 | tf_op jit(solution)/shard_map/all_to_all | solution.py:646
  87.1 0.8 shard_map.92
  87.9 3.8 %all-to-all-start.3 = ((f32[16,32,128]{2,1,0:T(8,128)}), f32[16,32,128]{2,1,0:T(8,128)S(1)}, u32[]{:S(2)}, u32[]{:S(2)}) async-start(f32[16,32,128]{2,1,0:T(8,128)} %shard_map.92), calls=%async_computation.3 | async-start | bytes 524288 | tf_op jit(solution)/shard_map/all_to_all | solution.py:651
  91.7 2.4 %collective-permute-done.6.right_hbm = f32[64,4096]{1,0:T(8,128)S(1)} collective-permute-done((f32[64,4096]{1,0:T(8,128)}, f32[64,4096]{1,0:T(8,128)S(1)}, u32[]{:S(2)}, u32[]{:S(2)}) %collective-permute-start.6) | collective-permute-done | bytes 1048608 | tf_op jit(solution)/shard_map/ppermute | solution.py:644
  94.1 0.0 copy-start.5
  94.1 0.0 collective-permute-done.7.left_hbm
  94.1 1.0 copy-done.5
  95.0 3.2 %shard_map.94 = bf16[64,4096]{1,0:T(8,128)(2,1)} custom-call(f32[192,4096]{1,0:T(8,128)} %get-tuple-element.83.near_keep_hbm.keep_hbm, f32[192,4096]{1,0:T(8,128)} %collective-permute-done.2.near_got_hbm.got_hbm, f32[64,4096]{1,0:T(8,128)} %copy-done.5, f32[64,4096]{1,0:T(8,128)} %collective-permute-done.7.left_hbm), custom_call_target="tpu_custom_call" | custom-call | flops 1000000 | bytes 100000 | tf_op jit(solution)/shard_map/pallas_call | solution.py:25
  98.2 1.8 %all-to-all-done.3.chunks_hbm = f32[16,32,128]{2,1,0:T(8,128)S(1)} async-done(((f32[16,32,128]{2,1,0:T(8,128)}), f32[16,32,128]{2,1,0:T(8,128)S(1)}, u32[]{:S(2)}, u32[]{:S(2)}) %all-to-all-start.3) | async-done | bytes 262176 | tf_op jit(solution)/shard_map/all_to_all | solution.py:651
  100.1 0.0 copy-start.4
  100.1 0.7 copy-done.4
  100.8 11.7 %shard_map.95 = (bf16[4096,896]{1,0:T(8,128)(2,1)}, f32[64,896]{1,0:T(8,128)}) custom-call(f32[16,32,128]{2,1,0:T(8,128)} %copy-done.4, bf16[4096,256]{1,0:T(8,128)(2,1)} %copy-done.2, bf16[512,896]{1,0:T(8,128)(2,1)} %cot_hbm.7, bf16[512,4096]{1,0:T(8,128)(2,1)} %acts_hbm.5, bf16[4096,896]{1,0:T(8,128)(2,1)} %bitcast.4), custom_call_target="tpu_custom_call" | custom-call | flops 1000000 | bytes 100000 | tf_op jit(solution)/shard_map/pallas_call | solution.py:25
Async XLA Ops:
  0.6 1.2 %copy-start = (bf16[512,896]{1,0:T(8,128)(2,1)S(1)}, bf16[512,896]{1,0:T(8,128)(2,1)}, u32[]{:S(2)}) copy-start(bf16[512,896]{1,0:T(8,128)(2,1)} %cot_hbm.7) | copy-start | bytes 2752516
  1.8 0.9 copy-start.3
  8.3 2.0 %collective-permute-start = (f32[128,8,128]{2,1,0:T(8,128)S(1)}, f32[128,8,128]{2,1,0:T(8,128)S(1)}, u32[]{:S(2)}, u32[]{:S(2)}) collective-permute-start(f32[128,8,128]{2,1,0:T(8,128)S(1)} %get-tuple-element.52), channel_id=1, source_target_pairs={{0,1},{1,0},{2,3},{3,2},{4,5},{5,4},{6,7},{7,6},{8,9},{9,8},{10,11... | collective-permute-start | bytes 1572872 | tf_op jit(solution)/shard_map/ppermute | solution.py:620
  11.1 24.8 %all-to-all-start = ((f32[128,8,128]{2,1,0:T(8,128)}), f32[128,8,128]{2,1,0:T(8,128)S(1)}, u32[]{:S(2)}, u32[]{:S(2)}) async-start(f32[128,8,128]{2,1,0:T(8,128)} %add.3), calls=%async_computation | async-start | bytes 1048576 | tf_op jit(solution)/shard_map/all_to_all | solution.py:622
  36.8 7.5 %collective-permute-start.2 = (f32[192,4096]{1,0:T(8,128)}, f32[192,4096]{1,0:T(8,128)}, u32[]{:S(2)}, u32[]{:S(2)}) collective-permute-start(f32[192,4096]{1,0:T(8,128)} %get-tuple-element.62), channel_id=1, source_target_pairs={{0,1},{1,0},{2,3},{3,2},{4,5},{5,4},{6,7},{7,6},{8,9},{9,8},{10,11... | collective-permute-start | bytes 9437192 | tf_op jit(solution)/shard_map/ppermute | solution.py:632
  36.8 7.0 %collective-permute-start.1 = (f32[64,4096]{1,0:T(8,128)}, f32[64,4096]{1,0:T(8,128)S(1)}, u32[]{:S(2)}, u32[]{:S(2)}) collective-permute-start(f32[64,4096]{1,0:T(8,128)} %get-tuple-element.60), channel_id=1, source_target_pairs={{0,1},{1,0},{2,3},{3,2},{4,5},{5,4},{6,7},{7,6},{8,9},{9,8},{10,11... | collective-permute-start | bytes 3145736 | tf_op jit(solution)/shard_map/ppermute | solution.py:631
  37.3 18.4 %all-to-all-start.1 = ((f32[128,8,128]{2,1,0:T(8,128)}), f32[128,8,128]{2,1,0:T(8,128)S(1)}, u32[]{:S(2)}, u32[]{:S(2)}) async-start(f32[128,8,128]{2,1,0:T(8,128)} %shard_map.87), calls=%async_computation.1 | async-start | bytes 1048576 | tf_op jit(solution)/shard_map/all_to_all | solution.py:629
  43.8 1.0 copy-start.6
  44.7 11.0 %copy-start.1 = (bf16[512,896]{1,0:T(8,128)(2,1)S(1)}, bf16[512,896]{1,0:T(8,128)(2,1)}, u32[]{:S(2)}) copy-start(bf16[512,896]{1,0:T(8,128)(2,1)} %cot_hbm.7) | copy-start | bytes 2752516
  49.2 15.2 %collective-permute-start.4 = (f32[64,2176]{1,0:T(8,128)}, f32[64,2176]{1,0:T(8,128)S(1)}, u32[]{:S(2)}, u32[]{:S(2)}) collective-permute-start(f32[64,2176]{1,0:T(8,128)} %get-tuple-element.64), channel_id=1, source_target_pairs={{0,6},{1,7},{2,0},{3,1},{4,2},{5,3},{6,4},{7,5},{8,14},{9,15},{10,... | collective-permute-start | bytes 1671176 | tf_op jit(solution)/shard_map/ppermute | solution.py:635
  50.1 16.0 %collective-permute-start.3 = (f32[64,2176]{1,0:T(8,128)}, f32[64,2176]{1,0:T(8,128)S(1)}, u32[]{:S(2)}, u32[]{:S(2)}) collective-permute-start(f32[64,2176]{1,0:T(8,128)} %get-tuple-element.63), channel_id=1, source_target_pairs={{0,2},{1,3},{2,4},{3,5},{4,6},{5,7},{6,0},{7,1},{8,10},{9,11},{10,... | collective-permute-start | bytes 1671176 | tf_op jit(solution)/shard_map/ppermute | solution.py:634
  55.7 5.0 %collective-permute-start.5 = (f32[128,8,128]{2,1,0:T(8,128)S(1)}, f32[128,8,128]{2,1,0:T(8,128)S(1)}, u32[]{:S(2)}, u32[]{:S(2)}) collective-permute-start(f32[128,8,128]{2,1,0:T(8,128)S(1)} %all-to-all-done.1.mine_hbm.mine_ref), channel_id=1, source_target_pairs={{0,1},{1,0},{2,3},{3,2},{4,5},{5,4},{6,7},{7,6},{8,9},{9,8},{10,11... | collective-permute-start | bytes 1572872 | tf_op jit(solution)/shard_map/ppermute | solution.py:638
  68.3 25.8 %collective-permute-start.6 = (f32[64,4096]{1,0:T(8,128)}, f32[64,4096]{1,0:T(8,128)S(1)}, u32[]{:S(2)}, u32[]{:S(2)}) collective-permute-start(f32[64,4096]{1,0:T(8,128)} %get-tuple-element.81), channel_id=1, source_target_pairs={{0,2},{1,3},{2,4},{3,5},{4,6},{5,7},{6,0},{7,1},{8,10},{9,11},{10,... | collective-permute-start | bytes 3145736 | tf_op jit(solution)/shard_map/ppermute | solution.py:644
  68.4 25.7 %collective-permute-start.7 = (f32[64,4096]{1,0:T(8,128)}, f32[64,4096]{1,0:T(8,128)}, u32[]{:S(2)}, u32[]{:S(2)}) collective-permute-start(f32[64,4096]{1,0:T(8,128)} %get-tuple-element.82), channel_id=1, source_target_pairs={{0,6},{1,7},{2,0},{3,1},{4,2},{5,3},{6,4},{7,5},{8,14},{9,15},{10,... | collective-permute-start | bytes 3145736 | tf_op jit(solution)/shard_map/ppermute | solution.py:645
  71.6 15.5 %all-to-all-start.2 = ((f32[16,32,128]{2,1,0:T(8,128)}), f32[16,32,128]{2,1,0:T(8,128)S(1)}, u32[]{:S(2)}, u32[]{:S(2)}) async-start(f32[16,32,128]{2,1,0:T(8,128)} %get-tuple-element.73), calls=%async_computation.2 | async-start | bytes 524288 | tf_op jit(solution)/shard_map/all_to_all | solution.py:646
  80.4 1.4 %copy-start.2 = (bf16[4096,256]{1,0:T(8,128)(2,1)}, bf16[4096,256]{1,0:T(8,128)(2,1)S(1)}, u32[]{:S(2)}) copy-start(bf16[4096,256]{1,0:T(8,128)(2,1)S(1)} %get-tuple-element.88.basis_hbm) | copy-start | bytes 6291460
  87.9 12.2 %all-to-all-start.3 = ((f32[16,32,128]{2,1,0:T(8,128)}), f32[16,32,128]{2,1,0:T(8,128)S(1)}, u32[]{:S(2)}, u32[]{:S(2)}) async-start(f32[16,32,128]{2,1,0:T(8,128)} %shard_map.92), calls=%async_computation.3 | async-start | bytes 524288 | tf_op jit(solution)/shard_map/all_to_all | solution.py:651
  94.1 1.0 copy-start.5
  100.1 0.7 copy-start.4

commit v6 on v5

--- a/solution.py
+++ b/solution.py
@@ -394,6 +394,9 @@
             )
         )
     chunks_copy.wait()
+    cot_copy.wait()
+    for copy in waits[0]:
+        copy.wait()
     tiles = q_ref.shape[1] // LANES
     for g in range(8):
         for j in range(tiles):
@@ -402,14 +405,15 @@
     q = -q_ref[...]
     high = q.astype(BF16)
     low = (q - high.astype(F32)).astype(BF16)
-    q4_ref[...] = jnp.concatenate([high, high, low, low], axis=0)
-    cot_copy.wait()
+    q4 = jnp.concatenate([high, high, low, low], axis=0)
+    q4_ref[...] = q4
     stores = []
     for i in range(parts):
-        for copy in waits[i]:
-            copy.wait()
+        if i:
+            for copy in waits[i]:
+                copy.wait()
         merged = dot(acts_ref[i], cot_ref[...], TN) + error_ref[i].astype(F32)
-        out_ref[i] = (merged + dot(basis_ref[i], q4_ref[...])).astype(BF16)
+        out_ref[i] = (merged + dot(basis_ref[i], q4_ref[...] if i else q4)).astype(BF16)
         stores.append(copies.start(out_ref.at[i], out_hbm.at[i * step : (i + 1) * step, :]))
     for store in stores:
         store.wait()
@@ -493,54 +497,65 @@
     )
 
 
-def core_kernel(
-    far_keep_hbm,
-    far_got_hbm,
-    near_keep_hbm,
-    near_got_hbm,
-    far_low_hbm,
-    far_high_hbm,
-    plus_hbm,
-    minus_hbm,
-    keep_ref,
-    got_ref,
-    sems,
-):
-    copies = Copies(sems)
-    n, d = plus_hbm.shape
-    wide = far_low_hbm.shape[1]
-    rows = [slice(i * n, (i + 1) * n) for i in range(3)]
-    loads = [(copies.start(far_keep_hbm, keep_ref.at[rows[0], :]), copies.start(far_got_hbm, got_ref.at[rows[0], :]))]
-    for i in range(2):
-        loads.append(
-            (
-                copies.start(near_keep_hbm.at[rows[i], :], keep_ref.at[rows[i + 1], :]),
-                copies.start(near_got_hbm.at[rows[i], :], got_ref.at[rows[i + 1], :]),
-            )
-        )
+def far_kernel(keep_hbm, got_hbm, low_hbm, high_hbm, keep_ref, got_ref, sems):
+    copies = Copies(sems)
+    d = keep_ref.shape[1]
+    wide = low_hbm.shape[1]
+    halves = (slice(0, d // 2), slice(d // 2, d))
+    loads = [
+        (copies.start(keep_hbm.at[:, at], keep_ref.at[:, at]), copies.start(got_hbm.at[:, at], got_ref.at[:, at]))
+        for at in halves
+    ]
+    for at, pair in zip(halves, loads):
+        for copy in pair:
+            copy.wait()
+        keep_ref[:, at] += got_ref[:, at]
+    stores = [copies.start(keep_ref.at[:, :wide], low_hbm), copies.start(keep_ref.at[:, d - wide :], high_hbm)]
+    for store in stores:
+        store.wait()
+
+
+def far_sums(keep, got):
+    n, d = keep.shape
+    return call(
+        far_kernel,
+        (keep, got),
+        [HBM] * 2,
+        [shape((n, d // 2 + LANES))] * 2,
+        [HBM] * 2,
+        [((n, d), F32)] * 2,
+        6,
+    )
+
+
+def near_kernel(keep_hbm, got_hbm, plus_hbm, minus_hbm, keep_ref, got_ref, sems):
+    copies = Copies(sems)
+    n = plus_hbm.shape[0]
+    rows = (slice(0, n), slice(n, 2 * n))
+    loads = [
+        (copies.start(keep_hbm.at[at, :], keep_ref.at[at, :]), copies.start(got_hbm.at[at, :], got_ref.at[at, :]))
+        for at in rows
+    ]
     stores = []
-    for pair, at, outs in zip(loads, rows, ((far_low_hbm, far_high_hbm), (plus_hbm,), (minus_hbm,))):
+    for at, pair, out in zip(rows, loads, (plus_hbm, minus_hbm)):
         for copy in pair:
             copy.wait()
         keep_ref[at, :] += got_ref[at, :]
-        if len(outs) == 2:
-            stores += [copies.start(keep_ref.at[at, :wide], outs[0]), copies.start(keep_ref.at[at, d - wide :], outs[1])]
-        else:
-            stores.append(copies.start(keep_ref.at[at, :], outs[0]))
+        stores.append(copies.start(keep_ref.at[at, :], out))
     for store in stores:
         store.wait()
 
 
-def core_sums(far_keep, far_got, near_keep, near_got):
-    n, d = far_keep.shape
+def near_sums(keep, got, n):
+    d = keep.shape[1]
     return call(
-        core_kernel,
-        (far_keep, far_got, near_keep, near_got),
-        [HBM] * 4,
-        [shape((n, d // 2 + LANES))] * 2 + [shape((n, d))] * 2,
-        [HBM] * 4,
-        [((3 * n, d), F32)] * 2,
-        10,
+        near_kernel,
+        (keep, got),
+        [HBM] * 2,
+        [shape((n, d))] * 2,
+        [HBM] * 2,
+        [((2 * n, d), F32)] * 2,
+        6,
     )
 
 
@@ -630,10 +645,11 @@
     far_send, near_send, _ = lax.optimization_barrier((far_send, near_send, spread_left))
     far_got = lax.ppermute(far_send, "tensor", pairs)
     near_got = lax.ppermute(near_send, "tensor", pairs)
-    far_low, far_high, plus, minus = core_sums(far_keep, far_got, near_keep, near_got)
+    far_low, far_high = far_sums(far_keep, far_got)
     low_relay = lax.ppermute(far_low, "tensor", right_ring)
     high_relay = lax.ppermute(far_high, "tensor", left_ring)
-    mine, _ = lax.optimization_barrier((mine, far_low))
+    plus, minus = near_sums(near_keep, near_got, far_keep.shape[0])
+    mine, _, plus = lax.optimization_barrier((mine, far_low, plus))
 
     other = lax.ppermute(mine, "tensor", pairs)
     terms = first(mine, up_cot, acts, error)

time: 113 us -> 112 us (level)
  waiting for transfers between devices: 22.8 us -> 18.9 us
  Pallas kernels: 49.8 us -> 51.4 us
    ppermute x1, waiting for transfers between devices: 1.76 us -> 0.02 us  [body(): low_relay = lax.ppermute(far_low, 'tensor', right_ring)]
    all_to_all x1, waiting for transfers between devices: 4.36 us -> 2.75 us  [body(): mine = lax.all_to_all(spread_left, both, 0, 0)]
    pallas_call x6 -> x7, Pallas kernels: 38.5 us -> 40 us  [call(): pl.pallas_call(kernel, in_specs=specs, out_specs=out_specs, out_shape=out...]
    ppermute x1, waiting for transfers between devices: 2.42 us -> 3.69 us  [body(): from_left = lax.ppermute(plus, 'tensor', right_ring)]
    all_to_all x1, waiting for transfers between devices: 1.85 us -> 0.57 us  [body(): q_chunks = lax.all_to_all(spread_right, 'dp', 0, 0)]
  transfers between devices with their start and end apart: 12 -> 12, of which waited for: 8 -> 6; matrix products, arithmetic and copies ran while one was open for 0% -> 0% of each run, Pallas kernels for 26% -> 28%
where the time goes in v6:
time: 112 us; the launch traced here: 111 us
  Pallas kernels  51.4 us (46%)
  starting transfers between devices  32.7 us (29%)
  waiting for transfers between devices  18.9 us (17%)
  local copies, waits for them, and re-layouts  6.15 us (5%)
    pallas_call x7, Pallas kernels, call(): pl.pallas_call(kernel, in_specs=specs, out_specs=out_specs, out_shape=out...  40 us
    all_to_all x1, starting transfers between devices, body(): chunks = lax.all_to_all(total, both, 0, 0)  11.2 us
    all_to_all x1, starting transfers between devices, body(): right_parts = lax.all_to_all(right, 'dp', 0, 0)  6.84 us
    unnamed x14, local copies, waits for them, and re-layouts  6.15 us
    all_to_all x1, waiting for transfers between devices, body(): right_parts = lax.all_to_all(right, 'dp', 0, 0)  5.35 us
    all_to_all x1, waiting for transfers between devices, body(): chunks = lax.all_to_all(total, both, 0, 0)  4.92 us
    all_to_all x1, starting transfers between devices, body(): mine = lax.all_to_all(spread_left, both, 0, 0)  4.86 us
    all_to_all x1, starting transfers between devices, body(): q_chunks = lax.all_to_all(spread_right, 'dp', 0, 0)  3.75 us
  transfers between devices with their start and end apart: 12, of which 6 were waited for; matrix products, arithmetic and copies ran while one was open for 0% of the time, Pallas kernels for 28%

profile of v6, /device:TPU:0, one launch (start us, length us, event | category | flops | bytes accessed | tf_op | source)
XLA Modules:
  0.0 111.0 jit_solution(16877843196380157359)
XLA Ops:
  0.6 0.0 copy-start
  0.6 1.2 %copy-done = bf16[512,896]{1,0:T(8,128)(2,1)S(1)} copy-done((bf16[512,896]{1,0:T(8,128)(2,1)S(1)}, bf16[512,896]{1,0:T(8,128)(2,1)}, u32[]{:S(2)}) %copy-start) | copy-done | bytes 917528
  1.8 0.0 copy-start.3
  1.8 0.9 copy-done.3
  2.8 5.5 %shard_map.84 = (f32[128,8,128]{2,1,0:T(8,128)S(1)}, bf16[896,192]{1,0:T(8,128)(2,1)S(1)}, bf16[192,512]{1,0:T(8,128)(2,1)S(1)}, bf16[4,512,896]{2,1,0:T(8,128)(2,1)S(1)}, bf16[4,512,512]{2,1,0:T(8,128)(2,1)S(1)}) custom-call(f32[64,896]{1,0:T(8,128)S(1)} %copy-done.3, bf16[512,896]{1,0:T(8,128)(2,1)S(1)} %copy-done, bf16[512,4096]{1,0:T(8,128)(2,1)} %acts_hbm.5, ...), custom_call_target="tpu_custom_call" | custom-call | flops 1000000 | bytes 100000 | tf_op jit(solution)/shard_map/pallas_call | solution.py:25
  8.3 0.1 collective-permute-start
  8.3 1.9 %shard_map.85 = f32[128,8,128]{2,1,0:T(8,128)S(1)} custom-call(bf16[896,192]{1,0:T(8,128)(2,1)S(1)} %get-tuple-element.49.q3t_ref, bf16[192,512]{1,0:T(8,128)(2,1)S(1)} %get-tuple-element.50.p3_ref, bf16[4,512,896]{2,1,0:T(8,128)(2,1)S(1)} %get-tuple-element.51.error_ref, bf16[4,512,512]{2,1,0:T(8,128)(2,1)S(1)} %get-tuple-element.52.acts_ref), custom_call_target="tpu_custom_call" | custom-call | flops 1000000 | bytes 100000 | tf_op jit(solution)/shard_map/pallas_call | solution.py:171
  10.2 0.0 collective-permute-done
  10.3 0.8 add.3
  11.1 11.2 %all-to-all-start = ((f32[128,8,128]{2,1,0:T(8,128)}), f32[128,8,128]{2,1,0:T(8,128)S(1)}, u32[]{:S(2)}, u32[]{:S(2)}) async-start(f32[128,8,128]{2,1,0:T(8,128)} %add.3), calls=%async_computation | async-start | bytes 1048576 | tf_op jit(solution)/shard_map/all_to_all | solution.py:637
  22.3 8.6 %shard_map.86 = (f32[64,4096]{1,0:T(8,128)}, f32[192,4096]{1,0:T(8,128)}, f32[64,4096]{1,0:T(8,128)}, f32[192,4096]{1,0:T(8,128)}) custom-call(bf16[512,896]{1,0:T(8,128)(2,1)} %cot_hbm.7, bf16[4096,896]{1,0:T(8,128)(2,1)} %weight_hbm), custom_call_target="tpu_custom_call" | custom-call | flops 1000000 | bytes 100000 | tf_op jit(solution)/shard_map/pallas_call | solution.py:25
  31.0 4.9 %all-to-all-done.i = f32[128,8,128]{2,1,0:T(8,128)S(1)} async-done(((f32[128,8,128]{2,1,0:T(8,128)}), f32[128,8,128]{2,1,0:T(8,128)S(1)}, u32[]{:S(2)}, u32[]{:S(2)}) %all-to-all-start) | async-done | bytes 524320 | tf_op jit(solution)/shard_map/all_to_all | solution.py:637
  35.9 0.9 shard_map.87
  36.8 0.0 collective-permute-start.4
  36.8 0.5 collective-permute-start.1
  37.3 4.9 %all-to-all-start.1 = ((f32[128,8,128]{2,1,0:T(8,128)}), f32[128,8,128]{2,1,0:T(8,128)S(1)}, u32[]{:S(2)}, u32[]{:S(2)}) async-start(f32[128,8,128]{2,1,0:T(8,128)} %shard_map.87), calls=%async_computation.1 | async-start | bytes 1048576 | tf_op jit(solution)/shard_map/all_to_all | solution.py:644
  42.1 1.6 %collective-permute-done.1.got_hbm = f32[64,4096]{1,0:T(8,128)S(1)} collective-permute-done((f32[64,4096]{1,0:T(8,128)}, f32[64,4096]{1,0:T(8,128)S(1)}, u32[]{:S(2)}, u32[]{:S(2)}) %collective-permute-start.1) | collective-permute-done | bytes 1048608 | tf_op jit(solution)/shard_map/ppermute | solution.py:646
  43.8 0.0 copy-start.6
  43.8 1.0 copy-done.6
  44.7 2.7 %shard_map.88 = (f32[64,2176]{1,0:T(8,128)}, f32[64,2176]{1,0:T(8,128)}) custom-call(f32[64,4096]{1,0:T(8,128)} %get-tuple-element.55.keep_hbm, f32[64,4096]{1,0:T(8,128)} %copy-done.6), custom_call_target="tpu_custom_call" | custom-call | flops 1000000 | bytes 100000 | tf_op jit(solution)/shard_map/pallas_call | solution.py:25
  47.5 0.0 copy-start.1
  47.5 0.9 collective-permute-start.3
  48.4 1.2 %collective-permute-start.2 = (f32[64,2176]{1,0:T(8,128)}, f32[64,2176]{1,0:T(8,128)S(1)}, u32[]{:S(2)}, u32[]{:S(2)}) collective-permute-start(f32[64,2176]{1,0:T(8,128)} %get-tuple-element.62), channel_id=1, source_target_pairs={{0,2},{1,3},{2,4},{3,5},{4,6},{5,7},{6,0},{7,1},{8,10},{9,11},{10,... | collective-permute-start | bytes 1671176 | tf_op jit(solution)/shard_map/ppermute | solution.py:649
  49.6 0.0 collective-permute-done.4.got_hbm
  49.6 3.3 %shard_map.89 = (f32[64,4096]{1,0:T(8,128)}, f32[64,4096]{1,0:T(8,128)}) custom-call(f32[192,4096]{1,0:T(8,128)} %get-tuple-element.85.keep_hbm, f32[192,4096]{1,0:T(8,128)} %collective-permute-done.4.got_hbm), custom_call_target="tpu_custom_call" | custom-call | flops 1000000 | bytes 100000 | tf_op jit(solution)/shard_map/pallas_call | solution.py:25
  52.9 2.8 %all-to-all-done.1.mine_hbm.mine_ref = f32[128,8,128]{2,1,0:T(8,128)S(1)} async-done(((f32[128,8,128]{2,1,0:T(8,128)}), f32[128,8,128]{2,1,0:T(8,128)S(1)}, u32[]{:S(2)}, u32[]{:S(2)}) %all-to-all-start.1) | async-done | bytes 524320 | tf_op jit(solution)/shard_map/all_to_all | solution.py:644
  55.7 0.0 collective-permute-start.5
  55.7 0.0 copy-done.1
  55.7 5.0 %shard_map.90 = (f32[64,64]{1,0:T(8,128)S(1)}, f32[64,896]{1,0:T(8,128)S(1)}, f32[64,512]{1,0:T(8,128)S(1)}, bf16[512,896]{1,0:T(8,128)(2,1)S(1)}, bf16[1,2048,8...) custom-call(f32[128,8,128]{2,1,0:T(8,128)S(1)} %all-to-all-done.1.mine_hbm.mine_ref, ...), custom_call_target="tpu_custom_call" | custom-call | flops 1000000 | bytes 100000 | tf_op jit(solution)/shard_map/pallas_call | solution.py:25
  60.6 0.0 collective-permute-done.5.other_ref
  60.7 3.7 %shard_map.91 = (f32[64,64]{1,0:T(8,128)S(1)}, f32[16,32,128]{2,1,0:T(8,128)}) custom-call(f32[128,8,128]{2,1,0:T(8,128)S(1)} %collective-permute-done.5.other_ref, f32[64,64]{1,0:T(8,128)S(1)} %get-tuple-element.68.gram_ref, f32[64,896]{1,0:T(8,128)S(1)} %get-tuple-element.69.with_error_ref, f32[64,512]{1,0:T(8,128)S(1)} %get-tuple-element.70.with_acts_ref, ...), custom_call_target="tpu_custom_call" | custom-call | flops 1000000 | bytes 100000 | tf_op jit(solution)/shard_map/pallas_call | solution.py:329
  64.4 0.0 collective-permute-done.3.high_ref
  64.4 0.0 collective-permute-done.2.low_ref
  64.4 2.1 %shard_map.94 = (f32[64,4096]{1,0:T(8,128)}, f32[64,4096]{1,0:T(8,128)}) custom-call(f32[64,4096]{1,0:T(8,128)} %get-tuple-element.79.plus_hbm, f32[64,4096]{1,0:T(8,128)} %get-tuple-element.80.minus_hbm, f32[64,2176]{1,0:T(8,128)S(1)} %collective-permute-done.2.low_ref, ...), custom_call_target="tpu_custom_call", output_to_operand_aliasing={{0}: (0, {}), {1}: (1, {})} | custom-call | flops 1000000 | bytes 100000 | tf_op jit(solution)/shard_map/pallas_call | solution.py:583
  66.5 1.0 collective-permute-start.6
  67.5 2.3 %collective-permute-start.7 = (f32[64,4096]{1,0:T(8,128)}, f32[64,4096]{1,0:T(8,128)}, u32[]{:S(2)}, u32[]{:S(2)}) collective-permute-start(f32[64,4096]{1,0:T(8,128)} %get-tuple-element.84), channel_id=1, source_target_pairs={{0,6},{1,7},{2,0},{3,1},{4,2},{5,3},{6,4},{7,5},{8,14},{9,15},{10,... | collective-permute-start | bytes 3145736 | tf_op jit(solution)/shard_map/ppermute | solution.py:661
  69.8 6.8 %all-to-all-start.2 = ((f32[16,32,128]{2,1,0:T(8,128)}), f32[16,32,128]{2,1,0:T(8,128)S(1)}, u32[]{:S(2)}, u32[]{:S(2)}) async-start(f32[16,32,128]{2,1,0:T(8,128)} %get-tuple-element.75), calls=%async_computation.2 | async-start | bytes 524288 | tf_op jit(solution)/shard_map/all_to_all | solution.py:662
  76.7 2.0 %shard_map.92 = (f32[64,4096]{1,0:T(8,128)}, bf16[4096,256]{1,0:T(8,128)(2,1)S(1)}) custom-call(f32[64,64]{1,0:T(8,128)S(1)} %get-tuple-element.76.factor_ref, f32[128,8,128]{2,1,0:T(8,128)S(1)} %all-to-all-done.1.mine_hbm.mine_ref, f32[128,8,128]{2,1,0:T(8,128)S(1)} %collective-permute-done.5.other_ref), custom_call_target="tpu_custom_call" | custom-call | flops 1000000 | bytes 100000 | tf_op jit(solution)/shard_map/pallas_call | solution.py:355
  78.6 0.0 copy-start.2
  78.6 1.4 %copy-done.2 = bf16[4096,256]{1,0:T(8,128)(2,1)} copy-done((bf16[4096,256]{1,0:T(8,128)(2,1)}, bf16[4096,256]{1,0:T(8,128)(2,1)S(1)}, u32[]{:S(2)}) %copy-start.2) | copy-done | bytes 2097176
  80.0 5.3 %all-to-all-done.2.i = f32[16,32,128]{2,1,0:T(8,128)S(1)} async-done(((f32[16,32,128]{2,1,0:T(8,128)}), f32[16,32,128]{2,1,0:T(8,128)S(1)}, u32[]{:S(2)}, u32[]{:S(2)}) %all-to-all-start.2) | async-done | bytes 262176 | tf_op jit(solution)/shard_map/all_to_all | solution.py:662
  85.4 0.8 shard_map.93
  86.1 3.8 %all-to-all-start.3 = ((f32[16,32,128]{2,1,0:T(8,128)}), f32[16,32,128]{2,1,0:T(8,128)S(1)}, u32[]{:S(2)}, u32[]{:S(2)}) async-start(f32[16,32,128]{2,1,0:T(8,128)} %shard_map.93), calls=%async_computation.3 | async-start | bytes 524288 | tf_op jit(solution)/shard_map/all_to_all | solution.py:667
  89.9 3.7 %collective-permute-done.6.right_hbm = f32[64,4096]{1,0:T(8,128)S(1)} collective-permute-done((f32[64,4096]{1,0:T(8,128)}, f32[64,4096]{1,0:T(8,128)S(1)}, u32[]{:S(2)}, u32[]{:S(2)}) %collective-permute-start.6) | collective-permute-done | bytes 1048608 | tf_op jit(solution)/shard_map/ppermute | solution.py:660
  93.6 0.0 copy-start.5
  93.6 0.0 collective-permute-done.7.left_hbm
  93.6 1.0 copy-done.5
  94.6 3.2 %shard_map.95 = bf16[64,4096]{1,0:T(8,128)(2,1)} custom-call(f32[192,4096]{1,0:T(8,128)} %get-tuple-element.85.keep_hbm, f32[192,4096]{1,0:T(8,128)} %collective-permute-done.4.got_hbm, f32[64,4096]{1,0:T(8,128)} %copy-done.5, f32[64,4096]{1,0:T(8,128)} %collective-permute-done.7.left_hbm), custom_call_target="tpu_custom_call" | custom-call | flops 1000000 | bytes 100000 | tf_op jit(solution)/shard_map/pallas_call | solution.py:25
  97.8 0.6 all-to-all-done.3.chunks_hbm
  98.3 0.0 copy-start.4
  98.3 0.7 copy-done.4
  99.0 11.7 %shard_map.96 = (bf16[4096,896]{1,0:T(8,128)(2,1)}, f32[64,896]{1,0:T(8,128)}) custom-call(f32[16,32,128]{2,1,0:T(8,128)} %copy-done.4, bf16[4096,256]{1,0:T(8,128)(2,1)} %copy-done.2, bf16[512,896]{1,0:T(8,128)(2,1)} %cot_hbm.7, bf16[512,4096]{1,0:T(8,128)(2,1)} %acts_hbm.5, bf16[4096,896]{1,0:T(8,128)(2,1)} %bitcast.4), custom_call_target="tpu_custom_call" | custom-call | flops 1000000 | bytes 100000 | tf_op jit(solution)/shard_map/pallas_call | solution.py:25
Async XLA Ops:
  0.6 1.2 %copy-start = (bf16[512,896]{1,0:T(8,128)(2,1)S(1)}, bf16[512,896]{1,0:T(8,128)(2,1)}, u32[]{:S(2)}) copy-start(bf16[512,896]{1,0:T(8,128)(2,1)} %cot_hbm.7) | copy-start | bytes 2752516
  1.8 0.9 copy-start.3
  8.3 2.0 %collective-permute-start = (f32[128,8,128]{2,1,0:T(8,128)S(1)}, f32[128,8,128]{2,1,0:T(8,128)S(1)}, u32[]{:S(2)}, u32[]{:S(2)}) collective-permute-start(f32[128,8,128]{2,1,0:T(8,128)S(1)} %get-tuple-element.53), channel_id=1, source_target_pairs={{0,1},{1,0},{2,3},{3,2},{4,5},{5,4},{6,7},{7,6},{8,9},{9,8},{10,11... | collective-permute-start | bytes 1572872 | tf_op jit(solution)/shard_map/ppermute | solution.py:635
  11.1 24.8 %all-to-all-start = ((f32[128,8,128]{2,1,0:T(8,128)}), f32[128,8,128]{2,1,0:T(8,128)S(1)}, u32[]{:S(2)}, u32[]{:S(2)}) async-start(f32[128,8,128]{2,1,0:T(8,128)} %add.3), calls=%async_computation | async-start | bytes 1048576 | tf_op jit(solution)/shard_map/all_to_all | solution.py:637
  36.8 12.8 %collective-permute-start.4 = (f32[192,4096]{1,0:T(8,128)}, f32[192,4096]{1,0:T(8,128)}, u32[]{:S(2)}, u32[]{:S(2)}) collective-permute-start(f32[192,4096]{1,0:T(8,128)} %get-tuple-element.65), channel_id=1, source_target_pairs={{0,1},{1,0},{2,3},{3,2},{4,5},{5,4},{6,7},{7,6},{8,9},{9,8},{10,11... | collective-permute-start | bytes 9437192 | tf_op jit(solution)/shard_map/ppermute | solution.py:647
  36.8 7.0 %collective-permute-start.1 = (f32[64,4096]{1,0:T(8,128)}, f32[64,4096]{1,0:T(8,128)S(1)}, u32[]{:S(2)}, u32[]{:S(2)}) collective-permute-start(f32[64,4096]{1,0:T(8,128)} %get-tuple-element.61), channel_id=1, source_target_pairs={{0,1},{1,0},{2,3},{3,2},{4,5},{5,4},{6,7},{7,6},{8,9},{9,8},{10,11... | collective-permute-start | bytes 3145736 | tf_op jit(solution)/shard_map/ppermute | solution.py:646
  37.3 18.4 %all-to-all-start.1 = ((f32[128,8,128]{2,1,0:T(8,128)}), f32[128,8,128]{2,1,0:T(8,128)S(1)}, u32[]{:S(2)}, u32[]{:S(2)}) async-start(f32[128,8,128]{2,1,0:T(8,128)} %shard_map.87), calls=%async_computation.1 | async-start | bytes 1048576 | tf_op jit(solution)/shard_map/all_to_all | solution.py:644
  43.8 1.0 copy-start.6
  47.5 8.2 %copy-start.1 = (bf16[512,896]{1,0:T(8,128)(2,1)S(1)}, bf16[512,896]{1,0:T(8,128)(2,1)}, u32[]{:S(2)}) copy-start(bf16[512,896]{1,0:T(8,128)(2,1)} %cot_hbm.7) | copy-start | bytes 2752516
  47.5 16.9 %collective-permute-start.3 = (f32[64,2176]{1,0:T(8,128)}, f32[64,2176]{1,0:T(8,128)S(1)}, u32[]{:S(2)}, u32[]{:S(2)}) collective-permute-start(f32[64,2176]{1,0:T(8,128)} %get-tuple-element.63), channel_id=1, source_target_pairs={{0,6},{1,7},{2,0},{3,1},{4,2},{5,3},{6,4},{7,5},{8,14},{9,15},{10,... | collective-permute-start | bytes 1671176 | tf_op jit(solution)/shard_map/ppermute | solution.py:650
  48.4 16.0 %collective-permute-start.2 = (f32[64,2176]{1,0:T(8,128)}, f32[64,2176]{1,0:T(8,128)S(1)}, u32[]{:S(2)}, u32[]{:S(2)}) collective-permute-start(f32[64,2176]{1,0:T(8,128)} %get-tuple-element.62), channel_id=1, source_target_pairs={{0,2},{1,3},{2,4},{3,5},{4,6},{5,7},{6,0},{7,1},{8,10},{9,11},{10,... | collective-permute-start | bytes 1671176 | tf_op jit(solution)/shard_map/ppermute | solution.py:649
  55.7 5.0 %collective-permute-start.5 = (f32[128,8,128]{2,1,0:T(8,128)S(1)}, f32[128,8,128]{2,1,0:T(8,128)S(1)}, u32[]{:S(2)}, u32[]{:S(2)}) collective-permute-start(f32[128,8,128]{2,1,0:T(8,128)S(1)} %all-to-all-done.1.mine_hbm.mine_ref), channel_id=1, source_target_pairs={{0,1},{1,0},{2,3},{3,2},{4,5},{5,4},{6,7},{7,6},{8,9},{9,8},{10,11... | collective-permute-start | bytes 1572872 | tf_op jit(solution)/shard_map/ppermute | solution.py:654
  66.5 27.1 %collective-permute-start.6 = (f32[64,4096]{1,0:T(8,128)}, f32[64,4096]{1,0:T(8,128)S(1)}, u32[]{:S(2)}, u32[]{:S(2)}) collective-permute-start(f32[64,4096]{1,0:T(8,128)} %get-tuple-element.83), channel_id=1, source_target_pairs={{0,2},{1,3},{2,4},{3,5},{4,6},{5,7},{6,0},{7,1},{8,10},{9,11},{10,... | collective-permute-start | bytes 3145736 | tf_op jit(solution)/shard_map/ppermute | solution.py:660
  67.5 26.1 %collective-permute-start.7 = (f32[64,4096]{1,0:T(8,128)}, f32[64,4096]{1,0:T(8,128)}, u32[]{:S(2)}, u32[]{:S(2)}) collective-permute-start(f32[64,4096]{1,0:T(8,128)} %get-tuple-element.84), channel_id=1, source_target_pairs={{0,6},{1,7},{2,0},{3,1},{4,2},{5,3},{6,4},{7,5},{8,14},{9,15},{10,... | collective-permute-start | bytes 3145736 | tf_op jit(solution)/shard_map/ppermute | solution.py:661
  69.8 15.5 %all-to-all-start.2 = ((f32[16,32,128]{2,1,0:T(8,128)}), f32[16,32,128]{2,1,0:T(8,128)S(1)}, u32[]{:S(2)}, u32[]{:S(2)}) async-start(f32[16,32,128]{2,1,0:T(8,128)} %get-tuple-element.75), calls=%async_computation.2 | async-start | bytes 524288 | tf_op jit(solution)/shard_map/all_to_all | solution.py:662
  78.6 1.4 %copy-start.2 = (bf16[4096,256]{1,0:T(8,128)(2,1)}, bf16[4096,256]{1,0:T(8,128)(2,1)S(1)}, u32[]{:S(2)}) copy-start(bf16[4096,256]{1,0:T(8,128)(2,1)S(1)} %get-tuple-element.90.basis_hbm) | copy-start | bytes 6291460
  86.1 12.2 %all-to-all-start.3 = ((f32[16,32,128]{2,1,0:T(8,128)}), f32[16,32,128]{2,1,0:T(8,128)S(1)}, u32[]{:S(2)}, u32[]{:S(2)}) async-start(f32[16,32,128]{2,1,0:T(8,128)} %shard_map.93), calls=%async_computation.3 | async-start | bytes 524288 | tf_op jit(solution)/shard_map/all_to_all | solution.py:667
  93.6 1.0 copy-start.5
  98.3 0.7 copy-start.4

commit v7 on v6

--- a/solution.py
+++ b/solution.py
@@ -368,8 +368,13 @@
     cot_hbm,
     acts_hbm,
     error_hbm,
+    keep_hbm,
+    got_hbm,
+    left_hbm,
+    right_hbm,
     out_hbm,
     q_ref,
+    input_grad_hbm,
     chunks_ref,
     q4_ref,
     basis_ref,
@@ -377,6 +382,8 @@
     acts_ref,
     error_ref,
     out_ref,
+    sums_ref,
+    input_grad_ref,
     sems,
 ):
     parts, step = error_ref.shape[:2]
@@ -393,6 +400,12 @@
                 copies.start(basis_hbm.at[at, :], basis_ref.at[i]),
             )
         )
+    n = input_grad_ref.shape[0]
+    own = slice(2 * n, 3 * n)
+    sums = [
+        copies.start(src, sums_ref.at[i])
+        for i, src in enumerate((keep_hbm.at[own, :], got_hbm.at[own, :], left_hbm, right_hbm))
+    ]
     chunks_copy.wait()
     cot_copy.wait()
     for copy in waits[0]:
@@ -415,20 +428,26 @@
         merged = dot(acts_ref[i], cot_ref[...], TN) + error_ref[i].astype(F32)
         out_ref[i] = (merged + dot(basis_ref[i], q4_ref[...] if i else q4)).astype(BF16)
         stores.append(copies.start(out_ref.at[i], out_hbm.at[i * step : (i + 1) * step, :]))
+        if i == parts - 2:
+            for copy in sums:
+                copy.wait()
+            total = (sums_ref[0] + sums_ref[1]) + (sums_ref[2] + sums_ref[3])
+            input_grad_ref[...] = total.astype(BF16)
+            stores.append(copies.start(input_grad_ref, input_grad_hbm))
     for store in stores:
         store.wait()
 
 
-def final(chunks, basis4, cot, acts, error, parts=8):
+def final(chunks, basis4, cot, acts, error, keep, got, from_left, from_right, parts=8):
     tokens, d = acts.shape
     ff = cot.shape[1]
     step = d // parts
     return call(
         final_kernel,
-        (chunks, basis4, cot, acts, error),
-        [HBM] * 5,
-        [shape((d, ff), BF16), shape((RANK, ff))],
-        [HBM, VMEM],
+        (chunks, basis4, cot, acts, error, keep, got, from_left, from_right),
+        [HBM] * 9,
+        [shape((d, ff), BF16), shape((RANK, ff)), shape(from_left.shape, BF16)],
+        [HBM, VMEM, HBM],
         [
             (chunks.shape, F32),
             ((4 * RANK, ff), BF16),
@@ -437,8 +456,11 @@
             ((parts, tokens, step), BF16),
             ((parts, step, ff), BF16),
             ((parts, step, ff), BF16),
+            ((4,) + from_left.shape, F32),
+            (from_left.shape, BF16),
         ],
-        2 + 4 * parts,
+        7 + 4 * parts,
+        limit=52 << 20,
     )
 
 
@@ -595,33 +617,6 @@
     )(plus, minus, low, high)
 
 
-def close_kernel(keep_hbm, got_hbm, right_hbm, left_hbm, out_hbm, in_ref, out_ref, sems):
-    copies = Copies(sems)
-    n = out_ref.shape[0]
-    own = slice(2 * n, 3 * n)
-    loads = [
-        copies.start(src, in_ref.at[i])
-        for i, src in enumerate((keep_hbm.at[own, :], got_hbm.at[own, :], right_hbm, left_hbm))
-    ]
-    for copy in loads:
-        copy.wait()
-    out_ref[...] = ((in_ref[0] + in_ref[1]) + (in_ref[2] + in_ref[3])).astype(BF16)
-    copies.start(out_ref, out_hbm).wait()
-
-
-def close(keep, got, right, left):
-    n, d = right.shape
-    return call(
-        close_kernel,
-        (keep, got, right, left),
-        [HBM] * 4,
-        shape((n, d), BF16),
-        HBM,
-        [((4, n, d), F32), ((n, d), BF16)],
-        5,
-    )
-
-
 def body(acts, up_cot, up_weight, error_buf, q_init):
     n_dp = lax.axis_size("dp")
     n_tensor = lax.axis_size("tensor")
@@ -663,12 +658,10 @@
     basis, basis4 = prep(factor, mine, other)
     right_parts, basis4 = lax.optimization_barrier((right_parts, basis4))
 
-    spread_right = spread(right_parts, 1.0 / n_dp)
-    q_chunks = lax.all_to_all(spread_right, "dp", 0, 0)
-    near_keep, from_left, from_right, _ = lax.optimization_barrier((near_keep, from_left, from_right, spread_right))
-    input_grad = close(near_keep, near_got, from_left, from_right)
-    q_chunks, input_grad = lax.optimization_barrier((q_chunks, input_grad))
-    new_error, q_factor = final(q_chunks, basis4, up_cot, acts, error)
+    q_chunks = lax.all_to_all(spread(right_parts, 1.0 / n_dp), "dp", 0, 0)
+    new_error, q_factor, input_grad = final(
+        q_chunks, basis4, up_cot, acts, error, near_keep, near_got, from_left, from_right
+    )
     return (input_grad, new_error[None], basis, q_factor)
 
 

time: 112 us -> 110 us (0.982)
  blocking collectives: 0 us -> 11.6 us
  waiting for transfers between devices: 18.9 us -> 14.7 us
  Pallas kernels: 51.4 us -> 47.5 us
  starting transfers between devices: 32.7 us -> 29 us
  local copies, waits for them, and re-layouts: 6.15 us -> 4.48 us
    all_to_all x0 -> x1, blocking collectives: none -> 11.6 us  [body(): q_chunks = lax.all_to_all(spread(right_parts, 1.0 / n_dp), 'dp', 0, 0)]
    all_to_all x1 -> x0, starting transfers between devices: 3.75 us -> none  [body(): q_chunks = lax.all_to_all(spread_right, 'dp', 0, 0)]
    ppermute x1, waiting for transfers between devices: 3.69 us -> 0.01 us  [body(): from_left = lax.ppermute(plus, 'tensor', right_ring)]
    pallas_call x7 -> x6, Pallas kernels: 40 us -> 37 us  [call(): pl.pallas_call(kernel, in_specs=specs, out_specs=out_specs, out_shape=out...]
    unnamed x14 -> x10, local copies, waits for them, and re-layouts: 6.15 us -> 4.48 us
  transfers between devices with their start and end apart: 12 -> 11, of which waited for: 6 -> 4; matrix products, arithmetic and copies ran while one was open for 0% -> 0% of each run, Pallas kernels for 28% -> 25%
where the time goes in v7:
time: 110 us; the launch traced here: 109 us
  Pallas kernels  47.5 us (43%)
  starting transfers between devices  29 us (26%)
  waiting for transfers between devices  14.7 us (13%)
  blocking collectives  11.6 us (11%)
  local copies, waits for them, and re-layouts  4.48 us (4%)
    pallas_call x6, Pallas kernels, call(): pl.pallas_call(kernel, in_specs=specs, out_specs=out_specs, out_shape=out...  37 us
    all_to_all x1, blocking collectives, body(): q_chunks = lax.all_to_all(spread(right_parts, 1.0 / n_dp), 'dp', 0, 0)  11.6 us
    all_to_all x1, starting transfers between devices, body(): chunks = lax.all_to_all(total, both, 0, 0)  11.2 us
    all_to_all x1, starting transfers between devices, body(): right_parts = lax.all_to_all(right, 'dp', 0, 0)  6.85 us
    all_to_all x1, waiting for transfers between devices, body(): right_parts = lax.all_to_all(right, 'dp', 0, 0)  5.35 us
    all_to_all x1, waiting for transfers between devices, body(): chunks = lax.all_to_all(total, both, 0, 0)  4.9 us
    all_to_all x1, starting transfers between devices, body(): mine = lax.all_to_all(spread_left, both, 0, 0)  4.88 us
    unnamed x10, local copies, waits for them, and re-layouts  4.48 us
  transfers between devices with their start and end apart: 11, of which 4 were waited for; matrix products, arithmetic and copies ran while one was open for 0% of the time, Pallas kernels for 25%

profile of v7, /device:TPU:0, one launch (start us, length us, event | category | flops | bytes accessed | tf_op | source)
XLA Modules:
  0.0 109.1 jit_solution(773927251185034537)
XLA Ops:
  0.6 0.0 copy-start
  0.6 1.2 %copy-done = bf16[512,896]{1,0:T(8,128)(2,1)S(1)} copy-done((bf16[512,896]{1,0:T(8,128)(2,1)S(1)}, bf16[512,896]{1,0:T(8,128)(2,1)}, u32[]{:S(2)}) %copy-start) | copy-done | bytes 917528
  1.8 0.0 copy-start.3
  1.8 0.9 copy-done.3
  2.8 5.5 %shard_map.84 = (f32[128,8,128]{2,1,0:T(8,128)S(1)}, bf16[896,192]{1,0:T(8,128)(2,1)S(1)}, bf16[192,512]{1,0:T(8,128)(2,1)S(1)}, bf16[4,512,896]{2,1,0:T(8,128)(2,1)S(1)}, bf16[4,512,512]{2,1,0:T(8,128)(2,1)S(1)}) custom-call(f32[64,896]{1,0:T(8,128)S(1)} %copy-done.3, bf16[512,896]{1,0:T(8,128)(2,1)S(1)} %copy-done, bf16[512,4096]{1,0:T(8,128)(2,1)} %acts_hbm.5, ...), custom_call_target="tpu_custom_call" | custom-call | flops 1000000 | bytes 100000 | tf_op jit(solution)/shard_map/pallas_call | solution.py:25
  8.3 0.1 collective-permute-start
  8.3 1.9 %shard_map.85 = f32[128,8,128]{2,1,0:T(8,128)S(1)} custom-call(bf16[896,192]{1,0:T(8,128)(2,1)S(1)} %get-tuple-element.45.q3t_ref, bf16[192,512]{1,0:T(8,128)(2,1)S(1)} %get-tuple-element.46.p3_ref, bf16[4,512,896]{2,1,0:T(8,128)(2,1)S(1)} %get-tuple-element.47.error_ref, bf16[4,512,512]{2,1,0:T(8,128)(2,1)S(1)} %get-tuple-element.48.acts_ref), custom_call_target="tpu_custom_call" | custom-call | flops 1000000 | bytes 100000 | tf_op jit(solution)/shard_map/pallas_call | solution.py:171
  10.2 0.0 collective-permute-done
  10.3 0.8 add.3
  11.1 11.2 %all-to-all-start = ((f32[128,8,128]{2,1,0:T(8,128)}), f32[128,8,128]{2,1,0:T(8,128)S(1)}, u32[]{:S(2)}, u32[]{:S(2)}) async-start(f32[128,8,128]{2,1,0:T(8,128)} %add.3), calls=%async_computation | async-start | bytes 1048576 | tf_op jit(solution)/shard_map/all_to_all | solution.py:632
  22.3 8.6 %shard_map.86 = (f32[64,4096]{1,0:T(8,128)}, f32[192,4096]{1,0:T(8,128)}, f32[64,4096]{1,0:T(8,128)}, f32[192,4096]{1,0:T(8,128)}) custom-call(bf16[512,896]{1,0:T(8,128)(2,1)} %cot_hbm.7, bf16[4096,896]{1,0:T(8,128)(2,1)} %weight_hbm), custom_call_target="tpu_custom_call" | custom-call | flops 1000000 | bytes 100000 | tf_op jit(solution)/shard_map/pallas_call | solution.py:25
  31.0 4.9 %all-to-all-done.i = f32[128,8,128]{2,1,0:T(8,128)S(1)} async-done(((f32[128,8,128]{2,1,0:T(8,128)}), f32[128,8,128]{2,1,0:T(8,128)S(1)}, u32[]{:S(2)}, u32[]{:S(2)}) %all-to-all-start) | async-done | bytes 524320 | tf_op jit(solution)/shard_map/all_to_all | solution.py:632
  35.9 0.9 shard_map.87
  36.8 0.0 collective-permute-start.4
  36.8 0.5 collective-permute-start.1
  37.3 4.9 %all-to-all-start.1 = ((f32[128,8,128]{2,1,0:T(8,128)}), f32[128,8,128]{2,1,0:T(8,128)S(1)}, u32[]{:S(2)}, u32[]{:S(2)}) async-start(f32[128,8,128]{2,1,0:T(8,128)} %shard_map.87), calls=%async_computation.1 | async-start | bytes 1048576 | tf_op jit(solution)/shard_map/all_to_all | solution.py:639
  42.2 1.6 %collective-permute-done.1.got_hbm = f32[64,4096]{1,0:T(8,128)S(1)} collective-permute-done((f32[64,4096]{1,0:T(8,128)}, f32[64,4096]{1,0:T(8,128)S(1)}, u32[]{:S(2)}, u32[]{:S(2)}) %collective-permute-start.1) | collective-permute-done | bytes 1048608 | tf_op jit(solution)/shard_map/ppermute | solution.py:641
  43.8 0.0 copy-start.4
  43.8 1.0 copy-done.4
  44.7 2.7 %shard_map.88 = (f32[64,2176]{1,0:T(8,128)}, f32[64,2176]{1,0:T(8,128)}) custom-call(f32[64,4096]{1,0:T(8,128)} %get-tuple-element.51.keep_hbm, f32[64,4096]{1,0:T(8,128)} %copy-done.4), custom_call_target="tpu_custom_call" | custom-call | flops 1000000 | bytes 100000 | tf_op jit(solution)/shard_map/pallas_call | solution.py:25
  47.5 0.0 copy-start.1
  47.5 0.9 collective-permute-start.3
  48.4 1.2 %collective-permute-start.2 = (f32[64,2176]{1,0:T(8,128)}, f32[64,2176]{1,0:T(8,128)S(1)}, u32[]{:S(2)}, u32[]{:S(2)}) collective-permute-start(f32[64,2176]{1,0:T(8,128)} %get-tuple-element.58), channel_id=1, source_target_pairs={{0,2},{1,3},{2,4},{3,5},{4,6},{5,7},{6,0},{7,1},{8,10},{9,11},{10,... | collective-permute-start | bytes 1671176 | tf_op jit(solution)/shard_map/ppermute | solution.py:644
  49.6 0.0 collective-permute-done.4.got_hbm
  49.6 3.3 %shard_map.89 = (f32[64,4096]{1,0:T(8,128)}, f32[64,4096]{1,0:T(8,128)}) custom-call(f32[192,4096]{1,0:T(8,128)} %get-tuple-element.60.keep_hbm, f32[192,4096]{1,0:T(8,128)} %collective-permute-done.4.got_hbm), custom_call_target="tpu_custom_call" | custom-call | flops 1000000 | bytes 100000 | tf_op jit(solution)/shard_map/pallas_call | solution.py:25
  52.9 2.8 %all-to-all-done.1.mine_hbm.mine_ref = f32[128,8,128]{2,1,0:T(8,128)S(1)} async-done(((f32[128,8,128]{2,1,0:T(8,128)}), f32[128,8,128]{2,1,0:T(8,128)S(1)}, u32[]{:S(2)}, u32[]{:S(2)}) %all-to-all-start.1) | async-done | bytes 524320 | tf_op jit(solution)/shard_map/all_to_all | solution.py:639
  55.7 0.0 collective-permute-start.5
  55.7 0.0 copy-done.1
  55.7 5.0 %shard_map.90 = (f32[64,64]{1,0:T(8,128)S(1)}, f32[64,896]{1,0:T(8,128)S(1)}, f32[64,512]{1,0:T(8,128)S(1)}, bf16[512,896]{1,0:T(8,128)(2,1)S(1)}, bf16[1,2048,8...) custom-call(f32[128,8,128]{2,1,0:T(8,128)S(1)} %all-to-all-done.1.mine_hbm.mine_ref, ...), custom_call_target="tpu_custom_call" | custom-call | flops 1000000 | bytes 100000 | tf_op jit(solution)/shard_map/pallas_call | solution.py:25
  60.7 0.0 collective-permute-done.5.other_ref
  60.7 3.7 %shard_map.91 = (f32[64,64]{1,0:T(8,128)S(1)}, f32[16,32,128]{2,1,0:T(8,128)}) custom-call(f32[128,8,128]{2,1,0:T(8,128)S(1)} %collective-permute-done.5.other_ref, f32[64,64]{1,0:T(8,128)S(1)} %get-tuple-element.64.gram_ref, f32[64,896]{1,0:T(8,128)S(1)} %get-tuple-element.65.with_error_ref, f32[64,512]{1,0:T(8,128)S(1)} %get-tuple-element.66.with_acts_ref, ...), custom_call_target="tpu_custom_call" | custom-call | flops 1000000 | bytes 100000 | tf_op jit(solution)/shard_map/pallas_call | solution.py:329
  64.4 0.0 collective-permute-done.3.high_ref
  64.4 0.0 collective-permute-done.2.low_ref
  64.4 2.1 %shard_map.94 = (f32[64,4096]{1,0:T(8,128)}, f32[64,4096]{1,0:T(8,128)}) custom-call(f32[64,4096]{1,0:T(8,128)} %get-tuple-element.76.plus_hbm, f32[64,4096]{1,0:T(8,128)} %get-tuple-element.77.minus_hbm, f32[64,2176]{1,0:T(8,128)S(1)} %collective-permute-done.2.low_ref, ...), custom_call_target="tpu_custom_call", output_to_operand_aliasing={{0}: (0, {}), {1}: (1, {})} | custom-call | flops 1000000 | bytes 100000 | tf_op jit(solution)/shard_map/pallas_call | solution.py:605
  66.5 1.0 collective-permute-start.6
  67.5 2.3 %collective-permute-start.7 = (f32[64,4096]{1,0:T(8,128)}, f32[64,4096]{1,0:T(8,128)}, u32[]{:S(2)}, u32[]{:S(2)}) collective-permute-start(f32[64,4096]{1,0:T(8,128)} %get-tuple-element.81), channel_id=1, source_target_pairs={{0,6},{1,7},{2,0},{3,1},{4,2},{5,3},{6,4},{7,5},{8,14},{9,15},{10,... | collective-permute-start | bytes 3145736 | tf_op jit(solution)/shard_map/ppermute | solution.py:656
  69.8 6.8 %all-to-all-start.2 = ((f32[16,32,128]{2,1,0:T(8,128)}), f32[16,32,128]{2,1,0:T(8,128)S(1)}, u32[]{:S(2)}, u32[]{:S(2)}) async-start(f32[16,32,128]{2,1,0:T(8,128)} %get-tuple-element.71), calls=%async_computation.2 | async-start | bytes 524288 | tf_op jit(solution)/shard_map/all_to_all | solution.py:657
  76.7 2.0 %shard_map.92 = (f32[64,4096]{1,0:T(8,128)}, bf16[4096,256]{1,0:T(8,128)(2,1)S(1)}) custom-call(f32[64,64]{1,0:T(8,128)S(1)} %get-tuple-element.72.factor_ref, f32[128,8,128]{2,1,0:T(8,128)S(1)} %all-to-all-done.1.mine_hbm.mine_ref, f32[128,8,128]{2,1,0:T(8,128)S(1)} %collective-permute-done.5.other_ref), custom_call_target="tpu_custom_call" | custom-call | flops 1000000 | bytes 100000 | tf_op jit(solution)/shard_map/pallas_call | solution.py:355
  78.6 0.0 copy-start.2
  78.6 1.4 %copy-done.2 = bf16[4096,256]{1,0:T(8,128)(2,1)} copy-done((bf16[4096,256]{1,0:T(8,128)(2,1)}, bf16[4096,256]{1,0:T(8,128)(2,1)S(1)}, u32[]{:S(2)}) %copy-start.2) | copy-done | bytes 2097176
  80.0 5.3 %all-to-all-done.2.i = f32[16,32,128]{2,1,0:T(8,128)S(1)} async-done(((f32[16,32,128]{2,1,0:T(8,128)}), f32[16,32,128]{2,1,0:T(8,128)S(1)}, u32[]{:S(2)}, u32[]{:S(2)}) %all-to-all-start.2) | async-done | bytes 262176 | tf_op jit(solution)/shard_map/all_to_all | solution.py:657
  85.4 11.6 %all_to_all.20.chunks_hbm = f32[16,32,128]{2,1,0:T(8,128)S(1)} all-to-all(f32[16,32,128]{2,1,0:T(8,128)S(1)} %shard_map.93), channel_id=1, replica_groups=mesh['dp'=16,'tensor'=8] {'dp'}, dimensions={0} | all-to-all | bytes 524288 | tf_op jit(solution)/shard_map/all_to_all | solution.py:661
  97.0 0.0 collective-permute-done.6.left_hbm
  97.0 0.0 collective-permute-done.7.right_hbm
  97.0 11.9 %shard_map.95 = (bf16[4096,896]{1,0:T(8,128)(2,1)}, f32[64,896]{1,0:T(8,128)}, bf16[64,4096]{1,0:T(8,128)(2,1)}) custom-call(f32[16,32,128]{2,1,0:T(8,128)S(1)} %all_to_all.20.chunks_hbm, bf16[4096,256]{1,0:T(8,128)(2,1)} %copy-done.2, bf16[512,896]{1,0:T(8,128)(2,1)S(1)} %copy-done.1, bf16[512,4096]{1,0:T(8,128)(2,1)} %acts_hbm.5, ...), custom_call_target="tpu_custom_call" | custom-call | flops 1000000 | bytes 100000 | tf_op jit(solution)/shard_map/pallas_call | solution.py:25
  (1 shorter events, 0.0 us)
Async XLA Ops:
  0.6 1.2 %copy-start = (bf16[512,896]{1,0:T(8,128)(2,1)S(1)}, bf16[512,896]{1,0:T(8,128)(2,1)}, u32[]{:S(2)}) copy-start(bf16[512,896]{1,0:T(8,128)(2,1)} %cot_hbm.7) | copy-start | bytes 2752516
  1.8 0.9 copy-start.3
  8.3 2.0 %collective-permute-start = (f32[128,8,128]{2,1,0:T(8,128)S(1)}, f32[128,8,128]{2,1,0:T(8,128)S(1)}, u32[]{:S(2)}, u32[]{:S(2)}) collective-permute-start(f32[128,8,128]{2,1,0:T(8,128)S(1)} %get-tuple-element.49), channel_id=1, source_target_pairs={{0,1},{1,0},{2,3},{3,2},{4,5},{5,4},{6,7},{7,6},{8,9},{9,8},{10,11... | collective-permute-start | bytes 1572872 | tf_op jit(solution)/shard_map/ppermute | solution.py:630
  11.1 24.8 %all-to-all-start = ((f32[128,8,128]{2,1,0:T(8,128)}), f32[128,8,128]{2,1,0:T(8,128)S(1)}, u32[]{:S(2)}, u32[]{:S(2)}) async-start(f32[128,8,128]{2,1,0:T(8,128)} %add.3), calls=%async_computation | async-start | bytes 1048576 | tf_op jit(solution)/shard_map/all_to_all | solution.py:632
  36.8 12.8 %collective-permute-start.4 = (f32[192,4096]{1,0:T(8,128)}, f32[192,4096]{1,0:T(8,128)}, u32[]{:S(2)}, u32[]{:S(2)}) collective-permute-start(f32[192,4096]{1,0:T(8,128)} %get-tuple-element.61), channel_id=1, source_target_pairs={{0,1},{1,0},{2,3},{3,2},{4,5},{5,4},{6,7},{7,6},{8,9},{9,8},{10,11... | collective-permute-start | bytes 9437192 | tf_op jit(solution)/shard_map/ppermute | solution.py:642
  36.8 7.0 %collective-permute-start.1 = (f32[64,4096]{1,0:T(8,128)}, f32[64,4096]{1,0:T(8,128)S(1)}, u32[]{:S(2)}, u32[]{:S(2)}) collective-permute-start(f32[64,4096]{1,0:T(8,128)} %get-tuple-element.57), channel_id=1, source_target_pairs={{0,1},{1,0},{2,3},{3,2},{4,5},{5,4},{6,7},{7,6},{8,9},{9,8},{10,11... | collective-permute-start | bytes 3145736 | tf_op jit(solution)/shard_map/ppermute | solution.py:641
  37.3 18.4 %all-to-all-start.1 = ((f32[128,8,128]{2,1,0:T(8,128)}), f32[128,8,128]{2,1,0:T(8,128)S(1)}, u32[]{:S(2)}, u32[]{:S(2)}) async-start(f32[128,8,128]{2,1,0:T(8,128)} %shard_map.87), calls=%async_computation.1 | async-start | bytes 1048576 | tf_op jit(solution)/shard_map/all_to_all | solution.py:639
  43.8 1.0 copy-start.4
  47.5 8.2 %copy-start.1 = (bf16[512,896]{1,0:T(8,128)(2,1)S(1)}, bf16[512,896]{1,0:T(8,128)(2,1)}, u32[]{:S(2)}) copy-start(bf16[512,896]{1,0:T(8,128)(2,1)} %cot_hbm.7) | copy-start | bytes 2752516
  47.5 16.9 %collective-permute-start.3 = (f32[64,2176]{1,0:T(8,128)}, f32[64,2176]{1,0:T(8,128)S(1)}, u32[]{:S(2)}, u32[]{:S(2)}) collective-permute-start(f32[64,2176]{1,0:T(8,128)} %get-tuple-element.59), channel_id=1, source_target_pairs={{0,6},{1,7},{2,0},{3,1},{4,2},{5,3},{6,4},{7,5},{8,14},{9,15},{10,... | collective-permute-start | bytes 1671176 | tf_op jit(solution)/shard_map/ppermute | solution.py:645
  48.4 16.0 %collective-permute-start.2 = (f32[64,2176]{1,0:T(8,128)}, f32[64,2176]{1,0:T(8,128)S(1)}, u32[]{:S(2)}, u32[]{:S(2)}) collective-permute-start(f32[64,2176]{1,0:T(8,128)} %get-tuple-element.58), channel_id=1, source_target_pairs={{0,2},{1,3},{2,4},{3,5},{4,6},{5,7},{6,0},{7,1},{8,10},{9,11},{10,... | collective-permute-start | bytes 1671176 | tf_op jit(solution)/shard_map/ppermute | solution.py:644
  55.7 5.0 %collective-permute-start.5 = (f32[128,8,128]{2,1,0:T(8,128)S(1)}, f32[128,8,128]{2,1,0:T(8,128)S(1)}, u32[]{:S(2)}, u32[]{:S(2)}) collective-permute-start(f32[128,8,128]{2,1,0:T(8,128)S(1)} %all-to-all-done.1.mine_hbm.mine_ref), channel_id=1, source_target_pairs={{0,1},{1,0},{2,3},{3,2},{4,5},{5,4},{6,7},{7,6},{8,9},{9,8},{10,11... | collective-permute-start | bytes 1572872 | tf_op jit(solution)/shard_map/ppermute | solution.py:649
  66.5 30.5 %collective-permute-start.6 = (f32[64,4096]{1,0:T(8,128)}, f32[64,4096]{1,0:T(8,128)}, u32[]{:S(2)}, u32[]{:S(2)}) collective-permute-start(f32[64,4096]{1,0:T(8,128)} %get-tuple-element.80), channel_id=1, source_target_pairs={{0,2},{1,3},{2,4},{3,5},{4,6},{5,7},{6,0},{7,1},{8,10},{9,11},{10,... | collective-permute-start | bytes 3145736 | tf_op jit(solution)/shard_map/ppermute | solution.py:655
  67.5 29.5 %collective-permute-start.7 = (f32[64,4096]{1,0:T(8,128)}, f32[64,4096]{1,0:T(8,128)}, u32[]{:S(2)}, u32[]{:S(2)}) collective-permute-start(f32[64,4096]{1,0:T(8,128)} %get-tuple-element.81), channel_id=1, source_target_pairs={{0,6},{1,7},{2,0},{3,1},{4,2},{5,3},{6,4},{7,5},{8,14},{9,15},{10,... | collective-permute-start | bytes 3145736 | tf_op jit(solution)/shard_map/ppermute | solution.py:656
  69.8 15.5 %all-to-all-start.2 = ((f32[16,32,128]{2,1,0:T(8,128)}), f32[16,32,128]{2,1,0:T(8,128)S(1)}, u32[]{:S(2)}, u32[]{:S(2)}) async-start(f32[16,32,128]{2,1,0:T(8,128)} %get-tuple-element.71), calls=%async_computation.2 | async-start | bytes 524288 | tf_op jit(solution)/shard_map/all_to_all | solution.py:657
  78.6 1.4 %copy-start.2 = (bf16[4096,256]{1,0:T(8,128)(2,1)}, bf16[4096,256]{1,0:T(8,128)(2,1)S(1)}, u32[]{:S(2)}) copy-start(bf16[4096,256]{1,0:T(8,128)(2,1)S(1)} %get-tuple-element.75.basis_hbm) | copy-start | bytes 6291460

commit v8 on v7

--- a/solution.py
+++ b/solution.py
@@ -308,11 +308,48 @@
 
 
 def second_kernel(
-    other_ref, gram_ref, with_error_ref, with_acts_ref, cot_ref, error_ref, acts_ref, factor_ref, right_ref
+    other_ref,
+    gram_ref,
+    with_error_ref,
+    with_acts_ref,
+    cot_ref,
+    error_ref,
+    acts_ref,
+    low_hbm,
+    high_hbm,
+    plus_hbm,
+    minus_hbm,
+    factor_ref,
+    right_ref,
+    plus_out,
+    minus_out,
+    half_ref,
+    relay_ref,
+    sems,
 ):
+    copies = Copies(sems)
+    w = half_ref.shape[2]
+    wide = low_hbm.shape[1]
+    relays = (
+        (plus_hbm, plus_out, low_hbm, slice(0, w), slice(0, w)),
+        (minus_hbm, minus_out, high_hbm, slice(w, 2 * w), slice(wide - w, wide)),
+    )
+    loads = [
+        (copies.start(src.at[:, at], half_ref.at[i]), copies.start(relay, relay_ref.at[i]))
+        for i, (src, _, relay, at, _) in enumerate(relays)
+    ]
+
     gram, with_error, with_acts = half_terms(half_of(other_ref), error_ref, acts_ref)
     factor = inverse_factor(gram + gram_ref[...])
     factor_ref[...] = factor
+
+    stores = []
+    for i, (_, out, _, at, far) in enumerate(relays):
+        for copy in loads[i]:
+            copy.wait()
+        half_ref[i] += relay_ref[i, :, far]
+        stores.append(copies.start(half_ref.at[i], out.at[:, at]))
+
     with_acts = with_acts + with_acts_ref[...]
     merged_term = (with_error + with_error_ref[...]) + sum3(dot(split3(with_acts), cot_ref[...]))
     right = dot_highest(factor, merged_term)
@@ -323,17 +360,26 @@
             right_ref[v // 4, 8 * (v % 4) : 8 * (v % 4) + 8] = right[8 * g : 8 * g + 8, LANES * j : LANES * (j + 1)]
     for v in range(8 * tiles, 64):
         right_ref[v // 4, 8 * (v % 4) : 8 * (v % 4) + 8] = jnp.zeros((8, LANES), F32)
-
-
-def second(other, terms):
+    for store in stores:
+        store.wait()
+
+
+def second(other, terms, low, high, plus, minus):
+    n, d = plus.shape
     return pl.pallas_call(
         second_kernel,
-        in_specs=[VMEM] * 7,
-        out_specs=[VMEM, VMEM],
-        out_shape=[shape((RANK, RANK)), shape((16, 32, LANES))],
+        in_specs=[VMEM] * 7 + [HBM] * 4,
+        out_specs=[VMEM, VMEM, HBM, HBM],
+        out_shape=[shape((RANK, RANK)), shape((16, 32, LANES)), shape((n, d)), shape((n, d))],
+        input_output_aliases={9: 2, 10: 3},
+        scratch_shapes=[
+            pltpu.VMEM((2, n, d // 2), F32),
+            pltpu.VMEM((2,) + low.shape, F32),
+            pltpu.SemaphoreType.DMA((6,)),
+        ],
         compiler_params=pltpu.CompilerParams(vmem_limit_bytes=12 << 20),
         cost_estimate=pl.CostEstimate(flops=10**6, bytes_accessed=10**5, transcendentals=0),
-    )(other, *terms)
+    )(other, *terms, low, high, plus, minus)
 
 
 def prep_kernel(factor_ref, mine_ref, other_ref, basis_ref, out_ref):
@@ -581,42 +627,6 @@
     )
 
 
-def relay_kernel(plus_hbm, minus_hbm, low_ref, high_ref, plus_out, minus_out, half_ref, sems):
-    copies = Copies(sems)
-    d = plus_hbm.shape[1]
-    w = d // 2
-    wide = low_ref.shape[1]
-    parts = (
-        (plus_hbm, plus_out, low_ref, slice(0, w), slice(0, w)),
-        (minus_hbm, minus_out, high_ref, slice(w, d), slice(wide - w, wide)),
-    )
-    loads = [copies.start(src.at[:, at], half_ref.at[i]) for i, (src, _, _, at, _) in enumerate(parts)]
-    stores = []
-    for i, (_, out, relay, at, far) in enumerate(parts):
-        loads[i].wait()
-        half_ref[i] += relay[:, far]
-        stores.append(copies.start(half_ref.at[i], out.at[:, at]))
-    for store in stores:
-        store.wait()
-
-
-def relay_sums(plus, minus, low, high):
-    n, d = plus.shape
-    return pl.pallas_call(
-        relay_kernel,
-        in_specs=[HBM] * 2 + [VMEM] * 2,
-        out_specs=[HBM] * 2,
-        out_shape=[shape((n, d))] * 2,
-        input_output_aliases={0: 0, 1: 1},
-        scratch_shapes=[
-            pltpu.VMEM((2, n, d // 2), F32),
-            pltpu.SemaphoreType.DMA((4,)),
-        ],
-        compiler_params=pltpu.CompilerParams(vmem_limit_bytes=52 << 20),
-        cost_estimate=pl.CostEstimate(flops=10**6, bytes_accessed=10**5, transcendentals=0),
-    )(plus, minus, low, high)
-
-
 def body(acts, up_cot, up_weight, error_buf, q_init):
     n_dp = lax.axis_size("dp")
     n_tensor = lax.axis_size("tensor")
@@ -648,10 +658,7 @@
 
     other = lax.ppermute(mine, "tensor", pairs)
     terms = first(mine, up_cot, acts, error)
-    factor, right = second(other, terms)
-
-    low_relay, high_relay, right = lax.optimization_barrier((low_relay, high_relay, right))
-    plus, minus = relay_sums(plus, minus, low_relay, high_relay)
+    factor, right, plus, minus = second(other, terms, low_relay, high_relay, plus, minus)
     from_left = lax.ppermute(plus, "tensor", right_ring)
     from_right = lax.ppermute(minus, "tensor", left_ring)
     right_parts = lax.all_to_all(right, "dp", 0, 0)

time: 110 us -> 113 us (1.027)
  waiting for transfers between devices: 14.7 us -> 18.4 us
    ppermute x1, waiting for transfers between devices: 0.01 us -> 2.01 us  [body(): high_relay = lax.ppermute(far_high, 'tensor', left_ring)]
    ppermute x1, waiting for transfers between devices: 0.01 us -> 1.76 us  [body(): low_relay = lax.ppermute(far_low, 'tensor', right_ring)]
    pallas_call x2 -> x1, Pallas kernels: 5.83 us -> 5.92 us  [second(): pl.pallas_call(second_kernel, in_specs=[VMEM] * 7 + [HBM] * 4, out_specs=...]
    unnamed x10 -> x12, local copies, waits for them, and re-layouts: 4.48 us -> 4.48 us
  transfers between devices with their start and end apart: 11 -> 11, of which waited for: 4 -> 6; matrix products, arithmetic and copies ran while one was open for 0% -> 0% of each run, Pallas kernels for 25% -> 21%
where the time goes in v8:
time: 113 us
  Pallas kernels  47.7 us (42%)
  starting transfers between devices  29 us (26%)
  waiting for transfers between devices  18.4 us (16%)
  blocking collectives  11.6 us (10%)
  local copies, waits for them, and re-layouts  4.48 us (4%)
    pallas_call x6, Pallas kernels, call(): pl.pallas_call(kernel, in_specs=specs, out_specs=out_specs, out_shape=out...  37 us
    all_to_all x1, blocking collectives, body(): q_chunks = lax.all_to_all(spread(right_parts, 1.0 / n_dp), 'dp', 0, 0)  11.6 us
    all_to_all x1, starting transfers between devices, body(): chunks = lax.all_to_all(total, both, 0, 0)  11.2 us
    all_to_all x1, starting transfers between devices, body(): right_parts = lax.all_to_all(right, 'dp', 0, 0)  6.86 us
    pallas_call x1, Pallas kernels, second(): pl.pallas_call(second_kernel, in_specs=[VMEM] * 7 + [HBM] * 4, out_specs=...  5.92 us
    all_to_all x1, waiting for transfers between devices, body(): right_parts = lax.all_to_all(right, 'dp', 0, 0)  5.35 us
    all_to_all x1, waiting for transfers between devices, body(): chunks = lax.all_to_all(total, both, 0, 0)  4.9 us
    all_to_all x1, starting transfers between devices, body(): mine = lax.all_to_all(spread_left, both, 0, 0)  4.88 us
  transfers between devices with their start and end apart: 11, of which 6 were waited for; matrix products, arithmetic and copies ran while one was open for 0% of the time, Pallas kernels for 21%

profile of v8, /device:TPU:0, one launch (start us, length us, event | category | flops | bytes accessed | tf_op | source)
XLA Modules:
  0.0 113.0 jit_solution(11984069765729083723)
XLA Ops:
  0.6 0.0 copy-start
  0.6 1.2 %copy-done = bf16[512,896]{1,0:T(8,128)(2,1)S(1)} copy-done((bf16[512,896]{1,0:T(8,128)(2,1)S(1)}, bf16[512,896]{1,0:T(8,128)(2,1)}, u32[]{:S(2)}) %copy-start) | copy-done | bytes 917528
  1.8 0.0 copy-start.4
  1.8 0.9 copy-done.4
  2.8 5.5 %shard_map.84 = (f32[128,8,128]{2,1,0:T(8,128)S(1)}, bf16[896,192]{1,0:T(8,128)(2,1)S(1)}, bf16[192,512]{1,0:T(8,128)(2,1)S(1)}, bf16[4,512,896]{2,1,0:T(8,128)(2,1)S(1)}, bf16[4,512,512]{2,1,0:T(8,128)(2,1)S(1)}) custom-call(f32[64,896]{1,0:T(8,128)S(1)} %copy-done.4, bf16[512,896]{1,0:T(8,128)(2,1)S(1)} %copy-done, bf16[512,4096]{1,0:T(8,128)(2,1)} %acts_hbm.5, ...), custom_call_target="tpu_custom_call" | custom-call | flops 1000000 | bytes 100000 | tf_op jit(solution)/shard_map/pallas_call | solution.py:25
  8.3 0.1 collective-permute-start
  8.3 1.9 %shard_map.85 = f32[128,8,128]{2,1,0:T(8,128)S(1)} custom-call(bf16[896,192]{1,0:T(8,128)(2,1)S(1)} %get-tuple-element.42.q3t_ref, bf16[192,512]{1,0:T(8,128)(2,1)S(1)} %get-tuple-element.43.p3_ref, bf16[4,512,896]{2,1,0:T(8,128)(2,1)S(1)} %get-tuple-element.44.error_ref, bf16[4,512,512]{2,1,0:T(8,128)(2,1)S(1)} %get-tuple-element.45.acts_ref), custom_call_target="tpu_custom_call" | custom-call | flops 1000000 | bytes 100000 | tf_op jit(solution)/shard_map/pallas_call | solution.py:171
  10.2 0.0 collective-permute-done
  10.3 0.8 add.3
  11.1 11.2 %all-to-all-start = ((f32[128,8,128]{2,1,0:T(8,128)}), f32[128,8,128]{2,1,0:T(8,128)S(1)}, u32[]{:S(2)}, u32[]{:S(2)}) async-start(f32[128,8,128]{2,1,0:T(8,128)} %add.3), calls=%async_computation | async-start | bytes 1048576 | tf_op jit(solution)/shard_map/all_to_all | solution.py:642
  22.3 8.6 %shard_map.86 = (f32[64,4096]{1,0:T(8,128)}, f32[192,4096]{1,0:T(8,128)}, f32[64,4096]{1,0:T(8,128)}, f32[192,4096]{1,0:T(8,128)}) custom-call(bf16[512,896]{1,0:T(8,128)(2,1)} %cot_hbm.7, bf16[4096,896]{1,0:T(8,128)(2,1)} %weight_hbm), custom_call_target="tpu_custom_call" | custom-call | flops 1000000 | bytes 100000 | tf_op jit(solution)/shard_map/pallas_call | solution.py:25
  31.0 4.9 %all-to-all-done.i = f32[128,8,128]{2,1,0:T(8,128)S(1)} async-done(((f32[128,8,128]{2,1,0:T(8,128)}), f32[128,8,128]{2,1,0:T(8,128)S(1)}, u32[]{:S(2)}, u32[]{:S(2)}) %all-to-all-start) | async-done | bytes 524320 | tf_op jit(solution)/shard_map/all_to_all | solution.py:642
  35.9 0.9 shard_map.87
  36.8 0.0 collective-permute-start.2
  36.8 0.5 collective-permute-start.1
  37.3 4.9 %all-to-all-start.1 = ((f32[128,8,128]{2,1,0:T(8,128)}), f32[128,8,128]{2,1,0:T(8,128)S(1)}, u32[]{:S(2)}, u32[]{:S(2)}) async-start(f32[128,8,128]{2,1,0:T(8,128)} %shard_map.87), calls=%async_computation.1 | async-start | bytes 1048576 | tf_op jit(solution)/shard_map/all_to_all | solution.py:649
  42.2 1.6 %collective-permute-done.1.got_hbm = f32[64,4096]{1,0:T(8,128)S(1)} collective-permute-done((f32[64,4096]{1,0:T(8,128)}, f32[64,4096]{1,0:T(8,128)S(1)}, u32[]{:S(2)}, u32[]{:S(2)}) %collective-permute-start.1) | collective-permute-done | bytes 1048608 | tf_op jit(solution)/shard_map/ppermute | solution.py:651
  43.8 0.0 copy-start.5
  43.8 1.0 copy-done.5
  44.7 2.7 %shard_map.88 = (f32[64,2176]{1,0:T(8,128)}, f32[64,2176]{1,0:T(8,128)}) custom-call(f32[64,4096]{1,0:T(8,128)} %get-tuple-element.51.keep_hbm, f32[64,4096]{1,0:T(8,128)} %copy-done.5), custom_call_target="tpu_custom_call" | custom-call | flops 1000000 | bytes 100000 | tf_op jit(solution)/shard_map/pallas_call | solution.py:25
  47.5 0.0 copy-start.1
  47.5 0.9 collective-permute-start.5
  48.4 1.2 %collective-permute-start.4 = (f32[64,2176]{1,0:T(8,128)}, f32[64,2176]{1,0:T(8,128)}, u32[]{:S(2)}, u32[]{:S(2)}) collective-permute-start(f32[64,2176]{1,0:T(8,128)} %get-tuple-element.55), channel_id=1, source_target_pairs={{0,2},{1,3},{2,4},{3,5},{4,6},{5,7},{6,0},{7,1},{8,10},{9,11},{10,... | collective-permute-start | bytes 1671176 | tf_op jit(solution)/shard_map/ppermute | solution.py:654
  49.6 0.0 collective-permute-done.2.got_hbm
  49.6 3.3 %shard_map.89 = (f32[64,4096]{1,0:T(8,128)}, f32[64,4096]{1,0:T(8,128)}) custom-call(f32[192,4096]{1,0:T(8,128)} %get-tuple-element.56.keep_hbm, f32[192,4096]{1,0:T(8,128)} %collective-permute-done.2.got_hbm), custom_call_target="tpu_custom_call" | custom-call | flops 1000000 | bytes 100000 | tf_op jit(solution)/shard_map/pallas_call | solution.py:25
  52.9 2.8 %all-to-all-done.1.mine_hbm.mine_ref = f32[128,8,128]{2,1,0:T(8,128)S(1)} async-done(((f32[128,8,128]{2,1,0:T(8,128)}), f32[128,8,128]{2,1,0:T(8,128)S(1)}, u32[]{:S(2)}, u32[]{:S(2)}) %all-to-all-start.1) | async-done | bytes 524320 | tf_op jit(solution)/shard_map/all_to_all | solution.py:649
  55.7 0.0 copy-start.3
  55.7 0.0 collective-permute-start.3
  55.7 0.0 copy-done.1
  55.7 5.0 %shard_map.90 = (f32[64,64]{1,0:T(8,128)S(1)}, f32[64,896]{1,0:T(8,128)S(1)}, f32[64,512]{1,0:T(8,128)S(1)}, bf16[512,896]{1,0:T(8,128)(2,1)S(1)}, bf16[1,2048,8...) custom-call(f32[128,8,128]{2,1,0:T(8,128)S(1)} %all-to-all-done.1.mine_hbm.mine_ref, ...), custom_call_target="tpu_custom_call" | custom-call | flops 1000000 | bytes 100000 | tf_op jit(solution)/shard_map/pallas_call | solution.py:25
  60.8 2.0 %collective-permute-done.5.high_hbm = f32[64,2176]{1,0:T(8,128)} collective-permute-done((f32[64,2176]{1,0:T(8,128)}, f32[64,2176]{1,0:T(8,128)}, u32[]{:S(2)}, u32[]{:S(2)}) %collective-permute-start.5) | collective-permute-done | bytes 557088 | tf_op jit(solution)/shard_map/ppermute | solution.py:655
  62.8 1.8 %collective-permute-done.4.low_hbm = f32[64,2176]{1,0:T(8,128)} collective-permute-done((f32[64,2176]{1,0:T(8,128)}, f32[64,2176]{1,0:T(8,128)}, u32[]{:S(2)}, u32[]{:S(2)}) %collective-permute-start.4) | collective-permute-done | bytes 557088 | tf_op jit(solution)/shard_map/ppermute | solution.py:654
  64.5 0.0 collective-permute-done.3.other_ref
  64.5 0.0 copy-done.3
  64.5 5.9 %shard_map.91 = (f32[64,64]{1,0:T(8,128)S(1)}, f32[16,32,128]{2,1,0:T(8,128)}, f32[64,4096]{1,0:T(8,128)S(1)}, f32[64,4096]{1,0:T(8,128)}) custom-call(f32[128,8,128]{2,1,0:T(8,128)S(1)} %collective-permute-done.3.other_ref, f32[64,64]{1,0:T(8,128)S(1)} %get-tuple-element.60.gram_ref, ...), custom_call_target="tpu_custom_call", output_to_operand_aliasing={{2}: (9, {}), {3}: (10, {})} | custom-call | flops 1000000 | bytes 100000 | tf_op jit(solution)/shard_map/pallas_call | solution.py:369
  70.4 0.1 collective-permute-start.6
  70.5 3.2 %collective-permute-start.7 = (f32[64,4096]{1,0:T(8,128)}, f32[64,4096]{1,0:T(8,128)}, u32[]{:S(2)}, u32[]{:S(2)}) collective-permute-start(f32[64,4096]{1,0:T(8,128)} %get-tuple-element.75), channel_id=1, source_target_pairs={{0,6},{1,7},{2,0},{3,1},{4,2},{5,3},{6,4},{7,5},{8,14},{9,15},{10,... | collective-permute-start | bytes 3145736 | tf_op jit(solution)/shard_map/ppermute | solution.py:663
  73.8 6.9 %all-to-all-start.2 = ((f32[16,32,128]{2,1,0:T(8,128)}), f32[16,32,128]{2,1,0:T(8,128)S(1)}, u32[]{:S(2)}, u32[]{:S(2)}) async-start(f32[16,32,128]{2,1,0:T(8,128)} %get-tuple-element.69), calls=%async_computation.2 | async-start | bytes 524288 | tf_op jit(solution)/shard_map/all_to_all | solution.py:664
  80.6 2.0 %shard_map.92 = (f32[64,4096]{1,0:T(8,128)}, bf16[4096,256]{1,0:T(8,128)(2,1)S(1)}) custom-call(f32[64,64]{1,0:T(8,128)S(1)} %get-tuple-element.70.factor_ref, f32[128,8,128]{2,1,0:T(8,128)S(1)} %all-to-all-done.1.mine_hbm.mine_ref, f32[128,8,128]{2,1,0:T(8,128)S(1)} %collective-permute-done.3.other_ref), custom_call_target="tpu_custom_call" | custom-call | flops 1000000 | bytes 100000 | tf_op jit(solution)/shard_map/pallas_call | solution.py:401
  82.6 0.0 copy-start.2
  82.6 1.4 %copy-done.2 = bf16[4096,256]{1,0:T(8,128)(2,1)} copy-done((bf16[4096,256]{1,0:T(8,128)(2,1)}, bf16[4096,256]{1,0:T(8,128)(2,1)S(1)}, u32[]{:S(2)}) %copy-start.2) | copy-done | bytes 2097176
  84.0 5.3 %all-to-all-done.2.i = f32[16,32,128]{2,1,0:T(8,128)S(1)} async-done(((f32[16,32,128]{2,1,0:T(8,128)}), f32[16,32,128]{2,1,0:T(8,128)S(1)}, u32[]{:S(2)}, u32[]{:S(2)}) %all-to-all-start.2) | async-done | bytes 262176 | tf_op jit(solution)/shard_map/all_to_all | solution.py:664
  89.3 11.6 %all_to_all.20.chunks_hbm = f32[16,32,128]{2,1,0:T(8,128)S(1)} all-to-all(f32[16,32,128]{2,1,0:T(8,128)S(1)} %shard_map.93), channel_id=1, replica_groups=mesh['dp'=16,'tensor'=8] {'dp'}, dimensions={0} | all-to-all | bytes 524288 | tf_op jit(solution)/shard_map/all_to_all | solution.py:668
  100.9 0.0 collective-permute-done.6.left_hbm
  100.9 0.0 collective-permute-done.7.right_hbm
  100.9 11.9 %shard_map.94 = (bf16[4096,896]{1,0:T(8,128)(2,1)}, f32[64,896]{1,0:T(8,128)}, bf16[64,4096]{1,0:T(8,128)(2,1)}) custom-call(f32[16,32,128]{2,1,0:T(8,128)S(1)} %all_to_all.20.chunks_hbm, bf16[4096,256]{1,0:T(8,128)(2,1)} %copy-done.2, bf16[512,896]{1,0:T(8,128)(2,1)S(1)} %copy-done.1, bf16[512,4096]{1,0:T(8,128)(2,1)} %acts_hbm.5, ...), custom_call_target="tpu_custom_call" | custom-call | flops 1000000 | bytes 100000 | tf_op jit(solution)/shard_map/pallas_call | solution.py:25
  (1 shorter events, 0.0 us)
Async XLA Ops:
  0.6 1.2 %copy-start = (bf16[512,896]{1,0:T(8,128)(2,1)S(1)}, bf16[512,896]{1,0:T(8,128)(2,1)}, u32[]{:S(2)}) copy-start(bf16[512,896]{1,0:T(8,128)(2,1)} %cot_hbm.7) | copy-start | bytes 2752516
  1.8 0.9 copy-start.4
  8.3 2.0 %collective-permute-start = (f32[128,8,128]{2,1,0:T(8,128)S(1)}, f32[128,8,128]{2,1,0:T(8,128)S(1)}, u32[]{:S(2)}, u32[]{:S(2)}) collective-permute-start(f32[128,8,128]{2,1,0:T(8,128)S(1)} %get-tuple-element.46), channel_id=1, source_target_pairs={{0,1},{1,0},{2,3},{3,2},{4,5},{5,4},{6,7},{7,6},{8,9},{9,8},{10,11... | collective-permute-start | bytes 1572872 | tf_op jit(solution)/shard_map/ppermute | solution.py:640
  11.1 24.8 %all-to-all-start = ((f32[128,8,128]{2,1,0:T(8,128)}), f32[128,8,128]{2,1,0:T(8,128)S(1)}, u32[]{:S(2)}, u32[]{:S(2)}) async-start(f32[128,8,128]{2,1,0:T(8,128)} %add.3), calls=%async_computation | async-start | bytes 1048576 | tf_op jit(solution)/shard_map/all_to_all | solution.py:642
  36.8 12.8 %collective-permute-start.2 = (f32[192,4096]{1,0:T(8,128)}, f32[192,4096]{1,0:T(8,128)}, u32[]{:S(2)}, u32[]{:S(2)}) collective-permute-start(f32[192,4096]{1,0:T(8,128)} %get-tuple-element.57), channel_id=1, source_target_pairs={{0,1},{1,0},{2,3},{3,2},{4,5},{5,4},{6,7},{7,6},{8,9},{9,8},{10,11... | collective-permute-start | bytes 9437192 | tf_op jit(solution)/shard_map/ppermute | solution.py:652
  36.8 7.0 %collective-permute-start.1 = (f32[64,4096]{1,0:T(8,128)}, f32[64,4096]{1,0:T(8,128)S(1)}, u32[]{:S(2)}, u32[]{:S(2)}) collective-permute-start(f32[64,4096]{1,0:T(8,128)} %get-tuple-element.54), channel_id=1, source_target_pairs={{0,1},{1,0},{2,3},{3,2},{4,5},{5,4},{6,7},{7,6},{8,9},{9,8},{10,11... | collective-permute-start | bytes 3145736 | tf_op jit(solution)/shard_map/ppermute | solution.py:651
  37.3 18.4 %all-to-all-start.1 = ((f32[128,8,128]{2,1,0:T(8,128)}), f32[128,8,128]{2,1,0:T(8,128)S(1)}, u32[]{:S(2)}, u32[]{:S(2)}) async-start(f32[128,8,128]{2,1,0:T(8,128)} %shard_map.87), calls=%async_computation.1 | async-start | bytes 1048576 | tf_op jit(solution)/shard_map/all_to_all | solution.py:649
  43.8 1.0 copy-start.5
  47.5 8.2 %copy-start.1 = (bf16[512,896]{1,0:T(8,128)(2,1)S(1)}, bf16[512,896]{1,0:T(8,128)(2,1)}, u32[]{:S(2)}) copy-start(bf16[512,896]{1,0:T(8,128)(2,1)} %cot_hbm.7) | copy-start | bytes 2752516
  47.5 15.3 %collective-permute-start.5 = (f32[64,2176]{1,0:T(8,128)}, f32[64,2176]{1,0:T(8,128)}, u32[]{:S(2)}, u32[]{:S(2)}) collective-permute-start(f32[64,2176]{1,0:T(8,128)} %get-tuple-element.66), channel_id=1, source_target_pairs={{0,6},{1,7},{2,0},{3,1},{4,2},{5,3},{6,4},{7,5},{8,14},{9,15},{10,... | collective-permute-start | bytes 1671176 | tf_op jit(solution)/shard_map/ppermute | solution.py:655
  48.4 16.1 %collective-permute-start.4 = (f32[64,2176]{1,0:T(8,128)}, f32[64,2176]{1,0:T(8,128)}, u32[]{:S(2)}, u32[]{:S(2)}) collective-permute-start(f32[64,2176]{1,0:T(8,128)} %get-tuple-element.55), channel_id=1, source_target_pairs={{0,2},{1,3},{2,4},{3,5},{4,6},{5,7},{6,0},{7,1},{8,10},{9,11},{10,... | collective-permute-start | bytes 1671176 | tf_op jit(solution)/shard_map/ppermute | solution.py:654
  55.7 8.8 %copy-start.3 = (f32[64,4096]{1,0:T(8,128)S(1)}, f32[64,4096]{1,0:T(8,128)}, u32[]{:S(2)}) copy-start(f32[64,4096]{1,0:T(8,128)} %get-tuple-element.67.plus_hbm) | copy-start | bytes 3145732
  55.7 8.8 %collective-permute-start.3 = (f32[128,8,128]{2,1,0:T(8,128)S(1)}, f32[128,8,128]{2,1,0:T(8,128)S(1)}, u32[]{:S(2)}, u32[]{:S(2)}) collective-permute-start(f32[128,8,128]{2,1,0:T(8,128)S(1)} %all-to-all-done.1.mine_hbm.mine_ref), channel_id=1, source_target_pairs={{0,1},{1,0},{2,3},{3,2},{4,5},{5,4},{6,7},{7,6},{8,9},{9,8},{10,11... | collective-permute-start | bytes 1572872 | tf_op jit(solution)/shard_map/ppermute | solution.py:659
  70.4 30.5 %collective-permute-start.6 = (f32[64,4096]{1,0:T(8,128)S(1)}, f32[64,4096]{1,0:T(8,128)}, u32[]{:S(2)}, u32[]{:S(2)}) collective-permute-start(f32[64,4096]{1,0:T(8,128)S(1)} %get-tuple-element.74), channel_id=1, source_target_pairs={{0,2},{1,3},{2,4},{3,5},{4,6},{5,7},{6,0},{7,1},{8,10},{9,11},{10,... | collective-permute-start | bytes 3145736 | tf_op jit(solution)/shard_map/ppermute | solution.py:662
  70.5 30.4 %collective-permute-start.7 = (f32[64,4096]{1,0:T(8,128)}, f32[64,4096]{1,0:T(8,128)}, u32[]{:S(2)}, u32[]{:S(2)}) collective-permute-start(f32[64,4096]{1,0:T(8,128)} %get-tuple-element.75), channel_id=1, source_target_pairs={{0,6},{1,7},{2,0},{3,1},{4,2},{5,3},{6,4},{7,5},{8,14},{9,15},{10,... | collective-permute-start | bytes 3145736 | tf_op jit(solution)/shard_map/ppermute | solution.py:663
  73.8 15.6 %all-to-all-start.2 = ((f32[16,32,128]{2,1,0:T(8,128)}), f32[16,32,128]{2,1,0:T(8,128)S(1)}, u32[]{:S(2)}, u32[]{:S(2)}) async-start(f32[16,32,128]{2,1,0:T(8,128)} %get-tuple-element.69), calls=%async_computation.2 | async-start | bytes 524288 | tf_op jit(solution)/shard_map/all_to_all | solution.py:664
  82.6 1.4 %copy-start.2 = (bf16[4096,256]{1,0:T(8,128)(2,1)}, bf16[4096,256]{1,0:T(8,128)(2,1)S(1)}, u32[]{:S(2)}) copy-start(bf16[4096,256]{1,0:T(8,128)(2,1)S(1)} %get-tuple-element.73.basis_hbm) | copy-start | bytes 6291460

commit v9 on v7

--- a/solution.py
+++ b/solution.py
@@ -74,7 +74,7 @@
     return pl.ds(pl.multiple_of(place * width + i * step, step), step)
 
 
-PARTS = 4
+PARTS = 2
 
 
 def left_part(q3t, p3, error, acts):
@@ -401,7 +401,7 @@
             )
         )
     n = input_grad_ref.shape[0]
-    own = slice(2 * n, 3 * n)
+    own = slice(3 * n, 4 * n)
     sums = [
         copies.start(src, sums_ref.at[i])
         for i, src in enumerate((keep_hbm.at[own, :], got_hbm.at[own, :], left_hbm, right_hbm))
@@ -467,10 +467,8 @@
 def partial_kernel(
     cot_hbm,
     weight_hbm,
-    far_send_hbm,
-    near_send_hbm,
-    far_keep_hbm,
-    near_keep_hbm,
+    send_hbm,
+    keep_hbm,
     cot_ref,
     weight_ref,
     out_ref,
@@ -493,7 +491,7 @@
     for copy in waits:
         copy.wait()
     stores = []
-    targets = ((far_send_hbm, 0, n), (near_send_hbm, n, 4 * n), (far_keep_hbm, 4 * n, 5 * n), (near_keep_hbm, 5 * n, 8 * n))
+    targets = ((send_hbm, 0, 4 * n), (keep_hbm, 4 * n, 8 * n))
     for i in range(parts):
         weight_copies[i].wait()
         out_ref[i] = dot(cot_ref[...], weight_ref[i], NT)
@@ -512,20 +510,20 @@
         partial_kernel,
         (cot, weight),
         [HBM, HBM],
-        [shape((r, d)) for r in (n, 3 * n, n, 3 * n)],
-        [HBM] * 4,
+        [shape((4 * n, d))] * 2,
+        [HBM] * 2,
         [((tokens, ff), BF16), ((parts, step, ff), BF16), ((parts, tokens, step), F32)],
-        8 + 5 * parts,
+        8 + 3 * parts,
     )
 
 
 def far_kernel(keep_hbm, got_hbm, low_hbm, high_hbm, keep_ref, got_ref, sems):
     copies = Copies(sems)
-    d = keep_ref.shape[1]
+    n, d = keep_ref.shape
     wide = low_hbm.shape[1]
     halves = (slice(0, d // 2), slice(d // 2, d))
     loads = [
-        (copies.start(keep_hbm.at[:, at], keep_ref.at[:, at]), copies.start(got_hbm.at[:, at], got_ref.at[:, at]))
+        (copies.start(keep_hbm.at[:n, at], keep_ref.at[:, at]), copies.start(got_hbm.at[:n, at], got_ref.at[:, at]))
         for at in halves
     ]
     for at, pair in zip(halves, loads):
@@ -538,7 +536,7 @@
 
 
 def far_sums(keep, got):
-    n, d = keep.shape
+    n, d = keep.shape[0] // 4, keep.shape[1]
     return call(
         far_kernel,
         (keep, got),
@@ -555,8 +553,8 @@
     n = plus_hbm.shape[0]
     rows = (slice(0, n), slice(n, 2 * n))
     loads = [
-        (copies.start(keep_hbm.at[at, :], keep_ref.at[at, :]), copies.start(got_hbm.at[at, :], got_ref.at[at, :]))
-        for at in rows
+        (copies.start(keep_hbm.at[src, :], keep_ref.at[at, :]), copies.start(got_hbm.at[src, :], got_ref.at[at, :]))
+        for at, src in zip(rows, (slice(n, 2 * n), slice(2 * n, 3 * n)))
     ]
     stores = []
     for at, pair, out in zip(rows, loads, (plus_hbm, minus_hbm)):
@@ -568,8 +566,8 @@
         store.wait()
 
 
-def near_sums(keep, got, n):
-    d = keep.shape[1]
+def near_sums(keep, got):
+    n, d = keep.shape[0] // 4, keep.shape[1]
     return call(
         near_kernel,
         (keep, got),
@@ -632,18 +630,17 @@
     chunks = lax.all_to_all(total, both, 0, 0)
 
     up_weight, _ = lax.optimization_barrier((up_weight, total))
-    far_send, near_send, far_keep, near_keep = partials(up_cot, up_weight)
-    chunks, far_send, near_send = lax.optimization_barrier((chunks, far_send, near_send))
+    grad_send, grad_keep = partials(up_cot, up_weight)
+    chunks, grad_send = lax.optimization_barrier((chunks, grad_send))
 
     spread_left = spread(chunks, 1.0, kinds=2)
     mine = lax.all_to_all(spread_left, both, 0, 0)
-    far_send, near_send, _ = lax.optimization_barrier((far_send, near_send, spread_left))
-    far_got = lax.ppermute(far_send, "tensor", pairs)
-    near_got = lax.ppermute(near_send, "tensor", pairs)
-    far_low, far_high = far_sums(far_keep, far_got)
+    grad_send, _ = lax.optimization_barrier((grad_send, spread_left))
+    grad_got = lax.ppermute(grad_send, "tensor", pairs)
+    far_low, far_high = far_sums(grad_keep, grad_got)
     low_relay = lax.ppermute(far_low, "tensor", right_ring)
     high_relay = lax.ppermute(far_high, "tensor", left_ring)
-    plus, minus = near_sums(near_keep, near_got, far_keep.shape[0])
+    plus, minus = near_sums(grad_keep, grad_got)
     mine, _, plus = lax.optimization_barrier((mine, far_low, plus))
 
     other = lax.ppermute(mine, "tensor", pairs)
@@ -660,7 +657,7 @@
 
     q_chunks = lax.all_to_all(spread(right_parts, 1.0 / n_dp), "dp", 0, 0)
     new_error, q_factor, input_grad = final(
-        q_chunks, basis4, up_cot, acts, error, near_keep, near_got, from_left, from_right
+        q_chunks, basis4, up_cot, acts, error, grad_keep, grad_got, from_left, from_right
     )
     return (input_grad, new_error[None], basis, q_factor)
 

time: 110 us -> 108 us (0.982)
  starting transfers between devices: 29 us -> 27.1 us
  waiting for transfers between devices: 14.7 us -> 16.2 us
    all_to_all x1, starting transfers between devices: 6.85 us -> 5.4 us  [body(): right_parts = lax.all_to_all(right, 'dp', 0, 0)]
    unnamed x10 -> x8, local copies, waits for them, and re-layouts: 4.48 us -> 3.52 us
    ppermute x2 -> x1, waiting for transfers between devices: 1.6 us -> 2.55 us  [body(): grad_got = lax.ppermute(grad_send, 'tensor', pairs)]
  transfers between devices with their start and end apart: 11 -> 10, of which waited for: 4 -> 4; matrix products, arithmetic and copies ran while one was open for 0% -> 0% of each run, Pallas kernels for 25% -> 25%
where the time goes in v9:
time: 108 us
  Pallas kernels  47.4 us (44%)
  starting transfers between devices  27.1 us (25%)
  waiting for transfers between devices  16.2 us (15%)
  blocking collectives  11.6 us (11%)
  local copies, waits for them, and re-layouts  3.52 us (3%)
    pallas_call x6, Pallas kernels, call(): pl.pallas_call(kernel, in_specs=specs, out_specs=out_specs, out_shape=out...  36.7 us
    all_to_all x1, blocking collectives, body(): q_chunks = lax.all_to_all(spread(right_parts, 1.0 / n_dp), 'dp', 0, 0)  11.6 us
    all_to_all x1, starting transfers between devices, body(): chunks = lax.all_to_all(total, both, 0, 0)  11.2 us
    all_to_all x1, starting transfers between devices, body(): right_parts = lax.all_to_all(right, 'dp', 0, 0)  5.4 us
    all_to_all x1, waiting for transfers between devices, body(): right_parts = lax.all_to_all(right, 'dp', 0, 0)  5.34 us
    all_to_all x1, waiting for transfers between devices, body(): chunks = lax.all_to_all(total, both, 0, 0)  4.98 us
    all_to_all x1, starting transfers between devices, body(): mine = lax.all_to_all(spread_left, both, 0, 0)  4.94 us
    pallas_call x1, Pallas kernels, second(): pl.pallas_call(second_kernel, in_specs=[VMEM] * 7, out_specs=[VMEM, VMEM]...  3.73 us
  transfers between devices with their start and end apart: 10, of which 4 were waited for; matrix products, arithmetic and copies ran while one was open for 0% of the time, Pallas kernels for 25%

profile of v9, /device:TPU:0, one launch (start us, length us, event | category | flops | bytes accessed | tf_op | source)
XLA Modules:
  0.0 107.5 jit_solution(1392162457926689120)
XLA Ops:
  0.6 0.0 copy-start
  0.6 1.2 %copy-done = bf16[512,896]{1,0:T(8,128)(2,1)S(1)} copy-done((bf16[512,896]{1,0:T(8,128)(2,1)S(1)}, bf16[512,896]{1,0:T(8,128)(2,1)}, u32[]{:S(2)}) %copy-start) | copy-done | bytes 917528
  1.8 0.0 copy-start.3
  1.8 0.9 copy-done.3
  2.8 5.3 %shard_map.84 = (f32[128,8,128]{2,1,0:T(8,128)S(1)}, bf16[896,192]{1,0:T(8,128)(2,1)S(1)}, bf16[192,512]{1,0:T(8,128)(2,1)S(1)}, bf16[2,1024,896]{2,1,0:T(8,128)(2,1)S(1)}, bf16[2,512,1024]{2,1,0:T(8,128)(2,1)S(1)}) custom-call(f32[64,896]{1,0:T(8,128)S(1)} %copy-done.3, bf16[512,896]{1,0:T(8,128)(2,1)S(1)} %copy-done, bf16[512,4096]{1,0:T(8,128)(2,1)} %acts_hbm.5, ...), custom_call_target="tpu_custom_call" | custom-call | flops 1000000 | bytes 100000 | tf_op jit(solution)/shard_map/pallas_call | solution.py:25
  8.1 0.1 collective-permute-start
  8.2 1.9 %shard_map.85 = f32[128,8,128]{2,1,0:T(8,128)S(1)} custom-call(bf16[896,192]{1,0:T(8,128)(2,1)S(1)} %get-tuple-element.41.q3t_ref, bf16[192,512]{1,0:T(8,128)(2,1)S(1)} %get-tuple-element.42.p3_ref, bf16[2,1024,896]{2,1,0:T(8,128)(2,1)S(1)} %get-tuple-element.43.error_ref, bf16[2,512,1024]{2,1,0:T(8,128)(2,1)S(1)} %get-tuple-element.44.acts_ref), custom_call_target="tpu_custom_call" | custom-call | flops 1000000 | bytes 100000 | tf_op jit(solution)/shard_map/pallas_call | solution.py:171
  10.1 0.0 collective-permute-done
  10.1 0.8 add.3
  11.0 11.2 %all-to-all-start = ((f32[128,8,128]{2,1,0:T(8,128)}), f32[128,8,128]{2,1,0:T(8,128)S(1)}, u32[]{:S(2)}, u32[]{:S(2)}) async-start(f32[128,8,128]{2,1,0:T(8,128)} %add.3), calls=%async_computation | async-start | bytes 1048576 | tf_op jit(solution)/shard_map/all_to_all | solution.py:630
  22.3 8.5 %shard_map.86 = (f32[256,4096]{1,0:T(8,128)}, f32[256,4096]{1,0:T(8,128)}) custom-call(bf16[512,896]{1,0:T(8,128)(2,1)} %cot_hbm.7, bf16[4096,896]{1,0:T(8,128)(2,1)} %weight_hbm), custom_call_target="tpu_custom_call" | custom-call | flops 1000000 | bytes 100000 | tf_op jit(solution)/shard_map/pallas_call | solution.py:25
  30.8 5.0 %all-to-all-done.i = f32[128,8,128]{2,1,0:T(8,128)S(1)} async-done(((f32[128,8,128]{2,1,0:T(8,128)}), f32[128,8,128]{2,1,0:T(8,128)S(1)}, u32[]{:S(2)}, u32[]{:S(2)}) %all-to-all-start) | async-done | bytes 524320 | tf_op jit(solution)/shard_map/all_to_all | solution.py:630
  35.8 0.9 shard_map.87
  36.7 0.0 collective-permute-start.1
  36.7 4.9 %all-to-all-start.1 = ((f32[128,8,128]{2,1,0:T(8,128)}), f32[128,8,128]{2,1,0:T(8,128)S(1)}, u32[]{:S(2)}, u32[]{:S(2)}) async-start(f32[128,8,128]{2,1,0:T(8,128)} %shard_map.87), calls=%async_computation.1 | async-start | bytes 1048576 | tf_op jit(solution)/shard_map/all_to_all | solution.py:637
  41.6 2.6 %collective-permute-done.1.got_hbm = f32[256,4096]{1,0:T(8,128)} collective-permute-done((f32[256,4096]{1,0:T(8,128)}, f32[256,4096]{1,0:T(8,128)}, u32[]{:S(2)}, u32[]{:S(2)}) %collective-permute-start.1) | collective-permute-done | bytes 4194336 | tf_op jit(solution)/shard_map/ppermute | solution.py:639
  44.2 2.7 %shard_map.88 = (f32[64,2176]{1,0:T(8,128)}, f32[64,2176]{1,0:T(8,128)}) custom-call(f32[256,4096]{1,0:T(8,128)} %get-tuple-element.47.keep_hbm, f32[256,4096]{1,0:T(8,128)} %collective-permute-done.1.got_hbm), custom_call_target="tpu_custom_call" | custom-call | flops 1000000 | bytes 100000 | tf_op jit(solution)/shard_map/pallas_call | solution.py:25
  46.9 0.7 collective-permute-start.3
  47.6 0.0 copy-start.1
  47.6 1.4 %collective-permute-start.2 = (f32[64,2176]{1,0:T(8,128)}, f32[64,2176]{1,0:T(8,128)S(1)}, u32[]{:S(2)}, u32[]{:S(2)}) collective-permute-start(f32[64,2176]{1,0:T(8,128)} %get-tuple-element.52), channel_id=1, source_target_pairs={{0,2},{1,3},{2,4},{3,5},{4,6},{5,7},{6,0},{7,1},{8,10},{9,11},{10,... | collective-permute-start | bytes 1671176 | tf_op jit(solution)/shard_map/ppermute | solution.py:641
  49.0 3.4 %shard_map.89 = (f32[64,4096]{1,0:T(8,128)}, f32[64,4096]{1,0:T(8,128)}) custom-call(f32[256,4096]{1,0:T(8,128)} %get-tuple-element.47.keep_hbm, f32[256,4096]{1,0:T(8,128)} %collective-permute-done.1.got_hbm), custom_call_target="tpu_custom_call" | custom-call | flops 1000000 | bytes 100000 | tf_op jit(solution)/shard_map/pallas_call | solution.py:25
  52.3 3.3 %all-to-all-done.1.mine_hbm.mine_ref = f32[128,8,128]{2,1,0:T(8,128)S(1)} async-done(((f32[128,8,128]{2,1,0:T(8,128)}), f32[128,8,128]{2,1,0:T(8,128)S(1)}, u32[]{:S(2)}, u32[]{:S(2)}) %all-to-all-start.1) | async-done | bytes 524320 | tf_op jit(solution)/shard_map/all_to_all | solution.py:637
  55.6 0.0 collective-permute-start.4
  55.6 0.0 copy-done.1
  55.6 5.0 %shard_map.90 = (f32[64,64]{1,0:T(8,128)S(1)}, f32[64,896]{1,0:T(8,128)S(1)}, f32[64,512]{1,0:T(8,128)S(1)}, bf16[512,896]{1,0:T(8,128)(2,1)S(1)}, bf16[1,2048,8...) custom-call(f32[128,8,128]{2,1,0:T(8,128)S(1)} %all-to-all-done.1.mine_hbm.mine_ref, ...), custom_call_target="tpu_custom_call" | custom-call | flops 1000000 | bytes 100000 | tf_op jit(solution)/shard_map/pallas_call | solution.py:25
  60.6 0.0 collective-permute-done.4.other_ref
  60.6 3.7 %shard_map.91 = (f32[64,64]{1,0:T(8,128)S(1)}, f32[16,32,128]{2,1,0:T(8,128)}) custom-call(f32[128,8,128]{2,1,0:T(8,128)S(1)} %collective-permute-done.4.other_ref, f32[64,64]{1,0:T(8,128)S(1)} %get-tuple-element.56.gram_ref, f32[64,896]{1,0:T(8,128)S(1)} %get-tuple-element.57.with_error_ref, f32[64,512]{1,0:T(8,128)S(1)} %get-tuple-element.58.with_acts_ref, ...), custom_call_target="tpu_custom_call" | custom-call | flops 1000000 | bytes 100000 | tf_op jit(solution)/shard_map/pallas_call | solution.py:329
  64.3 0.0 collective-permute-done.3.high_ref
  64.3 0.0 collective-permute-done.2.low_ref
  64.3 2.1 %shard_map.94 = (f32[64,4096]{1,0:T(8,128)}, f32[64,4096]{1,0:T(8,128)}) custom-call(f32[64,4096]{1,0:T(8,128)} %get-tuple-element.68.plus_hbm, f32[64,4096]{1,0:T(8,128)} %get-tuple-element.69.minus_hbm, f32[64,2176]{1,0:T(8,128)S(1)} %collective-permute-done.2.low_ref, ...), custom_call_target="tpu_custom_call", output_to_operand_aliasing={{0}: (0, {}), {1}: (1, {})} | custom-call | flops 1000000 | bytes 100000 | tf_op jit(solution)/shard_map/pallas_call | solution.py:603
  66.5 0.7 collective-permute-start.5
  67.1 2.6 %collective-permute-start.6 = (f32[64,4096]{1,0:T(8,128)}, f32[64,4096]{1,0:T(8,128)}, u32[]{:S(2)}, u32[]{:S(2)}) collective-permute-start(f32[64,4096]{1,0:T(8,128)} %get-tuple-element.73), channel_id=1, source_target_pairs={{0,6},{1,7},{2,0},{3,1},{4,2},{5,3},{6,4},{7,5},{8,14},{9,15},{10,... | collective-permute-start | bytes 3145736 | tf_op jit(solution)/shard_map/ppermute | solution.py:653
  69.8 5.4 %all-to-all-start.2 = ((f32[16,32,128]{2,1,0:T(8,128)}), f32[16,32,128]{2,1,0:T(8,128)S(1)}, u32[]{:S(2)}, u32[]{:S(2)}) async-start(f32[16,32,128]{2,1,0:T(8,128)} %get-tuple-element.63), calls=%async_computation.2 | async-start | bytes 524288 | tf_op jit(solution)/shard_map/all_to_all | solution.py:654
  75.2 1.9 %shard_map.92 = (f32[64,4096]{1,0:T(8,128)}, bf16[4096,256]{1,0:T(8,128)(2,1)S(1)}) custom-call(f32[64,64]{1,0:T(8,128)S(1)} %get-tuple-element.64.factor_ref, f32[128,8,128]{2,1,0:T(8,128)S(1)} %all-to-all-done.1.mine_hbm.mine_ref, f32[128,8,128]{2,1,0:T(8,128)S(1)} %collective-permute-done.4.other_ref), custom_call_target="tpu_custom_call" | custom-call | flops 1000000 | bytes 100000 | tf_op jit(solution)/shard_map/pallas_call | solution.py:355
  77.1 0.0 copy-start.2
  77.1 1.4 %copy-done.2 = bf16[4096,256]{1,0:T(8,128)(2,1)} copy-done((bf16[4096,256]{1,0:T(8,128)(2,1)}, bf16[4096,256]{1,0:T(8,128)(2,1)S(1)}, u32[]{:S(2)}) %copy-start.2) | copy-done | bytes 2097176
  78.5 5.3 %all-to-all-done.2.i = f32[16,32,128]{2,1,0:T(8,128)S(1)} async-done(((f32[16,32,128]{2,1,0:T(8,128)}), f32[16,32,128]{2,1,0:T(8,128)S(1)}, u32[]{:S(2)}, u32[]{:S(2)}) %all-to-all-start.2) | async-done | bytes 262176 | tf_op jit(solution)/shard_map/all_to_all | solution.py:654
  83.9 11.6 %all_to_all.20.chunks_hbm = f32[16,32,128]{2,1,0:T(8,128)S(1)} all-to-all(f32[16,32,128]{2,1,0:T(8,128)S(1)} %shard_map.93), channel_id=1, replica_groups=mesh['dp'=16,'tensor'=8] {'dp'}, dimensions={0} | all-to-all | bytes 524288 | tf_op jit(solution)/shard_map/all_to_all | solution.py:658
  95.5 0.0 collective-permute-done.5.left_hbm
  95.5 0.0 collective-permute-done.6.right_hbm
  95.5 11.9 %shard_map.95 = (bf16[4096,896]{1,0:T(8,128)(2,1)}, f32[64,896]{1,0:T(8,128)}, bf16[64,4096]{1,0:T(8,128)(2,1)}) custom-call(f32[16,32,128]{2,1,0:T(8,128)S(1)} %all_to_all.20.chunks_hbm, bf16[4096,256]{1,0:T(8,128)(2,1)} %copy-done.2, bf16[512,896]{1,0:T(8,128)(2,1)S(1)} %copy-done.1, bf16[512,4096]{1,0:T(8,128)(2,1)} %acts_hbm.5, ...), custom_call_target="tpu_custom_call" | custom-call | flops 1000000 | bytes 100000 | tf_op jit(solution)/shard_map/pallas_call | solution.py:25
  (1 shorter events, 0.0 us)
Async XLA Ops:
  0.6 1.2 %copy-start = (bf16[512,896]{1,0:T(8,128)(2,1)S(1)}, bf16[512,896]{1,0:T(8,128)(2,1)}, u32[]{:S(2)}) copy-start(bf16[512,896]{1,0:T(8,128)(2,1)} %cot_hbm.7) | copy-start | bytes 2752516
  1.8 0.9 copy-start.3
  8.1 2.0 %collective-permute-start = (f32[128,8,128]{2,1,0:T(8,128)S(1)}, f32[128,8,128]{2,1,0:T(8,128)S(1)}, u32[]{:S(2)}, u32[]{:S(2)}) collective-permute-start(f32[128,8,128]{2,1,0:T(8,128)S(1)} %get-tuple-element.45), channel_id=1, source_target_pairs={{0,1},{1,0},{2,3},{3,2},{4,5},{5,4},{6,7},{7,6},{8,9},{9,8},{10,11... | collective-permute-start | bytes 1572872 | tf_op jit(solution)/shard_map/ppermute | solution.py:628
  11.0 24.8 %all-to-all-start = ((f32[128,8,128]{2,1,0:T(8,128)}), f32[128,8,128]{2,1,0:T(8,128)S(1)}, u32[]{:S(2)}, u32[]{:S(2)}) async-start(f32[128,8,128]{2,1,0:T(8,128)} %add.3), calls=%async_computation | async-start | bytes 1048576 | tf_op jit(solution)/shard_map/all_to_all | solution.py:630
  36.7 7.5 %collective-permute-start.1 = (f32[256,4096]{1,0:T(8,128)}, f32[256,4096]{1,0:T(8,128)}, u32[]{:S(2)}, u32[]{:S(2)}) collective-permute-start(f32[256,4096]{1,0:T(8,128)} %get-tuple-element.51), channel_id=1, source_target_pairs={{0,1},{1,0},{2,3},{3,2},{4,5},{5,4},{6,7},{7,6},{8,9},{9,8},{10,11... | collective-permute-start | bytes 12582920 | tf_op jit(solution)/shard_map/ppermute | solution.py:639
  36.7 18.9 %all-to-all-start.1 = ((f32[128,8,128]{2,1,0:T(8,128)}), f32[128,8,128]{2,1,0:T(8,128)S(1)}, u32[]{:S(2)}, u32[]{:S(2)}) async-start(f32[128,8,128]{2,1,0:T(8,128)} %shard_map.87), calls=%async_computation.1 | async-start | bytes 1048576 | tf_op jit(solution)/shard_map/all_to_all | solution.py:637
  46.9 17.5 %collective-permute-start.3 = (f32[64,2176]{1,0:T(8,128)}, f32[64,2176]{1,0:T(8,128)S(1)}, u32[]{:S(2)}, u32[]{:S(2)}) collective-permute-start(f32[64,2176]{1,0:T(8,128)} %get-tuple-element.53), channel_id=1, source_target_pairs={{0,6},{1,7},{2,0},{3,1},{4,2},{5,3},{6,4},{7,5},{8,14},{9,15},{10,... | collective-permute-start | bytes 1671176 | tf_op jit(solution)/shard_map/ppermute | solution.py:642
  47.6 8.1 %copy-start.1 = (bf16[512,896]{1,0:T(8,128)(2,1)S(1)}, bf16[512,896]{1,0:T(8,128)(2,1)}, u32[]{:S(2)}) copy-start(bf16[512,896]{1,0:T(8,128)(2,1)} %cot_hbm.7) | copy-start | bytes 2752516
  47.6 16.8 %collective-permute-start.2 = (f32[64,2176]{1,0:T(8,128)}, f32[64,2176]{1,0:T(8,128)S(1)}, u32[]{:S(2)}, u32[]{:S(2)}) collective-permute-start(f32[64,2176]{1,0:T(8,128)} %get-tuple-element.52), channel_id=1, source_target_pairs={{0,2},{1,3},{2,4},{3,5},{4,6},{5,7},{6,0},{7,1},{8,10},{9,11},{10,... | collective-permute-start | bytes 1671176 | tf_op jit(solution)/shard_map/ppermute | solution.py:641
  55.6 5.0 %collective-permute-start.4 = (f32[128,8,128]{2,1,0:T(8,128)S(1)}, f32[128,8,128]{2,1,0:T(8,128)S(1)}, u32[]{:S(2)}, u32[]{:S(2)}) collective-permute-start(f32[128,8,128]{2,1,0:T(8,128)S(1)} %all-to-all-done.1.mine_hbm.mine_ref), channel_id=1, source_target_pairs={{0,1},{1,0},{2,3},{3,2},{4,5},{5,4},{6,7},{7,6},{8,9},{9,8},{10,11... | collective-permute-start | bytes 1572872 | tf_op jit(solution)/shard_map/ppermute | solution.py:646
  66.5 29.0 %collective-permute-start.5 = (f32[64,4096]{1,0:T(8,128)}, f32[64,4096]{1,0:T(8,128)}, u32[]{:S(2)}, u32[]{:S(2)}) collective-permute-start(f32[64,4096]{1,0:T(8,128)} %get-tuple-element.72), channel_id=1, source_target_pairs={{0,2},{1,3},{2,4},{3,5},{4,6},{5,7},{6,0},{7,1},{8,10},{9,11},{10,... | collective-permute-start | bytes 3145736 | tf_op jit(solution)/shard_map/ppermute | solution.py:652
  67.1 28.4 %collective-permute-start.6 = (f32[64,4096]{1,0:T(8,128)}, f32[64,4096]{1,0:T(8,128)}, u32[]{:S(2)}, u32[]{:S(2)}) collective-permute-start(f32[64,4096]{1,0:T(8,128)} %get-tuple-element.73), channel_id=1, source_target_pairs={{0,6},{1,7},{2,0},{3,1},{4,2},{5,3},{6,4},{7,5},{8,14},{9,15},{10,... | collective-permute-start | bytes 3145736 | tf_op jit(solution)/shard_map/ppermute | solution.py:653
  69.8 14.1 %all-to-all-start.2 = ((f32[16,32,128]{2,1,0:T(8,128)}), f32[16,32,128]{2,1,0:T(8,128)S(1)}, u32[]{:S(2)}, u32[]{:S(2)}) async-start(f32[16,32,128]{2,1,0:T(8,128)} %get-tuple-element.63), calls=%async_computation.2 | async-start | bytes 524288 | tf_op jit(solution)/shard_map/all_to_all | solution.py:654
  77.1 1.4 %copy-start.2 = (bf16[4096,256]{1,0:T(8,128)(2,1)}, bf16[4096,256]{1,0:T(8,128)(2,1)S(1)}, u32[]{:S(2)}) copy-start(bf16[4096,256]{1,0:T(8,128)(2,1)S(1)} %get-tuple-element.67.basis_hbm) | copy-start | bytes 6291460
